TPU v7x, 32 devices: a whole 2x2x4 slice. The times are simulated.
32 devices in a mesh: dp: 16 (over z, x, core), tensor: 2 (over y).
Axes of the slice: x: 2, y: 2, z: 4, core: 2. Of those that a mesh axis runs over, the one named last changes fastest.
Arguments:
- activations: bfloat16 [8192, 2048], P('dp'), may hold values from -6 to 6
- cotangent: bfloat16 [8192, 2048], P('dp'), may hold values from -12 to 12
- padding_mask: int32 [8192], P('dp'), may hold values from 0 to 1, as said below
- positions: int32 [8192], P('dp'), may hold values from 0 to 255, as said below
- norm_gains: float32 [2, 2048], replicated, may hold values from 0.1 to 1.9
- base_query: bfloat16 [2048, 2048], P('dp', 'tensor'), may hold values from -0.125 to 0.125
- base_key: bfloat16 [2048, 2048], P('dp', 'tensor'), may hold values from -0.125 to 0.125
- base_value: bfloat16 [2048, 2048], P('dp', 'tensor'), may hold values from -0.125 to 0.125
- base_gate: bfloat16 [2048, 5632], P('dp', 'tensor'), may hold values from -0.125 to 0.125
- base_widen: bfloat16 [2048, 5632], P('dp', 'tensor'), may hold values from -0.125 to 0.125
- base_mixer: bfloat16 [2048, 2048], P('tensor', 'dp'), may hold values from -0.125 to 0.125
- base_funnel: bfloat16 [5632, 2048], P('tensor', 'dp'), may hold values from -0.078125 to 0.078125
- entry_value: float32 [5, 2048, 16], replicated, may hold values from -0.125 to 0.125
- attend_value: float32 [3, 16, 2048], P(None, None, 'tensor'), may hold values from -0.75 to 0.75
- widen_value: float32 [2, 16, 5632], P(None, None, 'tensor'), may hold values from -0.75 to 0.75
- mixer_value: float32 [2048, 16], P('tensor'), may hold values from -0.125 to 0.125
- funnel_value: float32 [5632, 16], P('tensor'), may hold values from -0.078125 to 0.078125
- output_value: float32 [2, 16, 2048], replicated, may hold values from -0.75 to 0.75
- stature_value: float32 [3, 2048], P(None, 'tensor'), may hold values from 0.5 to 10
- amplitude_value: float32 [2, 5632], P(None, 'tensor'), may hold values from 0.5 to 10
- loudness_value: float32 [2, 2048], replicated, may hold values from 0.5 to 11.313708
- entry_first: float32 [5, 2048, 16], replicated, may hold values from -0.0008544922 to 0.0008544922
- attend_first: float32 [3, 16, 2048], P(None, None, 'tensor'), may hold values from -0.0008544922 to 0.0008544922
- widen_first: float32 [2, 16, 5632], P(None, None, 'tensor'), may hold values from -9.1552734e-05 to 9.1552734e-05
- mixer_first: float32 [2048, 16], P('tensor'), may hold values from -0.0008544922 to 0.0008544922
- funnel_first: float32 [5632, 16], P('tensor'), may hold values from -0.0008544922 to 0.0008544922
- output_first: float32 [2, 16, 2048], replicated, may hold values from -0.0008544922 to 0.0008544922
- stature_first: float32 [3, 2048], P(None, 'tensor'), may hold values from -0.00015258789 to 0.00015258789
- amplitude_first: float32 [2, 5632], P(None, 'tensor'), may hold values from -4.5776367e-05 to 4.5776367e-05
- loudness_first: float32 [2, 2048], replicated, may hold values from -3.8146973e-05 to 3.8146973e-05
- entry_second: float32 [5, 2048, 16], replicated, may hold values from 1.5330651e-09 to 6.1322605e-09
- attend_second: float32 [3, 16, 2048], P(None, None, 'tensor'), may hold values from 1.5330651e-09 to 6.1322605e-09
- widen_second: float32 [2, 16, 5632], P(None, None, 'tensor'), may hold values from 1.7421195e-11 to 6.968478e-11
- mixer_second: float32 [2048, 16], P('tensor'), may hold values from 1.5330651e-09 to 6.1322605e-09
- funnel_second: float32 [5632, 16], P('tensor'), may hold values from 1.5330651e-09 to 6.1322605e-09
- output_second: float32 [2, 16, 2048], replicated, may hold values from 1.5330651e-09 to 6.1322605e-09
- stature_second: float32 [3, 2048], P(None, 'tensor'), may hold values from 4.7908285e-11 to 1.9163314e-10
- amplitude_second: float32 [2, 5632], P(None, 'tensor'), may hold values from 4.3552987e-12 to 1.7421195e-11
- loudness_second: float32 [2, 2048], replicated, may hold values from 3.9923572e-12 to 1.5969429e-11
Outputs:
- block_output: bfloat16 [8192, 2048], P('dp')
- input_gradient: float32 [8192, 2048], P('dp')
- gradient_norm: float32 [], replicated
- entry_updated: float32 [5, 2048, 16], replicated
- attend_updated: float32 [3, 16, 2048], P(None, None, 'tensor')
- widen_updated: float32 [2, 16, 5632], P(None, None, 'tensor')
- mixer_updated: float32 [2048, 16], P('tensor')
- funnel_updated: float32 [5632, 16], P('tensor')
- output_updated: float32 [2, 16, 2048], replicated
- stature_updated: float32 [3, 2048], P(None, 'tensor')
- amplitude_updated: float32 [2, 5632], P(None, 'tensor')
- loudness_updated: float32 [2, 2048], replicated
- entry_momentum: float32 [5, 2048, 16], replicated
- attend_momentum: float32 [3, 16, 2048], P(None, None, 'tensor')
- widen_momentum: float32 [2, 16, 5632], P(None, None, 'tensor')
- mixer_momentum: float32 [2048, 16], P('tensor')
- funnel_momentum: float32 [5632, 16], P('tensor')
- output_momentum: float32 [2, 16, 2048], replicated
- stature_momentum: float32 [3, 2048], P(None, 'tensor')
- amplitude_momentum: float32 [2, 5632], P(None, 'tensor')
- loudness_momentum: float32 [2, 2048], replicated
- entry_variance: float32 [5, 2048, 16], replicated
- attend_variance: float32 [3, 16, 2048], P(None, None, 'tensor')
- widen_variance: float32 [2, 16, 5632], P(None, None, 'tensor')
- mixer_variance: float32 [2048, 16], P('tensor')
- funnel_variance: float32 [5632, 16], P('tensor')
- output_variance: float32 [2, 16, 2048], replicated
- stature_variance: float32 [3, 2048], P(None, 'tensor')
- amplitude_variance: float32 [2, 5632], P(None, 'tensor')
- loudness_variance: float32 [2, 2048], replicated
Inputs may be any that keep to these rules, and one draw needn't show every extreme that they name: `padding_mask`: sequences are 256 consecutive rows, pairs are sequences 2i and 2i+1. In each pair one sequence has no padding and the other has 1 to 128 leading padded positions, marked 0. Positions count from 0 at a sequence's first unpadded token; padded positions hold 0.
All inputs are finite; a program needn't handle non-finite values.
Results may differ from a plain program's by a relative error of at most 0.013.
The roundings to bfloat16 on the way count: a program that leaves them out, or rounds other values in their place, can miss the bound.
Values may be sent and summed in bfloat16 or wider, within the bound.
A program may use at most 264 MiB of HBM per device.

v0:
```python
import jax
import jax.numpy as jnp
from jax import lax
from jax.sharding import PartitionSpec as P

HEAD_DIM = 128
SEQ = 256
STEP = 5


HIGH_PRECISION = lax.Precision.HIGHEST
ADAPTER_SCALE = 2.0
NORM_EPS = 1e-05
COLUMN_EPS = 1e-06
BETA_ONE = 0.9
BETA_TWO = 0.999
ADAM_EPS = 1e-08
DECAY = 0.01
CLIP = 1.0
RATE_FACTOR = 0.02
RATE_LIFT = 0.2
RATE_SCALE = 0.5
RATE_LOUD = 2.0
ROPE_BASE = 10000.0
MASKED = -1e30


def root_norm(values, gain):
    return values * lax.rsqrt(jnp.mean(values * values, axis=-1, keepdims=True) + NORM_EPS) * gain


def rotate(values, places, sign):
    half = values.shape[-1] // 2
    steps = jnp.arange(half, dtype=jnp.float32)
    frequency = ROPE_BASE ** (-2.0 * steps / values.shape[-1])
    angles = places.astype(jnp.float32)[:, None] * frequency[None, :]
    cosine = jnp.cos(angles)[:, None, :]
    sine = sign * jnp.sin(angles)[:, None, :]
    first = values[..., :half]
    second = values[..., half:]
    return jnp.concatenate(
        [first * cosine - second * sine, second * cosine + first * sine], axis=-1
    )


def allowed_of(padding, count):
    valid = padding.reshape(count, SEQ) > 0
    index = jnp.arange(SEQ)
    causal = index[:, None] >= index[None, :]
    itself = index[:, None] == index[None, :]
    return (causal[None] & valid[:, None, :] | itself[None])[:, None]


def merge_weights(bases, params):
    entry, attend, widen, mixer, funnel, output, stature, amplitude, loudness = params
    plan = (
        (bases[0], entry[0], attend[0], stature[0]),
        (bases[1], entry[1], attend[1], stature[1]),
        (bases[2], entry[2], attend[2], stature[2]),
        (bases[3], entry[3], widen[0], amplitude[0]),
        (bases[4], entry[4], widen[1], amplitude[1]),
        (bases[5], mixer, output[0], loudness[0]),
        (bases[6], funnel, output[1], loudness[1]),
    )
    directions = []
    squares = []
    for param_entry in plan:
        unit_direction = param_entry[0].astype(jnp.float32) + ADAPTER_SCALE * jnp.dot(
            param_entry[1], param_entry[2], precision=HIGH_PRECISION
        )
        directions.append(unit_direction)
        squares.append(jnp.sum(unit_direction * unit_direction, axis=0))
    mixer_squares, funnel_squares = lax.psum((squares[5], squares[6]), "tensor")
    squares = squares[:5] + [mixer_squares, funnel_squares]
    norms = [jnp.sqrt(total + COLUMN_EPS) for total in squares]
    merged = [
        (unit_direction * (param_entry[3] / norm)).astype(jnp.bfloat16)
        for unit_direction, param_entry, norm in zip(directions, plan, norms)
    ]
    return (merged, directions, norms, plan)


def adapter_terms(gradient, unit_direction, norm, dots, param_entry):
    ratio = param_entry[3] / norm
    direction_gradient = ratio * (gradient - unit_direction * (dots / (norm * norm)))
    down_factor_gradient = ADAPTER_SCALE * jnp.dot(
        direction_gradient, param_entry[2].T, precision=HIGH_PRECISION
    )
    up_factor_gradient = ADAPTER_SCALE * jnp.dot(
        param_entry[1].T, direction_gradient, precision=HIGH_PRECISION
    )
    return (down_factor_gradient, up_factor_gradient, dots / norm)


def squares_of(items):
    total = jnp.zeros((), jnp.float32)
    for param_entry in items:
        total = total + jnp.sum(param_entry * param_entry)
    return total


def decoupled_update(value, gradient, first, second, rate):
    momentum = BETA_ONE * first + (1.0 - BETA_ONE) * gradient
    variance = BETA_TWO * second + (1.0 - BETA_TWO) * gradient * gradient
    corrected = momentum / (1.0 - BETA_ONE**STEP)
    spread = jnp.sqrt(variance / (1.0 - BETA_TWO**STEP))
    return (value - rate * (corrected / (spread + ADAM_EPS) + DECAY * value), momentum, variance)


def body(
    activations,
    cotangent,
    padding_mask,
    positions,
    norm_gains,
    base_query,
    base_key,
    base_value,
    base_gate,
    base_widen,
    base_mixer,
    base_funnel,
    entry_value,
    attend_value,
    widen_value,
    mixer_value,
    funnel_value,
    output_value,
    stature_value,
    amplitude_value,
    loudness_value,
    entry_first,
    attend_first,
    widen_first,
    mixer_first,
    funnel_first,
    output_first,
    stature_first,
    amplitude_first,
    loudness_first,
    entry_second,
    attend_second,
    widen_second,
    mixer_second,
    funnel_second,
    output_second,
    stature_second,
    amplitude_second,
    loudness_second,
):
    params = (
        entry_value,
        attend_value,
        widen_value,
        mixer_value,
        funnel_value,
        output_value,
        stature_value,
        amplitude_value,
        loudness_value,
    )
    firsts = (
        entry_first,
        attend_first,
        widen_first,
        mixer_first,
        funnel_first,
        output_first,
        stature_first,
        amplitude_first,
        loudness_first,
    )
    seconds = (
        entry_second,
        attend_second,
        widen_second,
        mixer_second,
        funnel_second,
        output_second,
        stature_second,
        amplitude_second,
        loudness_second,
    )
    gathered = (
        lax.all_gather(base_query, "dp", axis=0, tiled=True),
        lax.all_gather(base_key, "dp", axis=0, tiled=True),
        lax.all_gather(base_value, "dp", axis=0, tiled=True),
        lax.all_gather(base_gate, "dp", axis=0, tiled=True),
        lax.all_gather(base_widen, "dp", axis=0, tiled=True),
        lax.all_gather(base_mixer, "dp", axis=1, tiled=True),
        lax.all_gather(base_funnel, "dp", axis=1, tiled=True),
    )
    merged, directions, norms, plan = merge_weights(gathered, params)
    count = activations.shape[0] // SEQ
    heads = base_query.shape[1] // HEAD_DIM
    scale = HEAD_DIM ** (-0.5)
    floats = activations.astype(jnp.float32)
    normed_one = root_norm(floats, norm_gains[0]).astype(jnp.bfloat16)
    queries = jnp.dot(normed_one, merged[0], preferred_element_type=jnp.float32).reshape(
        -1, heads, HEAD_DIM
    )
    keys = jnp.dot(normed_one, merged[1], preferred_element_type=jnp.float32).reshape(
        -1, heads, HEAD_DIM
    )
    values = jnp.dot(normed_one, merged[2], preferred_element_type=jnp.float32)
    values = values.astype(jnp.bfloat16).reshape(count, SEQ, heads, HEAD_DIM)
    turned_queries = (
        rotate(queries, positions, 1.0).astype(jnp.bfloat16).reshape(count, SEQ, heads, HEAD_DIM)
    )
    turned_keys = (
        rotate(keys, positions, 1.0).astype(jnp.bfloat16).reshape(count, SEQ, heads, HEAD_DIM)
    )
    allowed = allowed_of(padding_mask, count)
    scores = (
        jnp.einsum(
            "bqhd,bkhd->bhqk", turned_queries, turned_keys, preferred_element_type=jnp.float32
        )
        * scale
    )
    masked = jnp.where(allowed, scores, MASKED)
    top = jnp.max(masked, axis=-1, keepdims=True)
    log_total = top + jnp.log(jnp.sum(jnp.exp(masked - top), axis=-1, keepdims=True))
    attention = jnp.exp(masked - log_total)
    attention_low = attention.astype(jnp.bfloat16)
    mixed = jnp.einsum("bhqk,bkhd->bqhd", attention_low, values, preferred_element_type=jnp.float32)
    mixed = mixed.reshape(activations.shape[0], heads * HEAD_DIM).astype(jnp.bfloat16)
    attended = lax.psum(jnp.dot(mixed, merged[5], preferred_element_type=jnp.float32), "tensor")
    residual = floats + attended
    normed_two = root_norm(residual, norm_gains[1]).astype(jnp.bfloat16)
    gate = jnp.dot(normed_two, merged[3], preferred_element_type=jnp.float32)
    lifted = jnp.dot(normed_two, merged[4], preferred_element_type=jnp.float32)
    hidden = (jax.nn.silu(gate) * lifted).astype(jnp.bfloat16)
    funneled = lax.psum(jnp.dot(hidden, merged[6], preferred_element_type=jnp.float32), "tensor")
    block_output = (residual + funneled).astype(jnp.bfloat16)
    again = (
        lax.all_gather(base_query, "dp", axis=0, tiled=True),
        lax.all_gather(base_key, "dp", axis=0, tiled=True),
        lax.all_gather(base_value, "dp", axis=0, tiled=True),
        lax.all_gather(base_gate, "dp", axis=0, tiled=True),
        lax.all_gather(base_widen, "dp", axis=0, tiled=True),
        lax.all_gather(base_mixer, "dp", axis=1, tiled=True),
        lax.all_gather(base_funnel, "dp", axis=1, tiled=True),
    )
    merged, directions, norms, plan = merge_weights(again, params)
    terms = [None] * 7
    back = cotangent.astype(jnp.float32)
    back_low = back.astype(jnp.bfloat16)
    gradient_funnel = jnp.einsum("tf,td->fd", hidden, back_low, preferred_element_type=jnp.float32)
    d_hidden = jnp.einsum("td,fd->tf", back_low, merged[6], preferred_element_type=jnp.float32)
    unused, silu_pull = jax.vjp(lambda g, u: jax.nn.silu(g) * u, gate, lifted)
    d_gate, d_lifted = silu_pull(d_hidden)
    d_gate = d_gate.astype(jnp.bfloat16)
    d_lifted = d_lifted.astype(jnp.bfloat16)
    for index, d_part in ((3, d_gate), (4, d_lifted)):
        gradient_part = jnp.einsum(
            "tk,tf->kf", normed_two, d_part, preferred_element_type=jnp.float32
        )
        terms[index] = adapter_terms(
            gradient_part,
            directions[index],
            norms[index],
            jnp.sum(gradient_part * directions[index], axis=0),
            plan[index],
        )
    unused, second_pull = jax.vjp(lambda v: root_norm(v, norm_gains[1]), residual)
    d_normed_two = lax.psum(
        jnp.einsum("tf,kf->tk", d_gate, merged[3], preferred_element_type=jnp.float32)
        + jnp.einsum("tf,kf->tk", d_lifted, merged[4], preferred_element_type=jnp.float32),
        "tensor",
    )
    d_residual = back + second_pull(d_normed_two)[0]
    d_residual_low = d_residual.astype(jnp.bfloat16)
    gradient_mixer = jnp.einsum(
        "tk,td->kd", mixed, d_residual_low, preferred_element_type=jnp.float32
    )
    d_mixed = jnp.einsum("td,kd->tk", d_residual_low, merged[5], preferred_element_type=jnp.float32)
    d_mixed = d_mixed.astype(jnp.bfloat16).reshape(count, SEQ, heads, HEAD_DIM)
    d_attention = jnp.einsum("bqhd,bkhd->bhqk", d_mixed, values, preferred_element_type=jnp.float32)
    d_values = jnp.einsum(
        "bhqk,bqhd->bkhd", attention_low, d_mixed, preferred_element_type=jnp.float32
    )
    d_values = d_values.astype(jnp.bfloat16).reshape(-1, heads * HEAD_DIM)
    d_scores = attention * (d_attention - jnp.sum(attention * d_attention, axis=-1, keepdims=True))
    d_scores = d_scores.astype(jnp.bfloat16)
    d_turned_queries = (
        jnp.einsum("bhqk,bkhd->bqhd", d_scores, turned_keys, preferred_element_type=jnp.float32)
        * scale
    )
    d_turned_keys = (
        jnp.einsum("bhqk,bqhd->bkhd", d_scores, turned_queries, preferred_element_type=jnp.float32)
        * scale
    )
    d_queries = rotate(d_turned_queries.reshape(-1, heads, HEAD_DIM), positions, -1.0)
    d_queries = d_queries.reshape(-1, heads * HEAD_DIM).astype(jnp.bfloat16)
    d_keys = rotate(d_turned_keys.reshape(-1, heads, HEAD_DIM), positions, -1.0)
    d_keys = d_keys.reshape(-1, heads * HEAD_DIM).astype(jnp.bfloat16)
    for index, d_part in ((0, d_queries), (1, d_keys), (2, d_values)):
        gradient_part = jnp.einsum(
            "tk,tn->kn", normed_one, d_part, preferred_element_type=jnp.float32
        )
        terms[index] = adapter_terms(
            gradient_part,
            directions[index],
            norms[index],
            jnp.sum(gradient_part * directions[index], axis=0),
            plan[index],
        )
    d_normed_one = lax.psum(
        jnp.einsum("tn,kn->tk", d_queries, merged[0], preferred_element_type=jnp.float32)
        + jnp.einsum("tn,kn->tk", d_keys, merged[1], preferred_element_type=jnp.float32)
        + jnp.einsum("tn,kn->tk", d_values, merged[2], preferred_element_type=jnp.float32),
        "tensor",
    )
    unused, first_pull = jax.vjp(lambda v: root_norm(v, norm_gains[0]), floats)
    input_gradient = d_residual + first_pull(d_normed_one)[0]
    mixer_dots, funnel_dots = lax.psum(
        (
            jnp.sum(gradient_mixer * directions[5], axis=0),
            jnp.sum(gradient_funnel * directions[6], axis=0),
        ),
        "tensor",
    )
    terms[5] = adapter_terms(gradient_mixer, directions[5], norms[5], mixer_dots, plan[5])
    terms[6] = adapter_terms(gradient_funnel, directions[6], norms[6], funnel_dots, plan[6])
    gradients = (
        jnp.stack([terms[0][0], terms[1][0], terms[2][0], terms[3][0], terms[4][0]]),
        jnp.stack([terms[0][1], terms[1][1], terms[2][1]]),
        jnp.stack([terms[3][1], terms[4][1]]),
        terms[5][0],
        terms[6][0],
        jnp.stack([terms[5][1], terms[6][1]]),
        jnp.stack([terms[0][2], terms[1][2], terms[2][2]]),
        jnp.stack([terms[3][2], terms[4][2]]),
        jnp.stack([terms[5][2], terms[6][2]]),
    )
    summed = lax.psum(
        (
            gradients[0],
            gradients[1],
            gradients[2],
            gradients[3],
            gradients[4],
            gradients[5],
            gradients[6],
            gradients[7],
            gradients[8],
        ),
        "dp",
    )
    split_squares = squares_of((summed[1], summed[2], summed[3], summed[4], summed[6], summed[7]))
    entry_sum, output_sum, split_total = lax.psum((summed[0], summed[5], split_squares), "tensor")
    totals = (
        entry_sum,
        summed[1],
        summed[2],
        summed[3],
        summed[4],
        output_sum,
        summed[6],
        summed[7],
        summed[8],
    )
    gradient_norm = jnp.sqrt(split_total + squares_of((totals[0], totals[5], totals[8])))
    down_factor = jnp.minimum(1.0, CLIP / (gradient_norm + 1e-06))
    rates = (
        RATE_FACTOR,
        RATE_LIFT,
        RATE_LIFT,
        RATE_FACTOR,
        RATE_FACTOR,
        RATE_LIFT,
        RATE_SCALE,
        RATE_SCALE,
        RATE_LOUD,
    )
    updated = []
    momenta = []
    variances = []
    for value, gradient, first, second, rate in zip(params, totals, firsts, seconds, rates):
        fresh, momentum, variance = decoupled_update(
            value, gradient * down_factor, first, second, rate
        )
        updated.append(fresh)
        momenta.append(momentum)
        variances.append(variance)
    return (
        block_output,
        input_gradient,
        gradient_norm,
        updated[0],
        updated[1],
        updated[2],
        updated[3],
        updated[4],
        updated[5],
        updated[6],
        updated[7],
        updated[8],
        momenta[0],
        momenta[1],
        momenta[2],
        momenta[3],
        momenta[4],
        momenta[5],
        momenta[6],
        momenta[7],
        momenta[8],
        variances[0],
        variances[1],
        variances[2],
        variances[3],
        variances[4],
        variances[5],
        variances[6],
        variances[7],
        variances[8],
    )


def solution(mesh):
    return jax.shard_map(
        body,
        mesh=mesh,
        in_specs=(
            P("dp", None),
            P("dp", None),
            P("dp"),
            P("dp"),
            P(),
            P("dp", "tensor"),
            P("dp", "tensor"),
            P("dp", "tensor"),
            P("dp", "tensor"),
            P("dp", "tensor"),
            P("tensor", "dp"),
            P("tensor", "dp"),
            P(),
            P(None, None, "tensor"),
            P(None, None, "tensor"),
            P("tensor", None),
            P("tensor", None),
            P(),
            P(None, "tensor"),
            P(None, "tensor"),
            P(),
            P(),
            P(None, None, "tensor"),
            P(None, None, "tensor"),
            P("tensor", None),
            P("tensor", None),
            P(),
            P(None, "tensor"),
            P(None, "tensor"),
            P(),
            P(),
            P(None, None, "tensor"),
            P(None, None, "tensor"),
            P("tensor", None),
            P("tensor", None),
            P(),
            P(None, "tensor"),
            P(None, "tensor"),
            P(),
        ),
        out_specs=(
            P("dp", None),
            P("dp", None),
            P(),
            P(),
            P(None, None, "tensor"),
            P(None, None, "tensor"),
            P("tensor", None),
            P("tensor", None),
            P(),
            P(None, "tensor"),
            P(None, "tensor"),
            P(),
            P(),
            P(None, None, "tensor"),
            P(None, None, "tensor"),
            P("tensor", None),
            P("tensor", None),
            P(),
            P(None, "tensor"),
            P(None, "tensor"),
            P(),
            P(),
            P(None, None, "tensor"),
            P(None, None, "tensor"),
            P("tensor", None),
            P("tensor", None),
            P(),
            P(None, "tensor"),
            P(None, "tensor"),
            P(),
        ),
        check_vma=False,
    )
```

profile of v0, /device:TPU:0, one launch (start us, length us, event | category | flops | bytes accessed | tf_op | source)
XLA Modules:
  0.0 1521.4 jit_solution(8284416073435950769)
XLA Ops:
  16.9 46.6 %all-gather.8.cloned.1.call-done = bf16[2048,1024]{1,0:T(8,128)(2,1)} async-done(((bf16[128,1024]{1,0:T(8,128)(2,1)}), bf16[2048,1024]{1,0:T(8,128)(2,1)}) %all-gather.8.cloned.1.call-update) | async-done | bytes 4194320 | tf_op jit(solution)/shard_map/all_gather | solution.py:187
  63.5 11.6 multiply_reduce_fusion.13
  75.1 39.6 %all-gather.12.cloned.1.call-done = bf16[2048,1024]{1,0:T(8,128)(2,1)} async-done(((bf16[128,1024]{1,0:T(8,128)(2,1)}), bf16[2048,1024]{1,0:T(8,128)(2,1)}) %all-gather.12.cloned.1.call-update) | async-done | bytes 4194320 | tf_op jit(solution)/shard_map/all_gather | solution.py:186
  114.8 11.5 multiply_reduce_fusion.11
  126.9 39.1 %all-gather.10.cloned.1.call-done = bf16[2048,1024]{1,0:T(8,128)(2,1)} async-done(((bf16[128,1024]{1,0:T(8,128)(2,1)}), bf16[2048,1024]{1,0:T(8,128)(2,1)}) %all-gather.10.cloned.1.call-update) | async-done | bytes 4194320 | tf_op jit(solution)/shard_map/all_gather | solution.py:185
  166.0 10.1 multiply_reduce_fusion.12
  192.6 27.1 %all-gather.14.cloned.1.call-done = bf16[1024,2048]{1,0:T(8,128)(2,1)} async-done(((bf16[1024,128]{1,0:T(8,128)(2,1)}), bf16[1024,2048]{1,0:T(8,128)(2,1)}) %all-gather.14.cloned.1.call-update) | async-done | bytes 4194320 | tf_op jit(solution)/shard_map/all_gather | solution.py:190
  219.8 12.1 multiply_reduce_fusion.10
  247.4 7.7 fusion.62
  257.4 103.9 %all-reduce.9.cloned.1.call-done = f32[512,2048]{1,0:T(8,128)} async-done(((f32[512,2048]{1,0:T(8,128)}), f32[512,2048]{1,0:T(8,128)}) %all-reduce.9.cloned.1.call-update) | async-done | bytes 4194320 | tf_op jit(solution)/shard_map/psum | solution.py:227
  367.0 91.1 %all-gather.18.cloned.1.call-done = bf16[2048,2816]{1,0:T(8,128)(2,1)} async-done(((bf16[128,2816]{1,0:T(8,128)(2,1)}), bf16[2048,2816]{1,0:T(8,128)(2,1)}) %all-gather.18.cloned.1.call-update) | async-done | bytes 11534352 | tf_op jit(solution)/shard_map/all_gather | solution.py:189
  458.1 25.0 %multiply_reduce_fusion.4 = (f32[2816]{0:T(1024)S(1)}, f32[2048,2816]{1,0:T(8,128)}) fusion(f32[2,16,2816]{2,1,0:T(8,128)S(1)} %copy-done.34, f32[5,2048,16]{1,2,0:T(8,128)S(1)} %copy-done.25, bf16[2048,2816]{1,0:T(8,128)(2,1)} %all-gather.18.cloned.1.call-done), kind=kOutput, calls=%fused_computation.10 | convolution fusion | flops 1136129280 | bytes 34925568 | tf_op jit(solution)/shard_map/dot_general | solution.py:68
  483.2 70.0 %all-gather.16.cloned.1.call-done = bf16[2048,2816]{1,0:T(8,128)(2,1)} async-done(((bf16[128,2816]{1,0:T(8,128)(2,1)}), bf16[2048,2816]{1,0:T(8,128)(2,1)}) %all-gather.16.cloned.1.call-update) | async-done | bytes 11534352 | tf_op jit(solution)/shard_map/all_gather | solution.py:188
  553.2 25.2 %multiply_reduce_fusion.5 = (f32[2816]{0:T(1024)S(1)}, f32[2048,2816]{1,0:T(8,128)}) fusion(f32[2,16,2816]{2,1,0:T(8,128)S(1)} %copy-done.34, f32[5,2048,16]{1,2,0:T(8,128)S(1)} %copy-done.25, bf16[2048,2816]{1,0:T(8,128)(2,1)} %all-gather.16.cloned.1.call-done), kind=kOutput, calls=%fused_computation.13 | convolution fusion | flops 1136129280 | bytes 34925568 | tf_op jit(solution)/shard_map/dot_general | solution.py:68
  578.5 13.6 fusion.14
  592.2 18.7 %multiply_convert_fusion.7 = (bf16[512,2816]{1,0:T(8,128)(2,1)}, f32[512,2816]{1,0:T(8,128)}) fusion(f32[512,2816]{1,0:T(8,128)} %fusion.14, bf16[512,2048]{1,0:T(8,128)(2,1)S(1)} %copy-done.14, f32[2048,2816]{1,0:T(8,128)} %get-tuple-element.119, f32[2816]{0:T(1024)S(1)} %get-tuple-element.33), kind=kOutput, calls=%fused_computation.55 | convolution fusion | flops 5925765120 | bytes 39595008 | tf_op jit(solution)/shard_map/dot_general | solution.py:231
  610.8 40.3 %all-gather.20.cloned.1.call-done = bf16[2816,2048]{1,0:T(8,128)(2,1)} async-done(((bf16[2816,128]{1,0:T(8,128)(2,1)}), bf16[2816,2048]{1,0:T(8,128)(2,1)}) %all-gather.20.cloned.1.call-update) | async-done | bytes 11534352 | tf_op jit(solution)/shard_map/all_gather | solution.py:191
  651.1 24.1 %multiply_add_fusion = f32[2816,2048]{1,0:T(8,128)} fusion(bf16[2816,2048]{1,0:T(8,128)(2,1)} %all-gather.20.cloned.1.call-done, f32[2816,16]{0,1:T(8,128)S(1)} %copy-done.42, f32[2,16,2048]{2,1,0:T(8,128)S(1)} %copy-done.37), kind=kOutput, calls=%fused_computation.8 | convolution fusion | flops 1124597760 | bytes 34914304 | tf_op jit(solution)/shard_map/dot_general | solution.py:68
  675.2 18.2 %multiply_reduce_fusion = (f32[2048]{0:T(1024)}, f32[2048]{0:T(1024)S(1)}, f32[2816,2048]{1,0:T(8,128)}) fusion(f32[2816,2048]{1,0:T(8,128)} %multiply_add_fusion, bf16[512,2816]{1,0:T(8,128)(2,1)} %get-tuple-element.120, bf16[512,2048]{1,0:T(8,128)(2,1)} %param.40), kind=kOutput, calls=%fused_computation.1 | convolution fusion | flops 5928644608 | bytes 51134464 | tf_op jit(solution)/shard_map/tf,td->fd/dot_general | solution.py:248
  698.4 17.7 %fusion.9 = (bf16[512,2816]{1,0:T(8,128)(2,1)}, bf16[512,2816]{1,0:T(8,128)(2,1)}) fusion(f32[512,2816]{1,0:T(8,128)} %fusion.14, f32[512,2816]{1,0:T(8,128)} %get-tuple-element.121, bf16[512,2048]{1,0:T(8,128)(2,1)} %param.40, f32[2816,2048]{1,0:T(8,128)} %multiply_add_fusion, f32[2048]{0:T(1024)S(1)} %fusion.162), kind=kOutput, calls=%fused_computation.54 | convolution fusion | flops 5937299456 | bytes 42475520 | tf_op jit(solution)/shard_map/td,fd->tf/dot_general | solution.py:249
  716.1 12.9 fusion.13
  729.0 16.0 %multiply_reduce_fusion.2 = (f32[2816]{0:T(1024)S(1)}, f32[2048,2816]{1,0:T(8,128)}) fusion(f32[2048,2816]{1,0:T(8,128)} %get-tuple-element.117, bf16[512,2048]{1,0:T(8,128)(2,1)S(1)} %copy-done.14, bf16[512,2816]{1,0:T(8,128)(2,1)} %get-tuple-element.77), kind=kOutput, calls=%fused_computation.5 | convolution fusion | flops 5917111296 | bytes 51129344 | tf_op jit(solution)/shard_map/tk,tf->kf/dot_general | solution.py:255
  745.0 16.1 %multiply_reduce_fusion.1 = (f32[2816]{0:T(1024)S(1)}, f32[2048,2816]{1,0:T(8,128)}) fusion(f32[2048,2816]{1,0:T(8,128)} %get-tuple-element.119, bf16[512,2048]{1,0:T(8,128)(2,1)S(1)} %copy-done.14, bf16[512,2816]{1,0:T(8,128)(2,1)} %get-tuple-element.76), kind=kOutput, calls=%fused_computation.3 | convolution fusion | flops 5917111296 | bytes 51129344 | tf_op jit(solution)/shard_map/tk,tf->kf/dot_general | solution.py:255
  761.2 14.1 fusion.29
  776.4 20.5 %fusion.25 = f32[1,16,2816]{2,1,0:T(8,128)S(1)} fusion(f32[2048,2816]{1,0:T(8,128)} %get-tuple-element.132, f32[2048,2816]{1,0:T(8,128)} %get-tuple-element.119, f32[2816]{0:T(1024)S(1)} %multiply_divide_fusion, f32[2816]{0:T(1024)S(1)} %get-tuple-element.33, f32[5,2048,16]{1,2,0:T(8,128)S(1)} %copy-done.26), kind=kOutput, calls=%fused_computation.82 | convolution fusion | flops 1124642816 | bytes 46473216 | tf_op jit(solution)/shard_map/dot_general | solution.py:89
  796.9 19.9 %fusion.27 = f32[1,16,2816]{2,1,0:T(8,128)S(1)} fusion(f32[2048,2816]{1,0:T(8,128)} %get-tuple-element.134, f32[2048,2816]{1,0:T(8,128)} %get-tuple-element.117, f32[2816]{0:T(1024)S(1)} %multiply_divide_fusion.1, f32[2816]{0:T(1024)S(1)} %get-tuple-element.32, f32[5,2048,16]{1,2,0:T(8,128)S(1)} %copy-done.26), kind=kOutput, calls=%fused_computation.84 | convolution fusion | flops 1124642816 | bytes 46473216 | tf_op jit(solution)/shard_map/dot_general | solution.py:89
  817.6 13.5 fusion.12
  831.1 50.4 %all-reduce.11.cloned.1.call-done = f32[512,2048]{1,0:T(8,128)} async-done(((f32[512,2048]{1,0:T(8,128)}), f32[512,2048]{1,0:T(8,128)}) %all-reduce.11.cloned.1.call-update) | async-done | bytes 4194320 | tf_op jit(solution)/shard_map/psum | solution.py:266
  921.2 7.9 fusion.60
  929.2 6.0 multiply_reduce_fusion.8
  946.2 6.2 fusion.75
  952.5 11.0 fusion.54
  969.5 6.9 all-reduce.2
  977.0 12.4 fusion.69
  989.4 8.3 fusion.45
  998.4 21.8 %fusion.56 = f32[1,16,2048]{2,1,0:T(8,128)} fusion(f32[2816,16]{0,1:T(8,128)S(1)} %copy-done.43, f32[2816,2048]{1,0:T(8,128)} %get-tuple-element.122, f32[2816,2048]{1,0:T(8,128)} %multiply_add_fusion, f32[2048]{0:T(1024)S(1)} %get-tuple-element.95, f32[2048]{0:T(1024)S(1)} %fusion.162), kind=kOutput, calls=%fused_computation.113 | convolution fusion | flops 1124630528 | bytes 46465024 | tf_op jit(solution)/shard_map/dot_general | solution.py:89
  1020.2 26.6 %fusion.23 = f32[2816,16]{0,1:T(8,128)} fusion(f32[2816,2048]{1,0:T(8,128)} %get-tuple-element.122, f32[2816,2048]{1,0:T(8,128)} %multiply_add_fusion, f32[2048]{0:T(1024)S(1)} %get-tuple-element.95, f32[2048]{0:T(1024)S(1)} %fusion.162, f32[2,16,2048]{2,1,0:T(8,128)S(1)} %copy-done.38), kind=kOutput, calls=%fused_computation.80 | convolution fusion | flops 1124642816 | bytes 46465024 | tf_op jit(solution)/shard_map/dot_general | solution.py:86
  1049.1 10.2 multiply_reduce_fusion.7
  1060.1 6.9 fusion.73
  1067.0 8.7 fusion.51
  1075.7 9.3 fusion.71
  1085.0 12.3 fusion.48
  1097.4 29.4 %fusion.43 = f32[5,2048,16]{1,2,0:T(8,128)} fusion(f32[5,2048,16]{1,2,0:T(8,128)} %fusion.48, f32[2048,2816]{1,0:T(8,128)} %get-tuple-element.134, f32[2048,2816]{1,0:T(8,128)} %get-tuple-element.117, f32[2816]{0:T(1024)} %copy-done.62, f32[2816]{0:T(1024)S(1)} %copy-done.59, f32[2,16,2816]{2,1,0:T(8,128)S(1)} %copy-done.35), kind=kOutput, calls=%fused_computation.100 | convolution fusion | flops 1124630528 | bytes 46473216 | tf_op jit(solution)/shard_map/dot_general | solution.py:86
  1126.8 29.7 %fusion.40 = f32[5,2048,16]{1,2,0:T(8,128)} fusion(f32[5,2048,16]{1,2,0:T(8,128)} %fusion.43, f32[2048,2816]{1,0:T(8,128)} %get-tuple-element.132, f32[2048,2816]{1,0:T(8,128)} %get-tuple-element.119, f32[2816]{0:T(1024)S(1)} %copy-done.61, f32[2816]{0:T(1024)S(1)} %copy-done.57, f32[2,16,2816]{2,1,0:T(8,128)S(1)} %copy-done.35), kind=kOutput, calls=%fused_computation.97 | convolution fusion | flops 1124630528 | bytes 46473216 | tf_op jit(solution)/shard_map/dot_general | solution.py:86
  1159.8 10.4 add_add_fusion.2
  1170.2 88.7 %all-reduce.13.cloned.1.call-done = (f32[3,16,1024]{2,1,0:T(8,128)}, f32[2,16,2816]{2,1,0:T(8,128)}, f32[1024,16]{0,1:T(8,128)}, f32[2816,16]{0,1:T(8,128)}, f32...) async-done(((f32[3,16,1024]{2,1,0:T(8,128)}, f32[2,16,2816]{2,1,0:T(8,128)}, f32[1024,16]{0,1:T(8,128)}, f32[2816,16]{0,1:T(8,128)}, f32[5,2048,16]{1,2,0:T(8,128)}, ...) | async-done | bytes 1720336 | tf_op jit(solution)/shard_map/psum | solution.py:336
  1259.9 58.9 %all-reduce = (f32[3,1024]{1,0:T(4,128)S(1)}, f32[2,2816]{1,0:T(2,128)S(1)}, f32[2,2048]{1,0:T(2,128)S(1)}) all-reduce(f32[3,1024]{1,0:T(4,128)S(1)} %pad_maximum_fusion.12, f32[2,2816]{1,0:T(2,128)S(1)} %pad_maximum_fusion.11, f32[2,2048]{1,0:T(2,128)S(1)} %pad_maximum_fusion.13), channel_id=1, replica_groups=mesh['dp'=16,'tensor'=2] {'dp'}, use_global_device_ids=true, to_apply=%region_37.38 | all-reduce | flops 12800 | bytes 102400 | tf_op jit(solution)/shard_map/psum | solution.py:336
  1332.6 148.0 %all-reduce.15.cloned.1.call-done = (f32[512,2048]{1,0:T(8,128)}, f32[512,2048]{1,0:T(8,128)}, f32[5,2048,16]{1,2,0:T(8,128)}, f32[2,16,2048]{2,1,0:T(8,128)}) async-done(((f32[512,2048]{1,0:T(8,128)}, f32[512,2048]{1,0:T(8,128)}, f32[5,2048,16]{1,2,0:T(8,128)}, f32[2,16,2048]{2,1,0:T(8,128)}), (f32[512,2048]{1,0:T(8,128)}, f32[512,2048]{1,0:T(8,128)}, f32[5,2048,16]{1,2,0:T(8,128)}, ...) | async-done | bytes 9306128 | tf_op jit(solution)/shard_map/psum | solution.py:233
  (420 shorter events, 161.0 us)
Async XLA Ops:
  7.2 56.3 %copy-start.24 = (f32[5,2048,16]{1,2,0:T(8,128)S(1)}, f32[5,2048,16]{1,2,0:T(8,128)}, u32[]{:S(2)}) copy-start(f32[5,2048,16]{1,2,0:T(8,128)} %param.51) | copy-start | bytes 1966084
  7.2 56.3 %copy-start.44 = (f32[3,16,1024]{2,1,0:T(8,128)S(1)}, f32[3,16,1024]{2,1,0:T(8,128)}, u32[]{:S(2)}) copy-start(f32[3,16,1024]{2,1,0:T(8,128)} %param.52) | copy-start | bytes 589828
  7.2 56.3 %all-gather.8.cloned.1.call-start = ((), (), s32[]{:S(2)}) async-start(), calls=%async_computation | async-start | bytes 4456448 | tf_op jit(solution)/shard_map/all_gather | solution.py:187
  8.0 106.8 %all-gather.12.cloned.1.call-start = ((), (), s32[]{:S(2)}) async-start(), calls=%async_computation.2 | async-start | bytes 4456448 | tf_op jit(solution)/shard_map/all_gather | solution.py:186
  8.7 157.3 %all-gather.10.cloned.1.call-start = ((), (), s32[]{:S(2)}) async-start(), calls=%async_computation.1 | async-start | bytes 4456448 | tf_op jit(solution)/shard_map/all_gather | solution.py:185
  9.5 210.3 %all-gather.14.cloned.1.call-start = ((), (), s32[]{:S(2)}) async-start(), calls=%async_computation.3 | async-start | bytes 4456448 | tf_op jit(solution)/shard_map/all_gather | solution.py:190
  10.0 351.3 %all-reduce.9.cloned.1.call-start = ((), (), s32[]{:S(2)}) async-start(), calls=%async_computation.4 | async-start | bytes 8388608 | tf_op jit(solution)/shard_map/psum | solution.py:227
  13.6 170.1 %copy-start.66 = (f32[512]{0:T(512)}, f32[512]{0:T(512)S(1)}, u32[]{:S(2)}) copy-start(f32[512]{0:T(512)S(1)} %fusion.163) | copy-start | bytes 6148
  14.4 227.2 %copy-start.32 = (pred[2,256,256]{1,2,0:T(8,128)(4,1)}, pred[2,256,256]{1,2,0:T(8,128)(4,1)S(1)}, u32[]{:S(2)}) copy-start(pred[2,256,256]{1,2,0:T(8,128)(4,1)S(1)} %and_or_fusion) | copy-start | bytes 393220
  16.2 170.5 %copy-start.40 = (f32[512,64]{1,0:T(8,128)}, f32[512,64]{1,0:T(8,128)S(1)}, u32[]{:S(2)}) copy-start(f32[512,64]{1,0:T(8,128)S(1)} %get-tuple-element.105) | copy-start | bytes 393220
  16.2 167.5 %copy-start.48 = (f32[1,2048]{1,0:T(1,128)}, f32[1,2048]{1,0:T(1,128)S(1)}, u32[]{:S(2)}) copy-start(f32[1,2048]{1,0:T(1,128)S(1)} %get-tuple-element.101) | copy-start | bytes 24580
  16.3 348.6 %copy-start.68 = (f32[1,2048]{1,0:T(1,128)}, f32[1,2048]{1,0:T(1,128)S(1)}, u32[]{:S(2)}) copy-start(f32[1,2048]{1,0:T(1,128)S(1)} %get-tuple-element.102) | copy-start | bytes 24580
  75.1 51.2 %copy-start.102 = (f32[1024]{0:T(1024)}, f32[1024]{0:T(1024)S(1)}, u32[]{:S(2)}) copy-start(f32[1024]{0:T(1024)S(1)} %get-tuple-element.110) | copy-start | bytes 12292
  75.1 101.1 %copy-start.108 = (f32[1024]{0:T(1024)}, f32[1024]{0:T(1024)S(1)}, u32[]{:S(2)}) copy-start(f32[1024]{0:T(1024)S(1)} %add_rsqrt_fusion.4) | copy-start | bytes 12292
  126.9 49.3 %copy-start.110 = (f32[1024]{0:T(1024)}, f32[1024]{0:T(1024)S(1)}, u32[]{:S(2)}) copy-start(f32[1024]{0:T(1024)S(1)} %add_rsqrt_fusion.2) | copy-start | bytes 12292
  126.9 49.3 %copy-start.95 = (f32[3,1024]{1,0:T(4,128)S(1)}, f32[3,1024]{1,0:T(4,128)}, u32[]{:S(2)}) copy-start(f32[3,1024]{1,0:T(4,128)} %param.57) | copy-start | bytes 36868
  126.9 49.4 %copy-start = (bf16[512,2048]{1,0:T(8,128)(2,1)S(1)}, bf16[512,2048]{1,0:T(8,128)(2,1)}, u32[]{:S(2)}) copy-start(bf16[512,2048]{1,0:T(8,128)(2,1)} %param.39) | copy-start | bytes 6291460
  188.8 31.0 %copy-start.37 = (f32[2,16,2048]{2,1,0:T(8,128)S(1)}, f32[2,16,2048]{2,1,0:T(8,128)}, u32[]{:S(2)}) copy-start(f32[2,16,2048]{2,1,0:T(8,128)} %param.56) | copy-start | bytes 786436
  189.0 48.0 %copy-start.16 = (bf16[2,256,8,64]{3,1,2,0:T(8,128)(2,1)}, bf16[2,256,8,64]{3,1,2,0:T(8,128)(2,1)S(1)}, u32[]{:S(2)}) copy-start(bf16[2,256,8,64]{3,1,2,0:T(8,128)(2,1)S(1)} %copy.82) | copy-start | bytes 1572868
  255.1 203.0 %all-gather.18.cloned.1.call-start = ((), (), s32[]{:S(2)}) async-start(), calls=%async_computation.6 | async-start | bytes 12255232 | tf_op jit(solution)/shard_map/all_gather | solution.py:189
  255.7 297.5 %all-gather.16.cloned.1.call-start = ((), (), s32[]{:S(2)}) async-start(), calls=%async_computation.5 | async-start | bytes 12255232 | tf_op jit(solution)/shard_map/all_gather | solution.py:188
  256.5 394.7 %all-gather.20.cloned.1.call-start = ((), (), s32[]{:S(2)}) async-start(), calls=%async_computation.7 | async-start | bytes 12255232 | tf_op jit(solution)/shard_map/all_gather | solution.py:191
  257.2 624.3 %all-reduce.11.cloned.1.call-start = ((), (), s32[]{:S(2)}) async-start(), calls=%async_computation.8 | async-start | bytes 8388608 | tf_op jit(solution)/shard_map/psum | solution.py:266
  364.9 93.2 %copy-start.25 = (f32[5,2048,16]{1,2,0:T(8,128)S(1)}, f32[5,2048,16]{1,2,0:T(8,128)}, u32[]{:S(2)}) copy-start(f32[5,2048,16]{1,2,0:T(8,128)} %param.51) | copy-start | bytes 1966084
  364.9 93.2 %copy-start.34 = (f32[2,16,2816]{2,1,0:T(8,128)S(1)}, f32[2,16,2816]{2,1,0:T(8,128)}, u32[]{:S(2)}) copy-start(f32[2,16,2816]{2,1,0:T(8,128)} %param.53) | copy-start | bytes 1081348
  483.1 95.2 %copy-start.70 = (f32[2816]{0:T(1024)}, f32[2816]{0:T(1024)S(1)}, u32[]{:S(2)}) copy-start(f32[2816]{0:T(1024)S(1)} %get-tuple-element.118) | copy-start | bytes 33796
  483.1 95.2 %copy-start.82 = (f32[2,2816]{1,0:T(2,128)S(1)}, f32[2,2816]{1,0:T(2,128)}, u32[]{:S(2)}) copy-start(f32[2,2816]{1,0:T(2,128)} %param.58) | copy-start | bytes 67588
  483.2 95.4 %copy-start.14 = (bf16[512,2048]{1,0:T(8,128)(2,1)S(1)}, bf16[512,2048]{1,0:T(8,128)(2,1)}, u32[]{:S(2)}) copy-start(bf16[512,2048]{1,0:T(8,128)(2,1)} %multiply_convert_fusion.15) | copy-start | bytes 6291460
  578.5 197.5 %copy-start.56 = (f32[2816]{0:T(1024)}, f32[2816]{0:T(1024)S(1)}, u32[]{:S(2)}) copy-start(f32[2816]{0:T(1024)S(1)} %get-tuple-element.33) | copy-start | bytes 33796
  578.5 218.4 %copy-start.58 = (f32[2816]{0:T(1024)}, f32[2816]{0:T(1024)S(1)}, u32[]{:S(2)}) copy-start(f32[2816]{0:T(1024)S(1)} %get-tuple-element.32) | copy-start | bytes 33796
  592.2 59.0 %copy-start.42 = (f32[2816,16]{0,1:T(8,128)S(1)}, f32[2816,16]{0,1:T(8,128)}, u32[]{:S(2)}) copy-start(f32[2816,16]{0,1:T(8,128)} %param.55) | copy-start | bytes 540676
  745.0 31.0 %copy-start.74 = (f32[2816]{0:T(1024)}, f32[2816]{0:T(1024)S(1)}, u32[]{:S(2)}) copy-start(f32[2816]{0:T(1024)S(1)} %get-tuple-element.133) | copy-start | bytes 33796
  775.3 483.6 %all-reduce.13.cloned.1.call-start = ((), (), s32[]{:S(2)}) async-start(), calls=%async_computation.9 | async-start | bytes 3440640 | tf_op jit(solution)/shard_map/psum | solution.py:336
  817.6 63.9 %copy-start.1 = (bf16[512,2048]{1,0:T(8,128)(2,1)S(1)}, bf16[512,2048]{1,0:T(8,128)(2,1)}, u32[]{:S(2)}) copy-start(bf16[512,2048]{1,0:T(8,128)(2,1)} %param.39) | copy-start | bytes 6291460
  817.6 63.9 %copy-start.69 = (f32[1,2048]{1,0:T(1,128)S(1)}, f32[1,2048]{1,0:T(1,128)}, u32[]{:S(2)}) copy-start(f32[1,2048]{1,0:T(1,128)} %copy-done.68) | copy-start | bytes 24580
  831.0 54.8 %copy-start.125 = (f32[512]{0:T(512)S(1)}, f32[512]{0:T(512)}, u32[]{:S(2)}) copy-start(f32[512]{0:T(512)} %copy-done.124) | copy-start | bytes 6148
  831.1 54.8 %copy-start.127 = (f32[512]{0:T(512)S(1)}, f32[512]{0:T(512)}, u32[]{:S(2)}) copy-start(f32[512]{0:T(512)} %copy-done.126) | copy-start | bytes 6148
  935.2 124.1 %copy-start.96 = (f32[1024]{0:T(1024)}, f32[1024]{0:T(1024)S(1)}, u32[]{:S(2)}) copy-start(f32[1024]{0:T(1024)S(1)} %get-tuple-element.127) | copy-start | bytes 12292
  1126.8 33.0 %copy-start.94 = (f32[1,1024]{1,0:T(1,128)S(1)}, f32[1,1024]{1,0:T(1,128)}, u32[]{:S(2)}) copy-start(f32[1,1024]{1,0:T(1,128)} %copy-done.92) | copy-start | bytes 12292
  1159.7 320.9 %all-reduce.15.cloned.1.call-start = ((), (), s32[]{:S(2)}) async-start(), calls=%async_computation.10 | async-start | bytes 18612224 | tf_op jit(solution)/shard_map/psum | solution.py:233
  1259.0 61.0 %copy-start.52 = (f32[3,16,1024]{2,1,0:T(8,128)S(1)}, f32[3,16,1024]{2,1,0:T(8,128)}, u32[]{:S(2)}) copy-start(f32[3,16,1024]{2,1,0:T(8,128)} %get-tuple-element.37) | copy-start | bytes 589828
  1259.0 61.6 %copy-start.46 = (f32[2,16,2816]{2,1,0:T(8,128)S(1)}, f32[2,16,2816]{2,1,0:T(8,128)}, u32[]{:S(2)}) copy-start(f32[2,16,2816]{2,1,0:T(8,128)} %get-tuple-element.38) | copy-start | bytes 1081348
  1259.0 63.6 %copy-start.63 = (f32[1024,16]{0,1:T(8,128)S(1)}, f32[1024,16]{0,1:T(8,128)}, u32[]{:S(2)}) copy-start(f32[1024,16]{0,1:T(8,128)} %get-tuple-element.39) | copy-start | bytes 196612
  1259.0 64.9 %copy-start.53 = (f32[2816,16]{0,1:T(8,128)S(1)}, f32[2816,16]{0,1:T(8,128)}, u32[]{:S(2)}) copy-start(f32[2816,16]{0,1:T(8,128)} %get-tuple-element.40) | copy-start | bytes 540676
  1259.7 230.1 %copy-start.123 = (f32[512]{0:T(512)S(1)}, f32[512]{0:T(512)}, u32[]{:S(2)}) copy-start(f32[512]{0:T(512)} %copy-done.122) | copy-start | bytes 6148
  1318.8 168.1 %copy-start.90 = (f32[3,1024]{1,0:T(4,128)}, f32[3,1024]{1,0:T(4,128)S(1)}, u32[]{:S(2)}) copy-start(f32[3,1024]{1,0:T(4,128)S(1)} %get-tuple-element.34) | copy-start | bytes 36868
  1318.8 168.1 %copy-start.91 = (f32[2,2048]{1,0:T(2,128)}, f32[2,2048]{1,0:T(2,128)S(1)}, u32[]{:S(2)}) copy-start(f32[2,2048]{1,0:T(2,128)S(1)} %get-tuple-element.36) | copy-start | bytes 49156
  1320.0 174.9 %copy-start.55 = (f32[1024,16]{0,1:T(8,128)S(1)}, f32[1024,16]{0,1:T(8,128)}, u32[]{:S(2)}) copy-start(f32[1024,16]{0,1:T(8,128)} %param.54) | copy-start | bytes 196612
  (108 other events, 845.6 us)
Sparse Core Ops, SparseCore 0:
  10.2 53.2 all-gather.7
  65.7 49.0 all-gather.11
  117.0 49.0 all-gather.9
  168.1 51.6 all-gather.13
  255.3 106.0 all-reduce.8
  363.8 94.3 all-gather.17
  460.6 92.4 all-gather.15
  555.5 95.5 all-gather.19
  775.4 106.0 all-reduce.10
  1159.9 99.0 all-reduce.12
  1261.7 218.8 all-reduce.14
where the time goes:
time: 1530 us; the launch traced here: 1520 us
  waiting for transfers between devices  750 us (49%)
  matrix products  565 us (37%)
  blocking collectives  81.3 us (5%)
  other arithmetic  69.4 us (5%)
  local copies, waits for them, and re-layouts  31.4 us (2%)
  between operations  23.7 us (2%)
    psum x1, waiting for transfers between devices, body(): lax.psum(jnp.dot(hidden, merged[6], preferred_element_type=jnp.float32),...  148 us
    dot_general x7, matrix products, adapter_terms(): jnp.dot(direction_gradient, param_entry[2].T, precision=HIGH_PRECISION)  130 us
    dot_general x7, matrix products, merge_weights(): jnp.dot(param_entry[1], param_entry[2], precision=HIGH_PRECISION)  120 us
    psum x1, waiting for transfers between devices, body(): lax.psum(jnp.dot(mixed, merged[5], preferred_element_type=jnp.float32), '...  104 us
    dot_general x7, matrix products, adapter_terms(): jnp.dot(param_entry[1].T, direction_gradient, precision=HIGH_PRECISION)  93 us
    all_gather x1, waiting for transfers between devices, body(): lax.all_gather(base_widen, 'dp', axis=0, tiled=True)  91.1 us
    psum x1, waiting for transfers between devices, body(): lax.psum((gradients[0], gradients[1], gradients[2], gradients[3], gradien...  88.7 us
    all_gather x1, waiting for transfers between devices, body(): lax.all_gather(base_gate, 'dp', axis=0, tiled=True)  70 us
  transfers between devices with their start and end apart: 11, of which 11 were waited for; matrix products, arithmetic and copies ran while one was open for 14% of the time, Pallas kernels for 0%

commit v1 on v0

v1 whole, which is shorter than its diff:
```python
import jax
import jax.numpy as jnp
from jax import lax
from jax.sharding import PartitionSpec as P

HEAD_DIM = 128
SEQ = 256
STEP = 5


HIGH_PRECISION = lax.Precision.HIGHEST
ADAPTER_SCALE = 2.0
NORM_EPS = 1e-05
COLUMN_EPS = 1e-06
BETA_ONE = 0.9
BETA_TWO = 0.999
ADAM_EPS = 1e-08
DECAY = 0.01
CLIP = 1.0
RATE_FACTOR = 0.02
RATE_LIFT = 0.2
RATE_SCALE = 0.5
RATE_LOUD = 2.0
ROPE_BASE = 10000.0
MASKED = -1e30


def root_norm(values, gain):
    return values * lax.rsqrt(jnp.mean(values * values, axis=-1, keepdims=True) + NORM_EPS) * gain


def rotate(values, places, sign):
    half = values.shape[-1] // 2
    steps = jnp.arange(half, dtype=jnp.float32)
    frequency = ROPE_BASE ** (-2.0 * steps / values.shape[-1])
    angles = places.astype(jnp.float32)[:, None] * frequency[None, :]
    cosine = jnp.cos(angles)[:, None, :]
    sine = sign * jnp.sin(angles)[:, None, :]
    first = values[..., :half]
    second = values[..., half:]
    return jnp.concatenate(
        [first * cosine - second * sine, second * cosine + first * sine], axis=-1
    )


def allowed_of(padding, count):
    valid = padding.reshape(count, SEQ) > 0
    index = jnp.arange(SEQ)
    causal = index[:, None] >= index[None, :]
    itself = index[:, None] == index[None, :]
    return (causal[None] & valid[:, None, :] | itself[None])[:, None]


def squares_of(items):
    total = jnp.zeros((), jnp.float32)
    for param_entry in items:
        total = total + jnp.sum(param_entry * param_entry)
    return total


def decoupled_update(value, gradient, first, second, rate):
    momentum = BETA_ONE * first + (1.0 - BETA_ONE) * gradient
    variance = BETA_TWO * second + (1.0 - BETA_TWO) * gradient * gradient
    corrected = momentum / (1.0 - BETA_ONE**STEP)
    spread = jnp.sqrt(variance / (1.0 - BETA_TWO**STEP))
    return (value - rate * (corrected / (spread + ADAM_EPS) + DECAY * value), momentum, variance)


def swap(partial):
    low = partial.astype(jnp.bfloat16)
    size = lax.axis_size("tensor")
    total = low.astype(jnp.float32)
    for step in range(1, size):
        other = lax.ppermute(low, "tensor", [(i, (i + step) % size) for i in range(size)])
        total = total + other.astype(jnp.float32)
    return total


def matmul(left, right):
    return jnp.dot(left, right, preferred_element_type=jnp.float32)


def matmul_nt(left, right):
    return jnp.einsum("ik,jk->ij", left, right, preferred_element_type=jnp.float32)


def matmul_tn(left, right):
    return jnp.einsum("ki,kj->ij", left, right, preferred_element_type=jnp.float32)


def low(values):
    return values.astype(jnp.bfloat16)


def body(
    activations,
    cotangent,
    padding_mask,
    positions,
    norm_gains,
    base_query,
    base_key,
    base_value,
    base_gate,
    base_widen,
    base_mixer,
    base_funnel,
    entry_value,
    attend_value,
    widen_value,
    mixer_value,
    funnel_value,
    output_value,
    stature_value,
    amplitude_value,
    loudness_value,
    entry_first,
    attend_first,
    widen_first,
    mixer_first,
    funnel_first,
    output_first,
    stature_first,
    amplitude_first,
    loudness_first,
    entry_second,
    attend_second,
    widen_second,
    mixer_second,
    funnel_second,
    output_second,
    stature_second,
    amplitude_second,
    loudness_second,
):
    params = (
        entry_value,
        attend_value,
        widen_value,
        mixer_value,
        funnel_value,
        output_value,
        stature_value,
        amplitude_value,
        loudness_value,
    )
    firsts = (
        entry_first,
        attend_first,
        widen_first,
        mixer_first,
        funnel_first,
        output_first,
        stature_first,
        amplitude_first,
        loudness_first,
    )
    seconds = (
        entry_second,
        attend_second,
        widen_second,
        mixer_second,
        funnel_second,
        output_second,
        stature_second,
        amplitude_second,
        loudness_second,
    )
    rows = base_query.shape[0]
    width = activations.shape[1]
    place = lax.axis_index("dp") * rows
    side = lax.axis_index("tensor")
    sides = lax.axis_size("tensor")
    cut = base_query.shape[1]
    wide = base_gate.shape[1]
    entry_rows = lax.dynamic_slice_in_dim(entry_value, place, rows, 1)
    output_columns = lax.dynamic_slice_in_dim(output_value, place, rows, 2)
    firsts_in = [base_query, base_key, base_value, base_gate, base_widen]
    lifts = [attend_value[0], attend_value[1], attend_value[2], widen_value[0], widen_value[1]]
    shards = [
        base.astype(jnp.float32)
        + ADAPTER_SCALE * jnp.dot(entry_rows[i], lifts[i], precision=HIGH_PRECISION)
        for i, base in enumerate(firsts_in)
    ]
    shards += [
        base.T.astype(jnp.float32)
        + ADAPTER_SCALE * jnp.dot(output_columns[i].T, down.T, precision=HIGH_PRECISION)
        for i, (base, down) in enumerate(((base_mixer, mixer_value), (base_funnel, funnel_value)))
    ]
    split_squares = jnp.concatenate([jnp.sum(v * v, axis=0) for v in shards[:5]])
    split_wide = split_squares.shape[0]
    shared_squares = jnp.stack([jnp.sum(v * v, axis=1) for v in shards[5:]])
    split_all = lax.dynamic_update_slice(
        jnp.zeros((sides, split_wide), jnp.float32), split_squares[None], (side, 0)
    )
    shared_all = lax.dynamic_update_slice(
        jnp.zeros((2, width), jnp.float32), shared_squares, (0, place)
    )
    packed = lax.psum(
        jnp.concatenate([split_all.reshape(-1), shared_all.reshape(-1)]), ("dp", "tensor")
    )
    split_squares = lax.dynamic_slice_in_dim(packed, side * split_wide, split_wide)
    shared_squares = packed[sides * split_wide :].reshape(2, width)
    split_norms = jnp.sqrt(split_squares + COLUMN_EPS)
    shared_norms = jnp.sqrt(shared_squares + COLUMN_EPS)
    split_magnitudes = jnp.concatenate([stature_value.reshape(-1), amplitude_value.reshape(-1)])
    split_ratio = split_magnitudes / split_norms
    shared_ratio = loudness_value / shared_norms
    own_ratio = lax.dynamic_slice_in_dim(shared_ratio, place, rows, 1)
    attend_shard = jnp.concatenate(
        [low(shards[i] * split_ratio[None, i * cut : (i + 1) * cut]) for i in range(3)]
        + [low(shards[5] * own_ratio[0][:, None])],
        axis=1,
    )
    feed_shard = jnp.concatenate(
        [
            low(shards[3 + i] * split_ratio[None, 3 * cut + i * wide : 3 * cut + (i + 1) * wide])
            for i in range(2)
        ]
        + [low(shards[6] * own_ratio[1][:, None])],
        axis=1,
    )
    attend_all = lax.all_gather(attend_shard, "dp", axis=0, tiled=True)
    feed_all = lax.all_gather(feed_shard, "dp", axis=0, tiled=True)
    merged_attend = attend_all[:, : 3 * cut]
    merged_mixer = attend_all[:, 3 * cut :]
    merged_gate = feed_all[:, :wide]
    merged_widen = feed_all[:, wide : 2 * wide]
    merged_funnel = feed_all[:, 2 * wide :]

    count = activations.shape[0] // SEQ
    heads = cut // HEAD_DIM
    scale = HEAD_DIM ** (-0.5)
    floats = activations.astype(jnp.float32)
    normed_one = low(root_norm(floats, norm_gains[0]))
    projected = matmul(normed_one, merged_attend)
    queries = projected[:, :cut]
    keys = projected[:, cut : 2 * cut]
    values = projected[:, 2 * cut :]
    values_low = low(values).reshape(count, SEQ, heads, HEAD_DIM)
    turned_queries = low(rotate(queries.reshape(-1, heads, HEAD_DIM), positions, 1.0))
    turned_queries = turned_queries.reshape(count, SEQ, heads, HEAD_DIM)
    turned_keys = low(rotate(keys.reshape(-1, heads, HEAD_DIM), positions, 1.0))
    turned_keys = turned_keys.reshape(count, SEQ, heads, HEAD_DIM)
    allowed = allowed_of(padding_mask, count)
    scores = (
        jnp.einsum(
            "bqhd,bkhd->bhqk", turned_queries, turned_keys, preferred_element_type=jnp.float32
        )
        * scale
    )
    masked = jnp.where(allowed, scores, MASKED)
    top = jnp.max(masked, axis=-1, keepdims=True)
    log_total = top + jnp.log(jnp.sum(jnp.exp(masked - top), axis=-1, keepdims=True))
    attention = jnp.exp(masked - log_total)
    attention_low = low(attention)
    mixed = jnp.einsum(
        "bhqk,bkhd->bqhd", attention_low, values_low, preferred_element_type=jnp.float32
    )
    mixed = low(mixed.reshape(activations.shape[0], cut))
    attended = swap(matmul_nt(mixed, merged_mixer))
    residual = floats + attended
    normed_two = low(root_norm(residual, norm_gains[1]))
    gate = matmul(normed_two, merged_gate)
    lifted = matmul(normed_two, merged_widen)
    hidden = low(jax.nn.silu(gate) * lifted)
    funneled = swap(matmul_nt(hidden, merged_funnel))
    block_output = low(residual + funneled)

    back = cotangent.astype(jnp.float32)
    d_hidden = matmul(cotangent, merged_funnel)
    unused, silu_pull = jax.vjp(lambda g, u: jax.nn.silu(g) * u, gate, lifted)
    d_gate, d_lifted = silu_pull(d_hidden)
    d_gate = low(d_gate)
    d_lifted = low(d_lifted)
    d_normed_two = swap(matmul_nt(d_gate, merged_gate) + matmul_nt(d_lifted, merged_widen))
    unused, second_pull = jax.vjp(lambda v: root_norm(v, norm_gains[1]), residual)
    d_residual = back + second_pull(d_normed_two)[0]
    d_residual_low = low(d_residual)
    d_mixed = low(matmul(d_residual_low, merged_mixer)).reshape(count, SEQ, heads, HEAD_DIM)
    d_attention = jnp.einsum(
        "bqhd,bkhd->bhqk", d_mixed, values_low, preferred_element_type=jnp.float32
    )
    d_values = jnp.einsum(
        "bhqk,bqhd->bkhd", attention_low, d_mixed, preferred_element_type=jnp.float32
    )
    d_values = low(d_values).reshape(-1, cut)
    d_scores = attention * (d_attention - jnp.sum(attention * d_attention, axis=-1, keepdims=True))
    d_scores = low(d_scores)
    d_turned_queries = (
        jnp.einsum("bhqk,bkhd->bqhd", d_scores, turned_keys, preferred_element_type=jnp.float32)
        * scale
    )
    d_turned_keys = (
        jnp.einsum("bhqk,bqhd->bkhd", d_scores, turned_queries, preferred_element_type=jnp.float32)
        * scale
    )
    d_queries = low(rotate(d_turned_queries.reshape(-1, heads, HEAD_DIM), positions, -1.0))
    d_keys = low(rotate(d_turned_keys.reshape(-1, heads, HEAD_DIM), positions, -1.0))
    d_queries = d_queries.reshape(-1, cut)
    d_keys = d_keys.reshape(-1, cut)
    d_projected = jnp.concatenate([d_queries, d_keys, d_values], axis=1)
    d_normed_one = swap(matmul_nt(d_projected, merged_attend))
    unused, first_pull = jax.vjp(lambda v: root_norm(v, norm_gains[0]), floats)
    input_gradient = d_residual + first_pull(d_normed_one)[0]

    d_parts = (d_queries, d_keys, d_values, d_gate, d_lifted)
    parts = (queries, keys, values, gate, lifted)
    split_dots = jnp.concatenate(
        [jnp.sum(d.astype(jnp.float32) * y, axis=0) for d, y in zip(d_parts, parts)]
    )
    shared_dots = jnp.stack(
        [
            jnp.sum(d_residual_low.astype(jnp.float32) * attended, axis=0),
            jnp.sum(back * funneled, axis=0),
        ]
    )
    split_pull = split_dots / (split_norms * split_magnitudes)
    shared_pull = shared_dots / (shared_norms * loudness_value)

    down_gradients = []
    up_gradients = []
    inputs = (normed_one, normed_one, normed_one, normed_two, normed_two)
    weights = (
        merged_attend[:, :cut],
        merged_attend[:, cut : 2 * cut],
        merged_attend[:, 2 * cut :],
        merged_gate,
        merged_widen,
    )
    offset = 0
    for i in range(5):
        out = weights[i].shape[1]
        ratio = split_ratio[offset : offset + out]
        pull = split_pull[offset : offset + out]
        offset += out
        low_lift = low(lifts[i] * ratio)
        pull_lift = low(lifts[i] * pull)
        lowered = low(matmul_nt(low_lift, d_parts[i]))
        down_gradients.append(
            ADAPTER_SCALE * (matmul(lowered, inputs[i]) - matmul_nt(pull_lift, weights[i]))
        )
        low_down = low(entry_value[i])
        reduced = low(matmul(inputs[i], low_down))
        up_gradients.append(
            ADAPTER_SCALE
            * (matmul_tn(reduced, d_parts[i]) * ratio - matmul_tn(low_down, weights[i]) * pull)
        )
    out_downs = []
    out_ups = []
    plan = (
        (mixed, d_residual_low, mixer_value, merged_mixer),
        (hidden, cotangent, funnel_value, merged_funnel),
    )
    for i, (source, d_out, down, weight) in enumerate(plan):
        low_lift = low(output_value[i] * shared_ratio[i])
        pull_lift = low(output_value[i] * shared_pull[i])
        lowered = low(matmul_nt(low_lift, d_out))
        out_downs.append(ADAPTER_SCALE * (matmul(lowered, source) - matmul(pull_lift, weight)))
        low_down = low(down)
        reduced = low(matmul(source, low_down))
        out_ups.append(
            ADAPTER_SCALE
            * (
                matmul_tn(reduced, d_out) * shared_ratio[i]
                - jnp.einsum("ir,ji->rj", low_down, weight, preferred_element_type=jnp.float32)
                * shared_pull[i]
            )
        )
    shared_terms = jnp.concatenate(down_gradients + out_ups, axis=1)
    split_terms = jnp.concatenate(up_gradients + out_downs, axis=1)
    shared_terms, split_terms, split_dots, shared_dots = lax.psum(
        (shared_terms, split_terms, split_dots, shared_dots), "dp"
    )
    split_scale = split_dots / split_magnitudes
    shared_scale = shared_dots / loudness_value
    split_total = jnp.sum(split_terms * split_terms) + jnp.sum(split_scale * split_scale)
    shared_terms, split_total = lax.psum((shared_terms, split_total), "tensor")
    totals = (
        jnp.stack([shared_terms[:, i * width : (i + 1) * width].T for i in range(5)]),
        jnp.stack([split_terms[:, i * cut : (i + 1) * cut] for i in range(3)]),
        jnp.stack([split_terms[:, 3 * cut + i * wide : 3 * cut + (i + 1) * wide] for i in range(2)]),
        split_terms[:, split_wide : split_wide + cut].T,
        split_terms[:, split_wide + cut :].T,
        jnp.stack([shared_terms[:, (5 + i) * width : (6 + i) * width] for i in range(2)]),
        split_scale[: 3 * cut].reshape(3, cut),
        split_scale[3 * cut :].reshape(2, wide),
        shared_scale,
    )
    gradient_norm = jnp.sqrt(split_total + squares_of((totals[0], totals[5], totals[8])))
    down_factor = jnp.minimum(1.0, CLIP / (gradient_norm + 1e-06))
    rates = (
        RATE_FACTOR,
        RATE_LIFT,
        RATE_LIFT,
        RATE_FACTOR,
        RATE_FACTOR,
        RATE_LIFT,
        RATE_SCALE,
        RATE_SCALE,
        RATE_LOUD,
    )
    updated = []
    momenta = []
    variances = []
    for value, gradient, first, second, rate in zip(params, totals, firsts, seconds, rates):
        fresh, momentum, variance = decoupled_update(
            value, gradient * down_factor, first, second, rate
        )
        updated.append(fresh)
        momenta.append(momentum)
        variances.append(variance)
    return (
        block_output,
        input_gradient,
        gradient_norm,
        updated[0],
        updated[1],
        updated[2],
        updated[3],
        updated[4],
        updated[5],
        updated[6],
        updated[7],
        updated[8],
        momenta[0],
        momenta[1],
        momenta[2],
        momenta[3],
        momenta[4],
        momenta[5],
        momenta[6],
        momenta[7],
        momenta[8],
        variances[0],
        variances[1],
        variances[2],
        variances[3],
        variances[4],
        variances[5],
        variances[6],
        variances[7],
        variances[8],
    )


def solution(mesh):
    return jax.shard_map(
        body,
        mesh=mesh,
        in_specs=(
            P("dp", None),
            P("dp", None),
            P("dp"),
            P("dp"),
            P(),
            P("dp", "tensor"),
            P("dp", "tensor"),
            P("dp", "tensor"),
            P("dp", "tensor"),
            P("dp", "tensor"),
            P("tensor", "dp"),
            P("tensor", "dp"),
            P(),
            P(None, None, "tensor"),
            P(None, None, "tensor"),
            P("tensor", None),
            P("tensor", None),
            P(),
            P(None, "tensor"),
            P(None, "tensor"),
            P(),
            P(),
            P(None, None, "tensor"),
            P(None, None, "tensor"),
            P("tensor", None),
            P("tensor", None),
            P(),
            P(None, "tensor"),
            P(None, "tensor"),
            P(),
            P(),
            P(None, None, "tensor"),
            P(None, None, "tensor"),
            P("tensor", None),
            P("tensor", None),
            P(),
            P(None, "tensor"),
            P(None, "tensor"),
            P(),
        ),
        out_specs=(
            P("dp", None),
            P("dp", None),
            P(),
            P(),
            P(None, None, "tensor"),
            P(None, None, "tensor"),
            P("tensor", None),
            P("tensor", None),
            P(),
            P(None, "tensor"),
            P(None, "tensor"),
            P(),
            P(),
            P(None, None, "tensor"),
            P(None, None, "tensor"),
            P("tensor", None),
            P("tensor", None),
            P(),
            P(None, "tensor"),
            P(None, "tensor"),
            P(),
            P(),
            P(None, None, "tensor"),
            P(None, None, "tensor"),
            P("tensor", None),
            P("tensor", None),
            P(),
            P(None, "tensor"),
            P(None, "tensor"),
            P(),
        ),
        check_vma=False,
    )
```

time: 1530 us -> 1030 us (0.67)
  matrix products: 565 us -> 254 us
  waiting for transfers between devices: 750 us -> 568 us
    dot_general x44 -> x47, matrix products: 552 us -> 247 us  [the longest x14 90.6 us: matmul(): return jnp.dot(left, right, preferred_element_type=jnp.float32)]
    psum x4 -> x3, waiting for transfers between devices: 391 us -> 230 us  [the longest x1 122 us: body(): lax.psum(jnp.concatenate([split_all.reshape(-1), shared_all.reshape(-1)])...]
    all_gather x7 -> x2, waiting for transfers between devices: 354 us -> 212 us  [the longest x1 119 us: body(): attend_all = lax.all_gather(attend_shard, 'dp', axis=0, tiled=True)]
    ppermute x0 -> x4, waiting for transfers between devices: none -> 125 us  [swap(): lax.ppermute(low, 'tensor', [(i, (i + step) % size) for i in range(size)])]
    psum x5 -> x2, blocking collectives: 81.3 us -> 66.2 us  [the longest x1 60.6 us: body(): lax.psum((shared_terms, split_terms, split_dots, shared_dots), 'dp')]
  transfers between devices with their start and end apart: 11 -> 9, of which waited for: 11 -> 8; matrix products, arithmetic and copies ran while one was open for 14% -> 9% of each run, Pallas kernels for 0% -> 0%
where the time goes in v1:
time: 1030 us
  waiting for transfers between devices  568 us (55%)
  matrix products  254 us (25%)
  other arithmetic  69.6 us (7%)
  blocking collectives  66.2 us (6%)
  local copies, waits for them, and re-layouts  42 us (4%)
  between operations  20.6 us (2%)
    ppermute x4, waiting for transfers between devices, swap(): lax.ppermute(low, 'tensor', [(i, (i + step) % size) for i in range(size)])  125 us
    psum x1, waiting for transfers between devices, body(): lax.psum(jnp.concatenate([split_all.reshape(-1), shared_all.reshape(-1)])...  122 us
    all_gather x1, waiting for transfers between devices, body(): attend_all = lax.all_gather(attend_shard, 'dp', axis=0, tiled=True)  119 us
    all_gather x1, waiting for transfers between devices, body(): feed_all = lax.all_gather(feed_shard, 'dp', axis=0, tiled=True)  93 us
    dot_general x14, matrix products, matmul(): return jnp.dot(left, right, preferred_element_type=jnp.float32)  90.6 us
    psum x1, waiting for transfers between devices, body(): lax.psum((shared_terms, split_terms, split_dots, shared_dots), 'dp')  80.5 us
    dot_general x10, matrix products, matmul_nt(): jnp.einsum('ik,jk->ij', left, right, preferred_element_type=jnp.float32)  69.2 us
    psum x1, blocking collectives, body(): lax.psum((shared_terms, split_terms, split_dots, shared_dots), 'dp')  60.6 us
  transfers between devices with their start and end apart: 9, of which 8 were waited for; matrix products, arithmetic and copies ran while one was open for 9% of the time, Pallas kernels for 0%

profile of v1, /device:TPU:0, one launch (start us, length us, event | category | flops | bytes accessed | tf_op | source)
XLA Modules:
  0.0 1025.8 jit_solution(12212841516849262805)
XLA Ops:
  25.1 3.8 multiply_reduce_fusion.9
  32.3 122.2 %all-reduce.6.cloned.1.call-done = f32[21504]{0:T(1024)} async-done(((f32[21504]{0:T(1024)}), f32[21504]{0:T(1024)}) %all-reduce.6.cloned.1.call-update) | async-done | bytes 86032 | tf_op jit(solution)/shard_map/psum | solution.py:199
  170.8 119.3 %all-gather.3.cloned.1.call-done = bf16[2048,4096]{1,0:T(8,128)(2,1)} async-done(((bf16[128,4096]{1,0:T(8,128)(2,1)}), bf16[2048,4096]{1,0:T(8,128)(2,1)}) %all-gather.3.cloned.1.call-update) | async-done | bytes 16777232 | tf_op jit(solution)/shard_map/all_gather | solution.py:223
  290.1 10.2 fusion.2
  313.6 4.9 convolution_convert_fusion
  319.8 46.5 %collective-permute-done = bf16[512,2048]{1,0:T(8,128)(2,1)S(1)} collective-permute-done((bf16[512,2048]{1,0:T(8,128)(2,1)S(1)}, bf16[512,2048]{1,0:T(8,128)(2,1)S(1)}, u32[]{:S(2)}, u32[]{:S(2)}) %collective-permute-start) | collective-permute-done | bytes 2097184 | tf_op jit(solution)/shard_map/ppermute | solution.py:74
  370.6 93.0 %all-gather.5.cloned.1.call-done = bf16[2048,8448]{1,0:T(8,128)(2,1)} async-done(((bf16[128,8448]{1,0:T(8,128)(2,1)}), bf16[2048,8448]{1,0:T(8,128)(2,1)}) %all-gather.5.cloned.1.call-update) | async-done | bytes 34603024 | tf_op jit(solution)/shard_map/all_gather | solution.py:224
  463.5 12.7 %fusion.18 = f32[512,2816]{1,0:T(8,128)} fusion(bf16[512,2048]{1,0:T(8,128)(2,1)} %multiply_convert_fusion.2, bf16[2048,8448]{1,0:T(8,128)(2,1)} %all-gather.5.cloned.1.call-done), kind=kOutput, calls=%fused_computation.24 | convolution fusion | flops 5905580032 | bytes 19398656 | tf_op jit(solution)/shard_map/dot_general | solution.py:80
  476.2 11.2 %fusion.8 = f32[2816,512]{0,1:T(8,128)} fusion(bf16[512,2048]{1,0:T(8,128)(2,1)S(1)} %copy-done.9, bf16[2048,8448]{1,0:T(8,128)(2,1)} %all-gather.5.cloned.1.call-done), kind=kOutput, calls=%fused_computation.14 | convolution fusion | flops 5905580032 | bytes 19398656 | tf_op jit(solution)/shard_map/dot_general | solution.py:80
  487.5 16.2 %multiply_reduce_fusion.1 = (f32[2816]{0:T(1024)}, bf16[512,2816]{1,0:T(8,128)(2,1)S(1)}, f32[2816]{0:T(1024)}, bf16[512,2816]{1,0:T(8,128)(2,1)S(1)}, bf16[512,2816]{1,0:T(8,128)(2,1)}) fusion(f32[512,2816]{1,0:T(8,128)} %fusion.18, f32[2816,512]{0,1:T(8,128)} %fusion.8, bf16[512,2048]{1,0:T(8,128)(2,1)S(1)} %copy-done.3, ...), kind=kOutput, calls=%fused_computation.43 | convolution fusion | flops 5937293312 | bytes 33839104 | tf_op jit(solution)/shard_map/dot_general | solution.py:80
  503.6 11.1 %fusion.16 = f32[512,2048]{1,0:T(8,128)S(1)} fusion(bf16[512,2816]{1,0:T(8,128)(2,1)S(1)} %get-tuple-element.76, bf16[2048,8448]{1,0:T(8,128)(2,1)} %all-gather.5.cloned.1.call-done), kind=kOutput, calls=%fused_computation.22 | convolution fusion | flops 5905580032 | bytes 18612224 | tf_op jit(solution)/shard_map/ik,jk->ij/dot_general | solution.py:84
  514.7 9.2 add_convert_fusion
  525.5 9.2 fusion.82
  536.7 35.8 %collective-permute-done.2 = bf16[512,2048]{1,0:T(8,128)(2,1)S(1)} collective-permute-done((bf16[512,2048]{1,0:T(8,128)(2,1)S(1)}, bf16[512,2048]{1,0:T(8,128)(2,1)S(1)}, u32[]{:S(2)}, u32[]{:S(2)}) %collective-permute-start.2) | collective-permute-done | bytes 2097184 | tf_op jit(solution)/shard_map/ppermute | solution.py:74
  574.1 42.7 %collective-permute-done.1 = bf16[512,2048]{1,0:T(8,128)(2,1)S(1)} collective-permute-done((bf16[512,2048]{1,0:T(8,128)(2,1)S(1)}, bf16[512,2048]{1,0:T(8,128)(2,1)S(1)}, u32[]{:S(2)}, u32[]{:S(2)}) %collective-permute-start.1) | collective-permute-done | bytes 2097184 | tf_op jit(solution)/shard_map/ppermute | solution.py:74
  616.8 7.3 multiply_reduce_fusion.2
  624.0 5.3 fusion.129
  631.1 4.4 multiply_reduce_fusion.3
  650.4 4.8 multiply_subtract_fusion.1
  659.0 60.6 %all-reduce = (f32[8704]{0:T(1024)}, f32[2,2048]{1,0:T(2,128)}) all-reduce(f32[8704]{0:T(1024)S(1)} %constant_dynamic-update-slice_fusion.9, f32[2,2048]{1,0:T(2,128)} %pad_maximum_fusion.10), channel_id=1, replica_groups=mesh['dp'=16,'tensor'=2] {'dp'}, use_global_device_ids=true, to_apply=%region_24.25 | all-reduce | flops 12800 | bytes 102400 | tf_op jit(solution)/shard_map/psum | solution.py:372
  721.7 3.7 fusion.197
  728.8 3.6 fusion.195
  746.1 3.4 fusion.198
  755.9 4.2 fusion.42
  763.1 5.9 fusion.20
  769.0 4.3 fusion.104
  773.4 6.1 fusion.12
  779.5 4.3 fusion.106
  783.8 4.2 fusion.110
  788.0 3.5 fusion.118
  791.5 6.0 fusion.65
  797.5 3.5 fusion.186
  801.0 3.5 fusion.177
  804.5 3.5 fusion.168
  808.0 4.9 fusion.56
  813.0 5.9 fusion.71
  818.9 5.0 fusion.59
  823.8 6.3 fusion.122
  830.2 4.9 fusion.115
  835.1 5.9 fusion.6
  841.0 3.5 fusion.192
  844.5 4.2 fusion.61
  848.8 11.8 %fusion.85 = bf16[512,2048]{1,0:T(8,128)(2,1)} fusion(bf16[2048,4096]{1,0:T(8,128)(2,1)} %all-gather.3.cloned.1.call-done, bf16[512,1024]{1,0:T(8,128)(2,1)} %bitcast.398, bf16[512,1024]{1,0:T(8,128)(2,1)} %bitcast.397, bf16[512,1024]{1,0:T(8,128)(2,1)} %bitcast.396), kind=kOutput, calls=%fused_computation.111 | convolution fusion | flops 6452936704 | bytes 17825792 | tf_op jit(solution)/shard_map/ik,jk->ij/dot_general | solution.py:84
  862.0 80.5 %all-reduce.10.cloned.1.call-done = (f32[16,12544]{1,0:T(8,128)}, f32[16,14336]{1,0:T(8,128)}) async-done(((f32[16,12544]{1,0:T(8,128)}, f32[16,14336]{1,0:T(8,128)}), (f32[16,12544]{1,0:T(8,128)}, f32[16,14336]{1,0:T(8,128)})) %all-reduce.10.cloned.1.call-update) | async-done | bytes 1720336 | tf_op jit(solution)/shard_map/psum | solution.py:372
  945.8 5.6 psum.52
  954.8 27.7 %all-reduce.8.cloned.1.call-done = f32[16,14336]{1,0:T(8,128)} async-done(((f32[16,14336]{1,0:T(8,128)}), f32[16,14336]{1,0:T(8,128)}) %all-reduce.8.cloned.1.call-update) | async-done | bytes 917520 | tf_op jit(solution)/shard_map/psum | solution.py:378
  1008.9 3.4 fusion.38
  1012.3 5.6 fusion.34
  (392 shorter events, 139.8 us)
Async XLA Ops:
  7.2 7.7 copy-start.43
  7.2 10.1 copy-start.29
  7.2 147.2 %all-reduce.6.cloned.1.call-start = ((), (), s32[]{:S(2)}) async-start(), calls=%async_computation | async-start | bytes 172032 | tf_op jit(solution)/shard_map/psum | solution.py:199
  9.8 7.5 copy-start.44
  19.5 9.4 copy-start.47
  19.6 12.6 %copy-start.88 = (f32[3,1024]{1,0:T(4,128)S(1)}, f32[3,1024]{1,0:T(4,128)}, u32[]{:S(2)}) copy-start(f32[3,1024]{1,0:T(4,128)} %param.57) | copy-start | bytes 36868
  19.6 12.6 %copy-start.75 = (f32[2,2816]{1,0:T(2,128)S(1)}, f32[2,2816]{1,0:T(2,128)}, u32[]{:S(2)}) copy-start(f32[2,2816]{1,0:T(2,128)} %param.58) | copy-start | bytes 67588
  21.1 134.1 %copy-start.66 = (f32[2,2048]{1,0:T(2,128)S(1)}, f32[2,2048]{1,0:T(2,128)}, u32[]{:S(2)}) copy-start(f32[2,2048]{1,0:T(2,128)} %param.59) | copy-start | bytes 49156
  25.1 133.8 %copy-start.37 = (f32[128,1024]{1,0:T(8,128)S(1)}, f32[128,1024]{1,0:T(8,128)}, u32[]{:S(2)}) copy-start(f32[128,1024]{1,0:T(8,128)} %get-tuple-element.131) | copy-start | bytes 1572868
  32.1 258.0 %all-gather.3.cloned.1.call-start = ((), (), s32[]{:S(2)}) async-start(), calls=%async_computation.1 | async-start | bytes 17825792 | tf_op jit(solution)/shard_map/all_gather | solution.py:223
  32.2 128.9 %copy-start.55 = (f32[8704]{0:T(1024)}, f32[8704]{0:T(1024)S(1)}, u32[]{:S(2)}) copy-start(f32[8704]{0:T(1024)S(1)} %constant_dynamic-update-slice_fusion.3) | copy-start | bytes 104452
  161.2 302.3 %all-gather.5.cloned.1.call-start = ((), (), s32[]{:S(2)}) async-start(), calls=%async_computation.2 | async-start | bytes 36765696 | tf_op jit(solution)/shard_map/all_gather | solution.py:224
  164.6 777.9 %all-reduce.10.cloned.1.call-start = ((), (), s32[]{:S(2)}) async-start(), calls=%async_computation.4 | async-start | bytes 3440640 | tf_op jit(solution)/shard_map/psum | solution.py:372
  165.9 134.4 %copy-start.109 = (f32[512]{0:T(512)}, f32[512]{0:T(512)S(1)}, u32[]{:S(2)}) copy-start(f32[512]{0:T(512)S(1)} %fusion.309) | copy-start | bytes 6148
  168.9 131.5 %copy-start.71 = (f32[1,2048]{1,0:T(1,128)}, f32[1,2048]{1,0:T(1,128)S(1)}, u32[]{:S(2)}) copy-start(f32[1,2048]{1,0:T(1,128)S(1)} %get-tuple-element.117) | copy-start | bytes 24580
  318.6 48.8 %copy-start.4 = (bf16[512,2048]{1,0:T(8,128)(2,1)}, bf16[512,2048]{1,0:T(8,128)(2,1)S(1)}, u32[]{:S(2)}) copy-start(bf16[512,2048]{1,0:T(8,128)(2,1)S(1)} %convolution_convert_fusion) | copy-start | bytes 6291460
  318.6 49.0 %copy-start.73 = (f32[1,2048]{1,0:T(1,128)S(1)}, f32[1,2048]{1,0:T(1,128)}, u32[]{:S(2)}) copy-start(f32[1,2048]{1,0:T(1,128)} %get-tuple-element.118) | copy-start | bytes 24580
  318.6 47.7 %collective-permute-start = (bf16[512,2048]{1,0:T(8,128)(2,1)S(1)}, bf16[512,2048]{1,0:T(8,128)(2,1)S(1)}, u32[]{:S(2)}, u32[]{:S(2)}) collective-permute-start(bf16[512,2048]{1,0:T(8,128)(2,1)S(1)} %convolution_convert_fusion), channel_id=1, source_target_pairs={{0,1},{1,0},{2,3},{3,2},{4,5},{5,4},{6,7},{7,6},{8,9},{9,8},{10,11... | collective-permute-start | bytes 6291464 | tf_op jit(solution)/shard_map/ppermute | solution.py:74
  463.5 12.7 %copy-start.9 = (bf16[512,2048]{1,0:T(8,128)(2,1)S(1)}, bf16[512,2048]{1,0:T(8,128)(2,1)}, u32[]{:S(2)}) copy-start(bf16[512,2048]{1,0:T(8,128)(2,1)} %param.40) | copy-start | bytes 6291460
  476.2 11.2 %copy-start.3 = (bf16[512,2048]{1,0:T(8,128)(2,1)S(1)}, bf16[512,2048]{1,0:T(8,128)(2,1)}, u32[]{:S(2)}) copy-start(bf16[512,2048]{1,0:T(8,128)(2,1)} %multiply_convert_fusion.2) | copy-start | bytes 6291460
  503.6 11.1 %copy-start.16 = (bf16[512,2816]{1,0:T(8,128)(2,1)}, bf16[512,2816]{1,0:T(8,128)(2,1)S(1)}, u32[]{:S(2)}) copy-start(bf16[512,2816]{1,0:T(8,128)(2,1)S(1)} %get-tuple-element.76) | copy-start | bytes 8650756
  503.6 11.1 %copy-start.17 = (bf16[512,2816]{1,0:T(8,128)(2,1)}, bf16[512,2816]{1,0:T(8,128)(2,1)S(1)}, u32[]{:S(2)}) copy-start(bf16[512,2816]{1,0:T(8,128)(2,1)S(1)} %get-tuple-element.74) | copy-start | bytes 8650756
  514.7 10.8 %copy-start.18 = (bf16[512,2816]{1,0:T(8,128)(2,1)S(1)}, bf16[512,2816]{1,0:T(8,128)(2,1)}, u32[]{:S(2)}) copy-start(bf16[512,2816]{1,0:T(8,128)(2,1)} %get-tuple-element.77) | copy-start | bytes 8650756
  524.0 48.5 %collective-permute-start.2 = (bf16[512,2048]{1,0:T(8,128)(2,1)S(1)}, bf16[512,2048]{1,0:T(8,128)(2,1)S(1)}, u32[]{:S(2)}, u32[]{:S(2)}) collective-permute-start(bf16[512,2048]{1,0:T(8,128)(2,1)S(1)} %add_convert_fusion), channel_id=1, source_target_pairs={{0,1},{1,0},{2,3},{3,2},{4,5},{5,4},{6,7},{7,6},{8,9},{9,8},{10,11... | collective-permute-start | bytes 6291464 | tf_op jit(solution)/shard_map/ppermute | solution.py:74
  525.5 9.8 copy-start.35
  525.5 10.6 %copy-start.84 = (f32[2,2048]{1,0:T(2,128)S(1)}, f32[2,2048]{1,0:T(2,128)}, u32[]{:S(2)}) copy-start(f32[2,2048]{1,0:T(2,128)} %copy-done.83) | copy-start | bytes 49156
  525.5 47.0 %copy-start.5 = (bf16[512,2048]{1,0:T(8,128)(2,1)S(1)}, bf16[512,2048]{1,0:T(8,128)(2,1)}, u32[]{:S(2)}) copy-start(bf16[512,2048]{1,0:T(8,128)(2,1)} %copy-done.4) | copy-start | bytes 6291460
  525.5 47.0 %copy-start.7 = (bf16[512,2048]{1,0:T(8,128)(2,1)S(1)}, bf16[512,2048]{1,0:T(8,128)(2,1)}, u32[]{:S(2)}) copy-start(bf16[512,2048]{1,0:T(8,128)(2,1)} %copy-done.6) | copy-start | bytes 6291460
  525.5 47.0 %copy-start.74 = (f32[1,2048]{1,0:T(1,128)S(1)}, f32[1,2048]{1,0:T(1,128)}, u32[]{:S(2)}) copy-start(f32[1,2048]{1,0:T(1,128)} %get-tuple-element.118) | copy-start | bytes 24580
  534.7 82.0 %collective-permute-start.1 = (bf16[512,2048]{1,0:T(8,128)(2,1)S(1)}, bf16[512,2048]{1,0:T(8,128)(2,1)S(1)}, u32[]{:S(2)}, u32[]{:S(2)}) collective-permute-start(bf16[512,2048]{1,0:T(8,128)(2,1)S(1)} %fusion.82), channel_id=1, source_target_pairs={{0,1},{1,0},{2,3},{3,2},{4,5},{5,4},{6,7},{7,6},{8,9},{9,8},{10,11... | collective-permute-start | bytes 6291464 | tf_op jit(solution)/shard_map/ppermute | solution.py:74
  656.6 63.0 %copy-start.56 = (f32[8704]{0:T(1024)S(1)}, f32[8704]{0:T(1024)}, u32[]{:S(2)}) copy-start(f32[8704]{0:T(1024)} %copy-done.55) | copy-start | bytes 104452
  656.7 65.0 %copy-start.38 = (bf16[5,2048,16]{1,2,0:T(8,128)(2,1)S(1)}, bf16[5,2048,16]{1,2,0:T(8,128)(2,1)}, u32[]{:S(2)}) copy-start(bf16[5,2048,16]{1,2,0:T(8,128)(2,1)} %convert.29) | copy-start | bytes 983044
  721.6 17.8 %copy-start.101 = (f32[1024]{0:T(1024)}, f32[1024]{0:T(1024)S(1)}, u32[]{:S(2)}) copy-start(f32[1024]{0:T(1024)S(1)} %get-tuple-element.106) | copy-start | bytes 12292
  721.7 27.9 %copy-start.99 = (f32[1024]{0:T(1024)}, f32[1024]{0:T(1024)S(1)}, u32[]{:S(2)}) copy-start(f32[1024]{0:T(1024)S(1)} %get-tuple-element.105) | copy-start | bytes 12292
  721.7 34.3 %copy-start.97 = (f32[1024]{0:T(1024)}, f32[1024]{0:T(1024)S(1)}, u32[]{:S(2)}) copy-start(f32[1024]{0:T(1024)S(1)} %get-tuple-element.104) | copy-start | bytes 12292
  721.7 7.1 copy-start.92
  732.4 7.0 copy-start.33
  739.4 6.7 copy-start.78
  755.9 7.2 copy-start.30
  848.7 133.7 %all-reduce.8.cloned.1.call-start = ((), (), s32[]{:S(2)}) async-start(), calls=%async_computation.3 | async-start | bytes 1835008 | tf_op jit(solution)/shard_map/psum | solution.py:378
  860.6 132.2 %copy-start.65 = (f32[8704]{0:T(1024)S(1)}, f32[8704]{0:T(1024)}, u32[]{:S(2)}) copy-start(f32[8704]{0:T(1024)} %get-tuple-element.67) | copy-start | bytes 104452
  860.6 148.3 %collective-permute-start.3 = (bf16[512,2048]{1,0:T(8,128)(2,1)}, bf16[512,2048]{1,0:T(8,128)(2,1)}, u32[]{:S(2)}, u32[]{:S(2)}) collective-permute-start(bf16[512,2048]{1,0:T(8,128)(2,1)} %fusion.85), channel_id=1, source_target_pairs={{0,1},{1,0},{2,3},{3,2},{4,5},{5,4},{6,7},{7,6},{8,9},{9,8},{10,11... | collective-permute-start | bytes 6291464 | tf_op jit(solution)/shard_map/ppermute | solution.py:74
  997.6 6.6 copy-start.34
  997.6 6.6 copy-start.52
  999.5 8.1 copy-start.45
  999.6 8.1 copy-start.46
  999.6 8.1 copy-start.48
  999.6 8.1 copy-start.49
  (84 other events, 348.3 us)
Sparse Core Ops, SparseCore 0:
  32.2 122.1 all-reduce.5
  161.3 128.8 all-gather.2
  292.3 171.1 all-gather.4
  848.9 93.6 all-reduce.9
  945.9 36.4 all-reduce.7

commit v2 on v1

--- a/solution.py
+++ b/solution.py
@@ -1,6 +1,10 @@
+import functools
+
 import jax
 import jax.numpy as jnp
 from jax import lax
+from jax.experimental import pallas as pl
+from jax.experimental.pallas import tpu as pltpu
 from jax.sharding import PartitionSpec as P
 
 HEAD_DIM = 128
@@ -90,6 +94,186 @@
 
 def low(values):
     return values.astype(jnp.bfloat16)
+
+
+MESH = pl.DeviceIdType.MESH
+LANES = 1024
+CHUNK = 256
+
+
+def partners_of(size):
+    me = lax.axis_index("dp")
+    found = []
+    bit = 1
+    while bit < size:
+        down = lax.rem(lax.div(me, bit), 2)
+        found.append(me + bit - 2 * bit * down)
+        bit *= 2
+    return found
+
+
+def double_sum(total, inbox, sends, receives, size, sides, shared_rows):
+    targets = [({"dp": p}, total.shape[0]) for p in partners_of(size)]
+    side = lax.axis_index("tensor")
+    targets += [
+        ({"tensor": lax.rem(side + step, sides)}, shared_rows) for step in range(1, sides)
+    ]
+    for step, (target, count) in enumerate(targets):
+        kept = pl.ds(0, count)
+        copy = pltpu.make_async_remote_copy(
+            src_ref=total,
+            dst_ref=inbox.at[step],
+            send_sem=sends.at[step],
+            recv_sem=receives.at[step],
+            device_id=target,
+            device_id_type=MESH,
+        )
+        copy.start()
+        copy.wait()
+        total[kept] += inbox[step, kept]
+
+
+def greet_sum(size, sides):
+    barrier = pltpu.get_barrier_semaphore()
+    side = lax.axis_index("tensor")
+    targets = [{"dp": p} for p in partners_of(size)]
+    targets += [{"tensor": lax.rem(side + step, sides)} for step in range(1, sides)]
+    for target in targets:
+        pl.semaphore_signal(barrier, inc=1, device_id=target, device_id_type=MESH)
+    pl.semaphore_wait(barrier, len(targets))
+
+
+def merge_kernel(
+    size,
+    sides,
+    query_ref,
+    key_ref,
+    value_ref,
+    gate_ref,
+    widen_ref,
+    mixer_ref,
+    funnel_ref,
+    entry_ref,
+    attend_ref,
+    lift_ref,
+    mixer_down_ref,
+    funnel_down_ref,
+    output_ref,
+    magnitude_ref,
+    attend_out,
+    feed_out,
+    squares_out,
+    total,
+    inbox,
+    direction_cut,
+    direction_wide,
+    direction_mixer,
+    direction_funnel,
+    sends,
+    receives,
+):
+    greet_sum(size, sides)
+    rows = query_ref.shape[0]
+    wide = gate_ref.shape[1]
+    me = lax.axis_index("dp")
+    total[...] = jnp.zeros_like(total)
+
+    def direction(base, down, up):
+        return base.astype(jnp.float32) + ADAPTER_SCALE * jnp.dot(
+            down, up, precision=HIGH_PRECISION, preferred_element_type=jnp.float32
+        )
+
+    group = LANES // rows
+    lane_group = lax.broadcasted_iota(jnp.int32, (1, LANES), 1) // rows
+    for i, (base, down) in enumerate(
+        ((mixer_ref, mixer_down_ref), (funnel_ref, funnel_down_ref))
+    ):
+        held = (direction_mixer, direction_funnel)[i]
+        sums = jnp.zeros((1, rows), jnp.float32)
+        for start in range(0, base.shape[0], CHUNK):
+            piece = pl.ds(start, CHUNK)
+            part = direction(base[piece], down[piece], output_ref[i])
+            held[piece] = part
+            sums += jnp.sum(part * part, axis=0, keepdims=True)
+        spread = jnp.concatenate([sums] * group, axis=1)
+        for r in range(2):
+            here = lane_group == me - r * group
+            total[2 * i + r : 2 * i + r + 1, :] = jnp.where(here, spread, 0.0)
+    for i, base in enumerate((query_ref, key_ref, value_ref)):
+        for start in range(0, LANES, CHUNK):
+            piece = pl.ds(start, CHUNK)
+            part = direction(base[:, piece], entry_ref[i], attend_ref[i, :, piece])
+            direction_cut[i, :, piece] = part
+            total[4 + i : 5 + i, piece] = jnp.sum(part * part, axis=0, keepdims=True)
+    for i, base in enumerate((gate_ref, widen_ref)):
+        for start in range(0, wide, CHUNK):
+            piece = pl.ds(start, CHUNK)
+            part = direction(base[:, piece], entry_ref[3 + i], lift_ref[i, :, piece])
+            direction_wide[i, :, piece] = part
+            row = 7 + 3 * i + start // LANES
+            total[row : row + 1, pl.ds(start % LANES, CHUNK)] = jnp.sum(
+                part * part, axis=0, keepdims=True
+            )
+    double_sum(total, inbox, sends, receives, size, sides, 4)
+    squares_out[...] = total[...]
+    ratio = magnitude_ref[...] / jnp.sqrt(total[...] + COLUMN_EPS)
+    for i in range(3):
+        attend_out[i] = (direction_cut[i] * ratio[4 + i : 5 + i]).astype(jnp.bfloat16)
+    for i in range(2):
+        for start in range(0, wide, CHUNK):
+            row = 7 + 3 * i + start // LANES
+            feed_out[i, :, pl.ds(start, CHUNK)] = (
+                direction_wide[i, :, pl.ds(start, CHUNK)]
+                * ratio[row : row + 1, start % LANES : start % LANES + CHUNK]
+            ).astype(jnp.bfloat16)
+    for i, held in enumerate((direction_mixer, direction_funnel)):
+        own = jnp.zeros((1, rows), jnp.float32)
+        for r in range(2):
+            for g in range(group):
+                own += jnp.where(
+                    me == r * group + g,
+                    ratio[2 * i + r : 2 * i + r + 1, g * rows : (g + 1) * rows],
+                    0.0,
+                )
+        for start in range(0, held.shape[0], CHUNK):
+            part = (held[pl.ds(start, CHUNK)] * own).T.astype(jnp.bfloat16)
+            if i == 0:
+                attend_out[3, :, pl.ds(start, CHUNK)] = part
+            else:
+                feed_out[2, :, pl.ds(start, CHUNK)] = part
+
+
+def merge(bases, entry_rows, attend, widen, mixer_down, funnel_down, output_columns, magnitudes):
+    size = lax.axis_size("dp")
+    sides = lax.axis_size("tensor")
+    rows, cut = bases[0].shape
+    wide = bases[3].shape[1]
+    steps = len(bin(size)) - 3 + sides - 1
+    lines = magnitudes.shape[0]
+    return pl.pallas_call(
+        functools.partial(merge_kernel, size, sides),
+        name="merge",
+        out_shape=(
+            jax.ShapeDtypeStruct((4, rows, cut), jnp.bfloat16),
+            jax.ShapeDtypeStruct((3, rows, wide), jnp.bfloat16),
+            jax.ShapeDtypeStruct((lines, LANES), jnp.float32),
+        ),
+        in_specs=[pl.BlockSpec(memory_space=pltpu.VMEM)] * 14,
+        out_specs=[pl.BlockSpec(memory_space=pltpu.VMEM)] * 3,
+        scratch_shapes=[
+            pltpu.VMEM((lines, LANES), jnp.float32),
+            pltpu.VMEM((steps, lines, LANES), jnp.float32),
+            pltpu.VMEM((3, rows, cut), jnp.float32),
+            pltpu.VMEM((2, rows, wide), jnp.float32),
+            pltpu.VMEM((cut, rows), jnp.float32),
+            pltpu.VMEM((wide, rows), jnp.float32),
+            pltpu.SemaphoreType.DMA((steps,)),
+            pltpu.SemaphoreType.DMA((steps,)),
+        ],
+        compiler_params=pltpu.CompilerParams(
+            collective_id=0, has_side_effects=True, vmem_limit_bytes=48 * 1024 * 1024
+        ),
+    )(*bases, entry_rows, attend, widen, mixer_down, funnel_down, output_columns, magnitudes)
 
 
 def body(
@@ -169,64 +353,51 @@
     rows = base_query.shape[0]
     width = activations.shape[1]
     place = lax.axis_index("dp") * rows
-    side = lax.axis_index("tensor")
-    sides = lax.axis_size("tensor")
     cut = base_query.shape[1]
     wide = base_gate.shape[1]
     entry_rows = lax.dynamic_slice_in_dim(entry_value, place, rows, 1)
     output_columns = lax.dynamic_slice_in_dim(output_value, place, rows, 2)
-    firsts_in = [base_query, base_key, base_value, base_gate, base_widen]
     lifts = [attend_value[0], attend_value[1], attend_value[2], widen_value[0], widen_value[1]]
-    shards = [
-        base.astype(jnp.float32)
-        + ADAPTER_SCALE * jnp.dot(entry_rows[i], lifts[i], precision=HIGH_PRECISION)
-        for i, base in enumerate(firsts_in)
-    ]
-    shards += [
-        base.T.astype(jnp.float32)
-        + ADAPTER_SCALE * jnp.dot(output_columns[i].T, down.T, precision=HIGH_PRECISION)
-        for i, (base, down) in enumerate(((base_mixer, mixer_value), (base_funnel, funnel_value)))
-    ]
-    split_squares = jnp.concatenate([jnp.sum(v * v, axis=0) for v in shards[:5]])
-    split_wide = split_squares.shape[0]
-    shared_squares = jnp.stack([jnp.sum(v * v, axis=1) for v in shards[5:]])
-    split_all = lax.dynamic_update_slice(
-        jnp.zeros((sides, split_wide), jnp.float32), split_squares[None], (side, 0)
-    )
-    shared_all = lax.dynamic_update_slice(
-        jnp.zeros((2, width), jnp.float32), shared_squares, (0, place)
-    )
-    packed = lax.psum(
-        jnp.concatenate([split_all.reshape(-1), shared_all.reshape(-1)]), ("dp", "tensor")
-    )
-    split_squares = lax.dynamic_slice_in_dim(packed, side * split_wide, split_wide)
-    shared_squares = packed[sides * split_wide :].reshape(2, width)
-    split_norms = jnp.sqrt(split_squares + COLUMN_EPS)
-    shared_norms = jnp.sqrt(shared_squares + COLUMN_EPS)
+    pad = -wide % LANES
+    magnitudes = jnp.concatenate(
+        [
+            loudness_value.reshape(-1, LANES),
+            stature_value.reshape(-1, LANES),
+            jnp.pad(amplitude_value, ((0, 0), (0, pad)), constant_values=1.0).reshape(-1, LANES),
+        ]
+    )
+    magnitudes = jnp.pad(magnitudes, ((0, -magnitudes.shape[0] % 8), (0, 0)), constant_values=1.0)
+    attend_shard, feed_shard, squares = merge(
+        (base_query, base_key, base_value, base_gate, base_widen, base_mixer, base_funnel),
+        entry_rows,
+        attend_value,
+        widen_value,
+        mixer_value,
+        funnel_value,
+        output_columns,
+        magnitudes,
+    )
+    lines = (wide + pad) // LANES
+    shared_norms = jnp.sqrt(squares[:4].reshape(2, width) + COLUMN_EPS)
+    split_norms = jnp.sqrt(
+        jnp.concatenate(
+            [squares[4:7].reshape(-1)]
+            + [
+                squares[7 + i * lines : 7 + (i + 1) * lines].reshape(-1)[:wide]
+                for i in range(2)
+            ]
+        )
+        + COLUMN_EPS
+    )
+    split_wide = split_norms.shape[0]
     split_magnitudes = jnp.concatenate([stature_value.reshape(-1), amplitude_value.reshape(-1)])
     split_ratio = split_magnitudes / split_norms
     shared_ratio = loudness_value / shared_norms
-    own_ratio = lax.dynamic_slice_in_dim(shared_ratio, place, rows, 1)
-    attend_shard = jnp.concatenate(
-        [low(shards[i] * split_ratio[None, i * cut : (i + 1) * cut]) for i in range(3)]
-        + [low(shards[5] * own_ratio[0][:, None])],
-        axis=1,
-    )
-    feed_shard = jnp.concatenate(
-        [
-            low(shards[3 + i] * split_ratio[None, 3 * cut + i * wide : 3 * cut + (i + 1) * wide])
-            for i in range(2)
-        ]
-        + [low(shards[6] * own_ratio[1][:, None])],
-        axis=1,
-    )
-    attend_all = lax.all_gather(attend_shard, "dp", axis=0, tiled=True)
-    feed_all = lax.all_gather(feed_shard, "dp", axis=0, tiled=True)
-    merged_attend = attend_all[:, : 3 * cut]
-    merged_mixer = attend_all[:, 3 * cut :]
-    merged_gate = feed_all[:, :wide]
-    merged_widen = feed_all[:, wide : 2 * wide]
-    merged_funnel = feed_all[:, 2 * wide :]
+    attend_all = lax.all_gather(attend_shard, "dp", axis=1, tiled=True)
+    feed_all = lax.all_gather(feed_shard, "dp", axis=1, tiled=True)
+    merged_attend = jnp.concatenate([attend_all[0], attend_all[1], attend_all[2]], axis=1)
+    merged_mixer = attend_all[3]
+    merged_gate, merged_widen, merged_funnel = feed_all
 
     count = activations.shape[0] // SEQ
     heads = cut // HEAD_DIM
@@ -322,9 +493,9 @@
     up_gradients = []
     inputs = (normed_one, normed_one, normed_one, normed_two, normed_two)
     weights = (
-        merged_attend[:, :cut],
-        merged_attend[:, cut : 2 * cut],
-        merged_attend[:, 2 * cut :],
+        attend_all[0],
+        attend_all[1],
+        attend_all[2],
         merged_gate,
         merged_widen,
     )

time: 1030 us -> 935 us (0.908)
  waiting for transfers between devices: 568 us -> 427 us
  local copies, waits for them, and re-layouts: 42 us -> 71.2 us
  Pallas kernels: 0 us -> 28.4 us
    psum x1 -> x0, waiting for transfers between devices: 122 us -> none  [body(): lax.psum(jnp.concatenate([split_all.reshape(-1), shared_all.reshape(-1)])...]
    pallas_call x0 -> x1, Pallas kernels: none -> 28.4 us  [merge(): pl.pallas_call(functools.partial(merge_kernel, size, sides), name='merge'...]
    dot_general x7 -> x0, matrix products: 18.4 us -> none  [the longest x5 12.2 us: body(): jnp.dot(entry_rows[i], lifts[i], precision=HIGH_PRECISION)]
    unnamed x271 -> x235, local copies, waits for them, and re-layouts: 19.9 us -> 36.3 us
    all_gather x2, waiting for transfers between devices: 212 us -> 196 us  [the longest x1 119 us: body(): attend_all = lax.all_gather(attend_shard, 'dp', axis=1, tiled=True)]
  transfers between devices with their start and end apart: 9 -> 8, of which waited for: 8 -> 7; matrix products, arithmetic and copies ran while one was open for 9% -> 12% of each run, Pallas kernels for 0% -> 0%
where the time goes in v2:
time: 935 us; the launch traced here: 927 us
  waiting for transfers between devices  427 us (46%)
  matrix products  244 us (26%)
  local copies, waits for them, and re-layouts  71.2 us (8%)
  other arithmetic  66.1 us (7%)
  blocking collectives  65.6 us (7%)
  Pallas kernels  28.4 us (3%)
  between operations  20.3 us (2%)
    ppermute x4, waiting for transfers between devices, swap(): lax.ppermute(low, 'tensor', [(i, (i + step) % size) for i in range(size)])  122 us
    all_gather x1, waiting for transfers between devices, body(): attend_all = lax.all_gather(attend_shard, 'dp', axis=1, tiled=True)  119 us
    dot_general x14, matrix products, matmul(): return jnp.dot(left, right, preferred_element_type=jnp.float32)  93.5 us
    psum x1, waiting for transfers between devices, body(): lax.psum((shared_terms, split_terms, split_dots, shared_dots), 'dp')  80.4 us
    all_gather x1, waiting for transfers between devices, body(): feed_all = lax.all_gather(feed_shard, 'dp', axis=1, tiled=True)  77.1 us
    dot_general x10, matrix products, matmul_nt(): jnp.einsum('ik,jk->ij', left, right, preferred_element_type=jnp.float32)  70.7 us
    psum x1, blocking collectives, body(): lax.psum((shared_terms, split_terms, split_dots, shared_dots), 'dp')  60.1 us
    dot_general x12, matrix products, matmul_tn(): jnp.einsum('ki,kj->ij', left, right, preferred_element_type=jnp.float32)  52.4 us
  transfers between devices with their start and end apart: 8, of which 7 were waited for; matrix products, arithmetic and copies ran while one was open for 12% of the time, Pallas kernels for 0%

profile of v2, /device:TPU:0, one launch (start us, length us, event | category | flops | bytes accessed | tf_op | source)
XLA Modules:
  0.0 927.0 jit_solution(3217046780901349309)
XLA Ops:
  23.8 28.4 %merge.1 = (bf16[4,128,1024]{2,1,0:T(8,128)(2,1)}, bf16[3,128,2816]{2,1,0:T(8,128)(2,1)}, f32[16,1024]{1,0:T(8,128)S(1)}) custom-call(bf16[128,1024]{1,0:T(8,128)(2,1)S(1)} %copy-done.7, bf16[128,1024]{1,0:T(8,128)(2,1)S(1)} %copy-done.8, bf16[128,1024]{1,0:T(8,128)(2,1)S(1)} %copy-done.9, bf16[128,2816]{1,0:T(8,128)(2,1)S(1)} %copy-done.4, ...), custom_call_target="tpu_custom_call" | custom-call | tf_op jit(solution)/shard_map/merge/pallas_call | solution.py:253
  58.5 118.9 %all-gather.3.cloned.1.call-done = bf16[4,2048,1024]{2,1,0:T(8,128)(2,1)} async-done(((bf16[4,128,1024]{2,1,0:T(8,128)(2,1)}), bf16[4,2048,1024]{2,1,0:T(8,128)(2,1)}) %all-gather.3.cloned.1.call-update) | async-done | bytes 16777232 | tf_op jit(solution)/shard_map/all_gather | solution.py:396
  177.4 8.4 slice_bitcast_fusion.18
  185.8 12.5 %fusion.18 = f32[512,3072]{1,0:T(8,128)} fusion(bf16[512,2048]{1,0:T(8,128)(2,1)S(1)} %copy-done.15, bf16[2048,1024]{1,0:T(8,128)(2,1)} %get-tuple-element.84, bf16[2048,1024]{1,0:T(8,128)(2,1)} %get-tuple-element.85, bf16[2048,1024]{1,0:T(8,128)(2,1)S(1)} %get-tuple-element.83), kind=kOutput, calls=%fused_computation.38 | convolution fusion | flops 6480199680 | bytes 20971520 | tf_op jit(solution)/shard_map/dot_general | solution.py:84
  216.2 5.0 convolution_convert_fusion
  222.7 46.2 %collective-permute-done = bf16[512,2048]{1,0:T(8,128)(2,1)S(1)} collective-permute-done((bf16[512,2048]{1,0:T(8,128)(2,1)S(1)}, bf16[512,2048]{1,0:T(8,128)(2,1)S(1)}, u32[]{:S(2)}, u32[]{:S(2)}) %collective-permute-start) | collective-permute-done | bytes 2097184 | tf_op jit(solution)/shard_map/ppermute | solution.py:78
  273.1 77.1 %all-gather.5.cloned.1.call-done = bf16[3,2048,2816]{2,1,0:T(8,128)(2,1)} async-done(((bf16[3,128,2816]{2,1,0:T(8,128)(2,1)}), bf16[3,2048,2816]{2,1,0:T(8,128)(2,1)}) %all-gather.5.cloned.1.call-update) | async-done | bytes 34603024 | tf_op jit(solution)/shard_map/all_gather | solution.py:397
  350.2 12.6 %fusion.3 = f32[512,2816]{1,0:T(8,128)} fusion(bf16[512,2048]{1,0:T(8,128)(2,1)} %multiply_convert_fusion.2, bf16[3,2048,2816]{2,1,0:T(8,128)(2,1)} %all-gather.5.cloned.1.call-done), kind=kOutput, calls=%fused_computation.13 | convolution fusion | flops 5905580032 | bytes 19398656 | tf_op jit(solution)/shard_map/dot_general | solution.py:84
  362.8 11.3 %fusion.10 = f32[2816,512]{0,1:T(8,128)} fusion(bf16[512,2048]{1,0:T(8,128)(2,1)S(1)} %copy-done.20, bf16[3,2048,2816]{2,1,0:T(8,128)(2,1)} %all-gather.5.cloned.1.call-done), kind=kOutput, calls=%fused_computation.20 | convolution fusion | flops 5905580032 | bytes 19398656 | tf_op jit(solution)/shard_map/dot_general | solution.py:84
  374.1 15.1 %multiply_reduce_fusion = (f32[2816]{0:T(1024)S(1)}, bf16[512,2816]{1,0:T(8,128)(2,1)S(1)}, f32[2816]{0:T(1024)S(1)}, bf16[512,2816]{1,0:T(8,128)(2,1)S(1)}, bf16[512,2816]{1,0:T(8,128)(2,1)}) fusion(f32[2816,512]{0,1:T(8,128)} %fusion.10, f32[512,2816]{1,0:T(8,128)} %fusion.3, bf16[512,2048]{1,0:T(8,128)(2,1)S(1)} %copy-done.14, ...), kind=kOutput, calls=%fused_computation.30 | convolution fusion | flops 5937293312 | bytes 33839104 | tf_op jit(solution)/shard_map/dot_general | solution.py:84
  389.2 11.1 %fusion.2 = f32[512,2048]{1,0:T(8,128)S(1)} fusion(bf16[512,2816]{1,0:T(8,128)(2,1)S(1)} %get-tuple-element.82, bf16[3,2048,2816]{2,1,0:T(8,128)(2,1)} %all-gather.5.cloned.1.call-done), kind=kOutput, calls=%fused_computation.12 | convolution fusion | flops 5905580032 | bytes 18612224 | tf_op jit(solution)/shard_map/ik,jk->ij/dot_general | solution.py:88
  400.3 10.2 %add_convert_fusion = bf16[512,2048]{1,0:T(8,128)(2,1)} fusion(f32[512,2048]{1,0:T(8,128)S(1)} %fusion.2, bf16[512,2816]{1,0:T(8,128)(2,1)S(1)} %get-tuple-element.78, bf16[3,2048,2816]{2,1,0:T(8,128)(2,1)} %all-gather.5.cloned.1.call-done), kind=kOutput, calls=%fused_computation.55 | convolution fusion | flops 5907677184 | bytes 20709376 | tf_op jit(solution)/shard_map/ik,jk->ij/dot_general | solution.py:88
  412.0 10.1 %fusion.46 = bf16[512,2048]{1,0:T(8,128)(2,1)} fusion(bf16[512,2816]{1,0:T(8,128)(2,1)S(1)} %copy-done.29, bf16[3,2048,2816]{2,1,0:T(8,128)(2,1)} %all-gather.5.cloned.1.call-done), kind=kOutput, calls=%fused_computation.87 | convolution fusion | flops 5906628608 | bytes 16515072 | tf_op jit(solution)/shard_map/ik,jk->ij/dot_general | solution.py:88
  422.9 36.4 %collective-permute-done.2 = bf16[512,2048]{1,0:T(8,128)(2,1)} collective-permute-done((bf16[512,2048]{1,0:T(8,128)(2,1)}, bf16[512,2048]{1,0:T(8,128)(2,1)}, u32[]{:S(2)}, u32[]{:S(2)}) %collective-permute-start.2) | collective-permute-done | bytes 2097184 | tf_op jit(solution)/shard_map/ppermute | solution.py:78
  459.3 5.1 multiply_reduce_fusion.4
  464.4 39.2 %collective-permute-done.1 = bf16[512,2048]{1,0:T(8,128)(2,1)} collective-permute-done((bf16[512,2048]{1,0:T(8,128)(2,1)}, bf16[512,2048]{1,0:T(8,128)(2,1)}, u32[]{:S(2)}, u32[]{:S(2)}) %collective-permute-start.1) | collective-permute-done | bytes 2097184 | tf_op jit(solution)/shard_map/ppermute | solution.py:78
  503.6 8.9 multiply_reduce_fusion.2
  512.5 5.3 fusion.72
  521.6 4.4 multiply_reduce_fusion.3
  543.1 5.1 multiply_subtract_fusion.1
  551.2 60.1 %all-reduce.2 = (f32[8704]{0:T(1024)S(1)}, f32[2,2048]{1,0:T(2,128)S(1)}) all-reduce(f32[8704]{0:T(1024)S(1)} %constant_dynamic-update-slice_fusion.5, f32[2,2048]{1,0:T(2,128)S(1)} %pad_maximum_fusion.12), channel_id=1, replica_groups=mesh['dp'=16,'tensor'=2] {'dp'}, use_global_device_ids=true, to_apply=%region_16.17 | all-reduce | flops 12800 | bytes 102400 | tf_op jit(solution)/shard_map/psum | solution.py:543
  620.3 3.6 fusion.95
  636.5 3.6 fusion.93
  640.1 3.6 fusion.94
  650.5 3.4 fusion.180
  657.2 5.9 fusion
  663.2 4.3 fusion.57
  667.5 6.3 fusion.4
  673.9 4.3 fusion.59
  681.6 3.9 fusion.67
  685.5 5.9 fusion.36
  691.4 3.5 fusion.84
  695.0 3.5 fusion.87
  698.5 3.5 fusion.90
  701.9 5.0 fusion.27
  706.9 6.6 fusion.34
  713.5 5.0 fusion.30
  718.4 8.0 fusion.69
  726.5 4.8 fusion.64
  731.3 6.9 fusion.9
  738.2 3.5 fusion.92
  741.6 4.3 fusion.32
  746.0 11.9 %fusion.43 = bf16[512,2048]{1,0:T(8,128)(2,1)} fusion(bf16[2048,1024]{1,0:T(8,128)(2,1)} %get-tuple-element.84, bf16[2048,1024]{1,0:T(8,128)(2,1)} %get-tuple-element.85, bf16[2048,1024]{1,0:T(8,128)(2,1)} %copy-done.38, bf16[512,1024]{1,0:T(8,128)(2,1)} %bitcast.389, bf16[512,1024]{1,0:T(8,128)(2,1)} %bitcast.388, bf16[512,1024]{1,0:T(8,128)(2,1)} %bitcast.387), kind=kOutput, calls=%fused_computation.85 | convolution fusion | flops 6490685440 | bytes 17825792 | tf_op jit(solution)/shard_map/ik,jk->ij/dot_general | solution.py:88
  759.4 80.4 %all-reduce.9.cloned.1.call-done = (f32[16,12544]{1,0:T(8,128)}, f32[16,14336]{1,0:T(8,128)}) async-done(((f32[16,12544]{1,0:T(8,128)}, f32[16,14336]{1,0:T(8,128)}), (f32[16,12544]{1,0:T(8,128)}, f32[16,14336]{1,0:T(8,128)})) %all-reduce.9.cloned.1.call-update) | async-done | bytes 1720336 | tf_op jit(solution)/shard_map/psum | solution.py:543
  843.0 5.4 psum.44
  851.8 27.9 %all-reduce.7.cloned.1.call-done = f32[16,14336]{1,0:T(8,128)} async-done(((f32[16,14336]{1,0:T(8,128)}), f32[16,14336]{1,0:T(8,128)}) %all-reduce.7.cloned.1.call-update) | async-done | bytes 917520 | tf_op jit(solution)/shard_map/psum | solution.py:549
  909.7 3.7 fusion.24
  913.5 5.7 fusion.20
  (338 shorter events, 141.0 us)
Async XLA Ops:
  7.2 170.2 %all-gather.3.cloned.1.call-start = ((), (), s32[]{:S(2)}) async-start(), calls=%async_computation | async-start | bytes 17825792 | tf_op jit(solution)/shard_map/all_gather | solution.py:396
  23.8 29.2 %copy-start.104 = (s32[512]{0:T(512)S(1)}, s32[512]{0:T(512)}, u32[]{:S(2)}) copy-start(s32[512]{0:T(512)} %param.42) | copy-start | bytes 6148
  23.8 29.3 %copy-start.103 = (s32[512]{0:T(512)S(1)}, s32[512]{0:T(512)}, u32[]{:S(2)}) copy-start(s32[512]{0:T(512)} %param.41) | copy-start | bytes 6148
  23.8 29.4 %copy-start.11 = (bf16[512,2048]{1,0:T(8,128)(2,1)S(1)}, bf16[512,2048]{1,0:T(8,128)(2,1)}, u32[]{:S(2)}) copy-start(bf16[512,2048]{1,0:T(8,128)(2,1)} %param.39) | copy-start | bytes 6291460
  52.2 298.0 %all-gather.5.cloned.1.call-start = ((), (), s32[]{:S(2)}) async-start(), calls=%async_computation.1 | async-start | bytes 36765696 | tf_op jit(solution)/shard_map/all_gather | solution.py:397
  52.9 786.8 %all-reduce.9.cloned.1.call-start = ((), (), s32[]{:S(2)}) async-start(), calls=%async_computation.3 | async-start | bytes 3440640 | tf_op jit(solution)/shard_map/psum | solution.py:543
  53.6 132.2 %copy-start.96 = (f32[512]{0:T(512)}, f32[512]{0:T(512)S(1)}, u32[]{:S(2)}) copy-start(f32[512]{0:T(512)S(1)} %fusion.213) | copy-start | bytes 6148
  56.6 145.3 %copy-start.45 = (f32[512,64]{1,0:T(8,128)}, f32[512,64]{1,0:T(8,128)S(1)}, u32[]{:S(2)}) copy-start(f32[512,64]{1,0:T(8,128)S(1)} %get-tuple-element.139) | copy-start | bytes 393220
  56.6 129.2 %copy-start.70 = (f32[1,2048]{1,0:T(1,128)}, f32[1,2048]{1,0:T(1,128)S(1)}, u32[]{:S(2)}) copy-start(f32[1,2048]{1,0:T(1,128)S(1)} %get-tuple-element.135) | copy-start | bytes 24580
  185.8 12.5 %copy-start.38 = (bf16[2048,1024]{1,0:T(8,128)(2,1)}, bf16[2048,1024]{1,0:T(8,128)(2,1)S(1)}, u32[]{:S(2)}) copy-start(bf16[2048,1024]{1,0:T(8,128)(2,1)S(1)} %get-tuple-element.83) | copy-start | bytes 12582916
  221.2 48.7 %copy-start.16 = (bf16[512,2048]{1,0:T(8,128)(2,1)}, bf16[512,2048]{1,0:T(8,128)(2,1)S(1)}, u32[]{:S(2)}) copy-start(bf16[512,2048]{1,0:T(8,128)(2,1)S(1)} %convolution_convert_fusion) | copy-start | bytes 6291460
  221.2 47.7 %collective-permute-start = (bf16[512,2048]{1,0:T(8,128)(2,1)S(1)}, bf16[512,2048]{1,0:T(8,128)(2,1)S(1)}, u32[]{:S(2)}, u32[]{:S(2)}) collective-permute-start(bf16[512,2048]{1,0:T(8,128)(2,1)S(1)} %convolution_convert_fusion), channel_id=1, source_target_pairs={{0,1},{1,0},{2,3},{3,2},{4,5},{5,4},{6,7},{7,6},{8,9},{9,8},{10,11... | collective-permute-start | bytes 6291464 | tf_op jit(solution)/shard_map/ppermute | solution.py:78
  350.2 12.6 %copy-start.20 = (bf16[512,2048]{1,0:T(8,128)(2,1)S(1)}, bf16[512,2048]{1,0:T(8,128)(2,1)}, u32[]{:S(2)}) copy-start(bf16[512,2048]{1,0:T(8,128)(2,1)} %param.40) | copy-start | bytes 6291460
  362.8 11.3 %copy-start.14 = (bf16[512,2048]{1,0:T(8,128)(2,1)S(1)}, bf16[512,2048]{1,0:T(8,128)(2,1)}, u32[]{:S(2)}) copy-start(bf16[512,2048]{1,0:T(8,128)(2,1)} %multiply_convert_fusion.2) | copy-start | bytes 6291460
  389.2 11.1 %copy-start.28 = (bf16[512,2816]{1,0:T(8,128)(2,1)}, bf16[512,2816]{1,0:T(8,128)(2,1)S(1)}, u32[]{:S(2)}) copy-start(bf16[512,2816]{1,0:T(8,128)(2,1)S(1)} %get-tuple-element.82) | copy-start | bytes 8650756
  389.2 11.1 %copy-start.27 = (bf16[512,2816]{1,0:T(8,128)(2,1)}, bf16[512,2816]{1,0:T(8,128)(2,1)S(1)}, u32[]{:S(2)}) copy-start(bf16[512,2816]{1,0:T(8,128)(2,1)S(1)} %get-tuple-element.78) | copy-start | bytes 8650756
  400.3 11.7 %copy-start.29 = (bf16[512,2816]{1,0:T(8,128)(2,1)S(1)}, bf16[512,2816]{1,0:T(8,128)(2,1)}, u32[]{:S(2)}) copy-start(bf16[512,2816]{1,0:T(8,128)(2,1)} %get-tuple-element.86) | copy-start | bytes 8650756
  410.5 48.8 %collective-permute-start.2 = (bf16[512,2048]{1,0:T(8,128)(2,1)}, bf16[512,2048]{1,0:T(8,128)(2,1)}, u32[]{:S(2)}, u32[]{:S(2)}) collective-permute-start(bf16[512,2048]{1,0:T(8,128)(2,1)} %add_convert_fusion), channel_id=1, source_target_pairs={{0,1},{1,0},{2,3},{3,2},{4,5},{5,4},{6,7},{7,6},{8,9},{9,8},{10,11... | collective-permute-start | bytes 6291464 | tf_op jit(solution)/shard_map/ppermute | solution.py:78
  412.0 10.6 %copy-start.68 = (f32[3,1024]{1,0:T(4,128)S(1)}, f32[3,1024]{1,0:T(4,128)}, u32[]{:S(2)}) copy-start(f32[3,1024]{1,0:T(4,128)} %param.57) | copy-start | bytes 36868
  412.0 10.7 %copy-start.60 = (f32[2,2816]{1,0:T(2,128)S(1)}, f32[2,2816]{1,0:T(2,128)}, u32[]{:S(2)}) copy-start(f32[2,2816]{1,0:T(2,128)} %param.58) | copy-start | bytes 67588
  422.1 81.5 %collective-permute-start.1 = (bf16[512,2048]{1,0:T(8,128)(2,1)}, bf16[512,2048]{1,0:T(8,128)(2,1)}, u32[]{:S(2)}, u32[]{:S(2)}) collective-permute-start(bf16[512,2048]{1,0:T(8,128)(2,1)} %fusion.46), channel_id=1, source_target_pairs={{0,1},{1,0},{2,3},{3,2},{4,5},{5,4},{6,7},{7,6},{8,9},{9,8},{10,11... | collective-permute-start | bytes 6291464 | tf_op jit(solution)/shard_map/ppermute | solution.py:78
  422.9 80.7 %copy-start.17 = (bf16[512,2048]{1,0:T(8,128)(2,1)S(1)}, bf16[512,2048]{1,0:T(8,128)(2,1)}, u32[]{:S(2)}) copy-start(bf16[512,2048]{1,0:T(8,128)(2,1)} %copy-done.16) | copy-start | bytes 6291460
  422.9 80.7 %copy-start.19 = (bf16[512,2048]{1,0:T(8,128)(2,1)S(1)}, bf16[512,2048]{1,0:T(8,128)(2,1)}, u32[]{:S(2)}) copy-start(bf16[512,2048]{1,0:T(8,128)(2,1)} %copy-done.18) | copy-start | bytes 6291460
  422.9 80.7 %copy-start.21 = (bf16[512,2048]{1,0:T(8,128)(2,1)S(1)}, bf16[512,2048]{1,0:T(8,128)(2,1)}, u32[]{:S(2)}) copy-start(bf16[512,2048]{1,0:T(8,128)(2,1)} %param.40) | copy-start | bytes 6291460
  551.1 69.2 %copy-start.41 = (f32[5,2048,16]{1,2,0:T(8,128)S(1)}, f32[5,2048,16]{1,2,0:T(8,128)}, u32[]{:S(2)}) copy-start(f32[5,2048,16]{1,2,0:T(8,128)} %param.51) | copy-start | bytes 1966084
  612.6 11.3 %copy-start.88 = (f32[1024]{0:T(1024)}, f32[1024]{0:T(1024)S(1)}, u32[]{:S(2)}) copy-start(f32[1024]{0:T(1024)S(1)} %get-tuple-element.123) | copy-start | bytes 12292
  612.6 31.2 %copy-start.86 = (f32[1024]{0:T(1024)}, f32[1024]{0:T(1024)S(1)}, u32[]{:S(2)}) copy-start(f32[1024]{0:T(1024)S(1)} %get-tuple-element.122) | copy-start | bytes 12292
  612.6 37.9 %copy-start.84 = (f32[1024]{0:T(1024)}, f32[1024]{0:T(1024)S(1)}, u32[]{:S(2)}) copy-start(f32[1024]{0:T(1024)S(1)} %get-tuple-element.121) | copy-start | bytes 12292
  612.6 44.6 %copy-start.75 = (f32[2816]{0:T(1024)}, f32[2816]{0:T(1024)S(1)}, u32[]{:S(2)}) copy-start(f32[2816]{0:T(1024)S(1)} %get-tuple-element.120) | copy-start | bytes 33796
  612.6 54.9 %copy-start.72 = (f32[2816]{0:T(1024)}, f32[2816]{0:T(1024)S(1)}, u32[]{:S(2)}) copy-start(f32[2816]{0:T(1024)S(1)} %get-tuple-element.119) | copy-start | bytes 33796
  612.6 50.5 %copy-start.74 = (f32[2816]{0:T(1024)}, f32[2816]{0:T(1024)S(1)}, u32[]{:S(2)}) copy-start(f32[2816]{0:T(1024)S(1)} %get-tuple-element.118) | copy-start | bytes 33796
  612.7 61.2 %copy-start.73 = (f32[2816]{0:T(1024)}, f32[2816]{0:T(1024)S(1)}, u32[]{:S(2)}) copy-start(f32[2816]{0:T(1024)S(1)} %get-tuple-element.117) | copy-start | bytes 33796
  623.9 9.2 copy-start.43
  633.1 10.6 %copy-start.77 = (f32[1,2048]{1,0:T(1,128)}, f32[1,2048]{1,0:T(1,128)S(1)}, u32[]{:S(2)}) copy-start(f32[1,2048]{1,0:T(1,128)S(1)} %get-tuple-element.132) | copy-start | bytes 24580
  746.0 133.7 %all-reduce.7.cloned.1.call-start = ((), (), s32[]{:S(2)}) async-start(), calls=%async_computation.2 | async-start | bytes 1835008 | tf_op jit(solution)/shard_map/psum | solution.py:549
  757.9 151.8 %collective-permute-start.3 = (bf16[512,2048]{1,0:T(8,128)(2,1)}, bf16[512,2048]{1,0:T(8,128)(2,1)}, u32[]{:S(2)}, u32[]{:S(2)}) collective-permute-start(bf16[512,2048]{1,0:T(8,128)(2,1)} %fusion.43), channel_id=1, source_target_pairs={{0,1},{1,0},{2,3},{3,2},{4,5},{5,4},{6,7},{7,6},{8,9},{9,8},{10,11... | collective-permute-start | bytes 6291464 | tf_op jit(solution)/shard_map/ppermute | solution.py:78
  896.3 8.8 copy-start.57
  896.4 9.6 %copy-start.61 = (f32[2,2816]{1,0:T(2,128)S(1)}, f32[2,2816]{1,0:T(2,128)}, u32[]{:S(2)}) copy-start(f32[2,2816]{1,0:T(2,128)} %param.58) | copy-start | bytes 67588
  896.4 9.6 %copy-start.76 = (f32[2,2816]{1,0:T(2,128)S(1)}, f32[2,2816]{1,0:T(2,128)}, u32[]{:S(2)}) copy-start(f32[2,2816]{1,0:T(2,128)} %mul.1347) | copy-start | bytes 67588
  896.4 9.6 %copy-start.92 = (f32[2,2816]{1,0:T(2,128)S(1)}, f32[2,2816]{1,0:T(2,128)}, u32[]{:S(2)}) copy-start(f32[2,2816]{1,0:T(2,128)} %param.67) | copy-start | bytes 67588
  896.4 9.6 %copy-start.93 = (f32[2,2816]{1,0:T(2,128)S(1)}, f32[2,2816]{1,0:T(2,128)}, u32[]{:S(2)}) copy-start(f32[2,2816]{1,0:T(2,128)} %param.76) | copy-start | bytes 67588
  896.4 10.3 %copy-start.64 = (f32[2816,16]{0,1:T(8,128)S(1)}, f32[2816,16]{0,1:T(8,128)}, u32[]{:S(2)}) copy-start(f32[2816,16]{0,1:T(8,128)} %param.64) | copy-start | bytes 540676
  896.4 10.3 %copy-start.65 = (f32[2816,16]{0,1:T(8,128)S(1)}, f32[2816,16]{0,1:T(8,128)}, u32[]{:S(2)}) copy-start(f32[2816,16]{0,1:T(8,128)} %param.73) | copy-start | bytes 540676
  898.9 9.7 %copy-start.51 = (f32[1,16,2816]{2,1,0:T(8,128)S(1)}, f32[1,16,2816]{2,1,0:T(8,128)}, u32[]{:S(2)}) copy-start(f32[1,16,2816]{2,1,0:T(8,128)} %get-tuple-element.101) | copy-start | bytes 540676
  898.9 9.7 %copy-start.52 = (f32[1,16,2816]{2,1,0:T(8,128)S(1)}, f32[1,16,2816]{2,1,0:T(8,128)}, u32[]{:S(2)}) copy-start(f32[1,16,2816]{2,1,0:T(8,128)} %get-tuple-element.102) | copy-start | bytes 540676
  898.9 9.7 %copy-start.54 = (f32[2,16,2816]{2,1,0:T(8,128)S(1)}, f32[2,16,2816]{2,1,0:T(8,128)}, u32[]{:S(2)}) copy-start(f32[2,16,2816]{2,1,0:T(8,128)} %param.62) | copy-start | bytes 1081348
  898.9 9.7 %copy-start.55 = (f32[2,16,2816]{2,1,0:T(8,128)S(1)}, f32[2,16,2816]{2,1,0:T(8,128)}, u32[]{:S(2)}) copy-start(f32[2,16,2816]{2,1,0:T(8,128)} %param.71) | copy-start | bytes 1081348
  900.6 9.1 copy-start.71
  (67 other events, 302.8 us)
Sparse Core Ops, SparseCore 0:
  52.3 125.0 all-gather.2
  179.0 171.1 all-gather.4
  746.1 93.6 all-reduce.8
  843.2 36.4 all-reduce.6

commit v3 on v2

--- a/solution.py
+++ b/solution.py
@@ -8,6 +8,7 @@
 from jax.sharding import PartitionSpec as P
 
 HEAD_DIM = 128
+RANK = 16
 SEQ = 256
 STEP = 5
 
@@ -160,8 +161,7 @@
     funnel_down_ref,
     output_ref,
     magnitude_ref,
-    attend_out,
-    feed_out,
+    shard_out,
     squares_out,
     total,
     inbox,
@@ -217,12 +217,17 @@
     double_sum(total, inbox, sends, receives, size, sides, 4)
     squares_out[...] = total[...]
     ratio = magnitude_ref[...] / jnp.sqrt(total[...] + COLUMN_EPS)
+    near = LANES // CHUNK
     for i in range(3):
-        attend_out[i] = (direction_cut[i] * ratio[4 + i : 5 + i]).astype(jnp.bfloat16)
+        for b in range(near):
+            lanes = slice(b * CHUNK, (b + 1) * CHUNK)
+            shard_out[near * i + b] = (
+                direction_cut[i, :, lanes] * ratio[4 + i : 5 + i, lanes]
+            ).astype(jnp.bfloat16)
     for i in range(2):
         for start in range(0, wide, CHUNK):
             row = 7 + 3 * i + start // LANES
-            feed_out[i, :, pl.ds(start, CHUNK)] = (
+            shard_out[4 * near + 3 * (start // CHUNK) + i] = (
                 direction_wide[i, :, pl.ds(start, CHUNK)]
                 * ratio[row : row + 1, start % LANES : start % LANES + CHUNK]
             ).astype(jnp.bfloat16)
@@ -238,9 +243,9 @@
         for start in range(0, held.shape[0], CHUNK):
             part = (held[pl.ds(start, CHUNK)] * own).T.astype(jnp.bfloat16)
             if i == 0:
-                attend_out[3, :, pl.ds(start, CHUNK)] = part
+                shard_out[3 * near + start // CHUNK] = part
             else:
-                feed_out[2, :, pl.ds(start, CHUNK)] = part
+                shard_out[4 * near + 3 * (start // CHUNK) + 2] = part
 
 
 def merge(bases, entry_rows, attend, widen, mixer_down, funnel_down, output_columns, magnitudes):
@@ -254,12 +259,11 @@
         functools.partial(merge_kernel, size, sides),
         name="merge",
         out_shape=(
-            jax.ShapeDtypeStruct((4, rows, cut), jnp.bfloat16),
-            jax.ShapeDtypeStruct((3, rows, wide), jnp.bfloat16),
+            jax.ShapeDtypeStruct(((4 * cut + 3 * wide) // CHUNK, rows, CHUNK), jnp.bfloat16),
             jax.ShapeDtypeStruct((lines, LANES), jnp.float32),
         ),
         in_specs=[pl.BlockSpec(memory_space=pltpu.VMEM)] * 14,
-        out_specs=[pl.BlockSpec(memory_space=pltpu.VMEM)] * 3,
+        out_specs=[pl.BlockSpec(memory_space=pltpu.VMEM)] * 2,
         scratch_shapes=[
             pltpu.VMEM((lines, LANES), jnp.float32),
             pltpu.VMEM((steps, lines, LANES), jnp.float32),
@@ -274,6 +278,588 @@
             collective_id=0, has_side_effects=True, vmem_limit_bytes=48 * 1024 * 1024
         ),
     )(*bases, entry_rows, attend, widen, mixer_down, funnel_down, output_columns, magnitudes)
+
+
+def dot_nn(left, right):
+    return jnp.dot(left, right, preferred_element_type=jnp.float32)
+
+
+def dot_nt(left, right):
+    return lax.dot_general(
+        left, right, (((1,), (1,)), ((), ())), preferred_element_type=jnp.float32
+    )
+
+
+BLOCKS = 3
+HEAD_CHUNKS = 5
+EXTRA_TICKS = 3
+
+
+def gather_parts(size, shard, full, sems):
+    line = size // 4
+    early = 16
+    late = shard.shape[1] - early
+    me = lax.axis_index("dp")
+    core, column, spot = lax.rem(me, 2), lax.rem(lax.div(me, 2), 2), lax.div(me, 4)
+    right_sends, left_sends, right_gets, left_gets, pair_sems, core_sems, early_sems = sems
+
+    def device(other_spot, other_column, other_core):
+        return {"dp": (other_spot * 2 + other_column) * 2 + other_core}
+
+    right = device(lax.rem(spot + 1, line), column, core)
+    left = device(lax.rem(spot + line - 1, line), column, core)
+    across = device(spot, 1 - column, core)
+    twin = device(spot, column, 1 - core)
+
+    def greet():
+        barrier = pltpu.get_barrier_semaphore()
+        ahead, behind = spot < line - 1, spot > 0
+
+        @pl.when(ahead)
+        def _():
+            pl.semaphore_signal(barrier, inc=1, device_id=right, device_id_type=MESH)
+
+        @pl.when(behind)
+        def _():
+            pl.semaphore_signal(barrier, inc=1, device_id=left, device_id_type=MESH)
+
+        for target in (across, twin, {"tensor": 1 - lax.axis_index("tensor")}):
+            pl.semaphore_signal(barrier, inc=1, device_id=target, device_id_type=MESH)
+        peers = 3 + ahead.astype(jnp.int32) + behind.astype(jnp.int32)
+        pl.semaphore_wait(barrier, peers)
+
+    def remote(source, target, send, get, where):
+        return pltpu.make_async_remote_copy(
+            src_ref=source,
+            dst_ref=target,
+            send_sem=send,
+            recv_sem=get,
+            device_id=where,
+            device_id_type=MESH,
+        )
+
+    def early_copy(part, owner):
+        first = 1 + BLOCKS
+        blocks = pl.ds(0, first) if part == 0 else pl.ds(first, shard.shape[0] - first)
+        return remote(
+            shard.at[blocks, pl.ds(0, early)],
+            full.at[blocks, spot, owner, core, pl.ds(0, early)],
+            early_sems.at[part, 0],
+            early_sems.at[part, 1],
+            across,
+        )
+
+    def early_start():
+        for part in range(2):
+            early_copy(part, column).start()
+
+    def early_wait(part):
+        early_copy(part, 1 - column).wait_recv()
+        early_copy(part, column).wait_send()
+
+    def place_of(part, origin, blocks):
+        if part == 0:
+            return full.at[blocks, origin, column, core, pl.ds(early, late)]
+        return full.at[blocks, origin, :, core, pl.ds(0, early)]
+
+    def moves(to_right, hop, chunk, start, count):
+        sends, gets = (right_sends, right_gets) if to_right else (left_sends, left_gets)
+        blocks = pl.ds(start, count)
+        found = []
+        for part in range(2):
+            place = place_of(part, spot - hop if to_right else spot + hop, blocks)
+            source = shard.at[blocks, pl.ds(early, late)] if hop == 0 and part == 0 else place
+            found.append(
+                remote(
+                    source,
+                    place,
+                    sends.at[chunk, 2 * hop + part],
+                    gets.at[chunk, 2 * hop + part],
+                    right if to_right else left,
+                )
+            )
+        return found
+
+    def arrivals(to_right, hop, chunk, start, count):
+        gets = right_gets if to_right else left_gets
+        for part in range(2):
+            place = place_of(part, spot - hop if to_right else spot + hop, pl.ds(start, count))
+            kept = 2 * (hop - 1) + part
+            remote(
+                place, place, right_sends.at[chunk, kept], gets.at[chunk, kept], right
+            ).wait_recv()
+
+    def pair_copy(chunk, start, count, owner):
+        place = full.at[pl.ds(start, count), :, owner, core, pl.ds(early, late)]
+        return remote(place, place, pair_sems.at[chunk, 0], pair_sems.at[chunk, 1], across)
+
+    def core_copy(chunk, start, count, owner):
+        place = full.at[pl.ds(start, count), :, :, owner]
+        return remote(place, place, core_sems.at[chunk, 0], core_sems.at[chunk, 1], twin)
+
+    def send_on(hop, chunk, start, count):
+        @pl.when((spot >= hop) & (spot < line - 1))
+        def _():
+            for copy in moves(True, hop, chunk, start, count):
+                copy.start()
+
+        @pl.when((spot < line - hop) & (spot > 0))
+        def _():
+            for copy in moves(False, hop, chunk, start, count):
+                copy.start()
+
+    def take_in(hop, chunk, start, count):
+        @pl.when(spot >= hop)
+        def _():
+            arrivals(True, hop, chunk, start, count)
+
+        @pl.when(spot < line - hop)
+        def _():
+            arrivals(False, hop, chunk, start, count)
+
+    def step(phase, chunk, start, count):
+        if 1 <= phase < line:
+            take_in(phase, chunk, start, count)
+        if phase < line - 1:
+            send_on(phase, chunk, start, count)
+        if phase == line - 1:
+            pair_copy(chunk, start, count, column).start()
+        elif phase == line + 1:
+            pair_copy(chunk, start, count, 1 - column).wait_recv()
+            core_copy(chunk, start, count, core).start()
+        elif phase == line + 2:
+            core_copy(chunk, start, count, 1 - core).wait_recv()
+        elif phase == line + 3:
+            finish(chunk, start, count)
+
+    def finish(chunk, start, count):
+        for hop in range(line - 1):
+
+            @pl.when((spot >= hop) & (spot < line - 1))
+            def _(hop=hop):
+                for copy in moves(True, hop, chunk, start, count):
+                    copy.wait_send()
+
+            @pl.when((spot < line - hop) & (spot > 0))
+            def _(hop=hop):
+                for copy in moves(False, hop, chunk, start, count):
+                    copy.wait_send()
+
+        pair_copy(chunk, start, count, column).wait_send()
+        core_copy(chunk, start, count, core).wait_send()
+
+    return greet, step, early_start, early_wait, finish
+
+
+def block_kernel(
+    size,
+    shard,
+    normed_ref,
+    rows_ref,
+    back_ref,
+    cosine_ref,
+    sine_ref,
+    keep_ref,
+    gain_ref,
+    entry_down_ref,
+    funnel_down_ref,
+    low_lift_ref,
+    pull_lift_ref,
+    ratio_ref,
+    pull_ref,
+    low_output_ref,
+    full,
+    turned_out,
+    plain_out,
+    mixed_out,
+    residual_out,
+    d_normed_out,
+    funneled_out,
+    up_out,
+    down_out,
+    funnel_down_out,
+    funnel_up_out,
+    funnel_seen_out,
+    dots_out,
+    normed,
+    back,
+    floats,
+    turned,
+    plain,
+    mixed,
+    heads_weight,
+    feed_weight,
+    residual,
+    d_normed,
+    funneled,
+    outbox,
+    inbox,
+    lowered,
+    reduced,
+    funnel_lowered,
+    funnel_reduced,
+    right_sends,
+    left_sends,
+    right_gets,
+    left_gets,
+    pair_sems,
+    core_sems,
+    early_sems,
+    local_sems,
+    weight_sems,
+    side_sends,
+    side_gets,
+    out_sems,
+):
+    line = size // 4
+    total_blocks = full.shape[0]
+    chunks = total_blocks // BLOCKS
+    tokens, width = normed.shape[0] - 2 * RANK, normed.shape[1]
+    count = tokens // SEQ
+    sides = {"tensor": 1 - lax.axis_index("tensor")}
+    sems = (right_sends, left_sends, right_gets, left_gets, pair_sems, core_sems, early_sems)
+    greet, step, early_start, early_wait, finish = gather_parts(size, shard, full, sems)
+    me = lax.axis_index("dp")
+    core, column, spot = lax.rem(me, 2), lax.rem(lax.div(me, 2), 2), lax.div(me, 4)
+
+    def tick(now):
+        for phase in range(line + 4):
+            chunk = now - phase
+            start = 1 + BLOCKS * chunk
+            if isinstance(now, int):
+                if 0 <= chunk < chunks:
+                    step(phase, chunk, start, BLOCKS)
+            else:
+
+                @pl.when((chunk >= 0) & (chunk < chunks))
+                def _(phase=phase, chunk=chunk, start=start):
+                    step(phase, chunk, start, BLOCKS)
+
+    own = pltpu.make_async_copy(shard, full.at[:, spot, column, core], local_sems.at[0])
+    own.start()
+    loads = [
+        pltpu.make_async_copy(normed_ref, normed.at[pl.ds(0, tokens)], local_sems.at[1]),
+        pltpu.make_async_copy(back_ref, back, local_sems.at[2]),
+        pltpu.make_async_copy(rows_ref, floats, local_sems.at[3]),
+    ]
+    for load in loads:
+        load.start()
+    greet()
+    early_start()
+    own.wait()
+    early_wait(0)
+    step(0, chunks, 0, 1)
+    tick(0)
+    early_wait(1)
+    for now in range(1, line + 4):
+        step(now, chunks, 0, 1)
+        tick(now)
+    ready = HEAD_CHUNKS - 2 + line + 2
+    lax.fori_loop(line + 4, ready + 1, lambda now, carry: (tick(now), carry)[1], 0)
+    for load in loads:
+        load.wait()
+
+    def head_load(block, slot):
+        return pltpu.make_async_copy(
+            full.at[block], heads_weight.at[slot], weight_sems.at[slot]
+        )
+
+    def head_weight(slot):
+        return heads_weight[slot].reshape(width, CHUNK)
+
+    cut_blocks = turned.shape[0] // 3
+    head_load(0, 0).start()
+
+    def project(block, carry):
+        slot = lax.rem(block, 2)
+
+        @pl.when(block < 3 * cut_blocks - 1)
+        def _():
+            head_load(block + 1, 1 - slot).start()
+
+        head_load(block, slot).wait()
+        for part in range(count):
+            place = pl.ds(part * SEQ, SEQ)
+            result = dot_nn(normed[place], head_weight(slot))
+            plain[block, place] = result.astype(jnp.bfloat16)
+
+            @pl.when(block < 2 * cut_blocks)
+            def _(result=result, place=place):
+                for half in range(CHUNK // HEAD_DIM):
+                    lanes = slice(half * HEAD_DIM, (half + 1) * HEAD_DIM)
+                    head = result[:, lanes]
+                    turned[block, place, lanes] = (
+                        head * cosine_ref[place]
+                        + pltpu.roll(head, HEAD_DIM // 2, 1) * sine_ref[place]
+                    ).astype(jnp.bfloat16)
+
+            @pl.when(block >= 2 * cut_blocks)
+            def _(result=result, place=place):
+                turned[block, place] = result.astype(jnp.bfloat16)
+
+        return carry
+
+    lax.fori_loop(0, 3 * cut_blocks, project, 0)
+    outs = [
+        pltpu.make_async_copy(turned, turned_out, out_sems.at[0]),
+        pltpu.make_async_copy(plain.at[pl.ds(0, 2 * cut_blocks)], plain_out, out_sems.at[1]),
+    ]
+    for out in outs:
+        out.start()
+    tick(ready + 1)
+
+    mixer_loads = [
+        pltpu.make_async_copy(
+            full.at[3 * cut_blocks + b],
+            feed_weight.at[:, :, :, :, pl.ds(b * CHUNK, CHUNK)],
+            weight_sems.at[b],
+        )
+        for b in range(cut_blocks)
+    ]
+    for load in mixer_loads:
+        load.start()
+    line_up = lax.broadcasted_iota(jnp.int32, (SEQ, SEQ), 0)
+    line_on = lax.broadcasted_iota(jnp.int32, (SEQ, SEQ), 1)
+
+    def attend(block, carry):
+        for part in range(count):
+            place = pl.ds(part * SEQ, SEQ)
+            allowed = ((line_up >= line_on) & (keep_ref[part] > 0)) | (line_up == line_on)
+            for half in range(CHUNK // HEAD_DIM):
+                lanes = slice(half * HEAD_DIM, (half + 1) * HEAD_DIM)
+                scores = dot_nt(
+                    turned[block, place, lanes], turned[cut_blocks + block, place, lanes]
+                ) * (HEAD_DIM ** (-0.5))
+                masked = jnp.where(allowed, scores, MASKED)
+                top = jnp.max(masked, axis=1, keepdims=True)
+                weight = jnp.exp(masked - top)
+                attention = weight / jnp.sum(weight, axis=1, keepdims=True)
+                mixed[block, place, lanes] = dot_nn(
+                    attention.astype(jnp.bfloat16), turned[2 * cut_blocks + block, place, lanes]
+                ).astype(jnp.bfloat16)
+        return carry
+
+    lax.fori_loop(0, cut_blocks, attend, 0)
+    outs.append(pltpu.make_async_copy(mixed, mixed_out, out_sems.at[2]))
+    outs[-1].start()
+    tick(ready + 2)
+
+    for load in mixer_loads:
+        load.wait()
+
+    def side_copy(part):
+        place = pl.ds(part * SEQ, SEQ)
+        return pltpu.make_async_remote_copy(
+            src_ref=outbox.at[place],
+            dst_ref=inbox.at[place],
+            send_sem=side_sends.at[part],
+            recv_sem=side_gets.at[part],
+            device_id=sides,
+            device_id_type=MESH,
+        )
+
+    for part in range(count):
+        place = pl.ds(part * SEQ, SEQ)
+        joined = jnp.concatenate([mixed[b, place] for b in range(cut_blocks)], axis=1)
+        per = 512 // (4 * feed_weight.shape[3])
+        for piece in range(width // 512):
+            weight = feed_weight[pl.ds(piece * per, per), :, :, :, pl.ds(0, cut_blocks * CHUNK)]
+            outbox[place, pl.ds(piece * 512, 512)] = dot_nt(
+                joined, weight.reshape(512, cut_blocks * CHUNK)
+            ).astype(jnp.bfloat16)
+        side_copy(part).start()
+    tick(ready + 3)
+
+    tile = 32
+    for part in range(count):
+        side_copy(part).wait()
+
+        def add_up(index, carry, part=part):
+            place = pl.ds(pl.multiple_of(part * SEQ + index * tile, tile), tile)
+            value = floats[place].astype(jnp.float32) + (
+                outbox[place].astype(jnp.float32) + inbox[place].astype(jnp.float32)
+            )
+            residual[place] = value
+            root = lax.rsqrt(jnp.mean(value * value, axis=1, keepdims=True) + NORM_EPS)
+            normed[place] = (value * root * gain_ref[...]).astype(jnp.bfloat16)
+            return carry
+
+        lax.fori_loop(0, SEQ // tile, add_up, 0)
+        if part == 0:
+            tick(ready + 4)
+    outs.append(pltpu.make_async_copy(residual, residual_out, out_sems.at[3]))
+    outs[-1].start()
+    normed[pl.ds(tokens, 2 * RANK)] = entry_down_ref[...]
+    reduced[...] = dot_nt(entry_down_ref[...], normed[pl.ds(0, tokens)]).astype(jnp.bfloat16)
+    funnel_lowered[...] = dot_nt(low_output_ref[...], back[...]).astype(jnp.bfloat16)
+    d_normed[...] = jnp.zeros_like(d_normed)
+    funneled[...] = jnp.zeros_like(funneled)
+    lowered[...] = jnp.zeros_like(lowered)
+    funnel_reduced[...] = jnp.zeros_like(funnel_reduced)
+
+    def feed_load(index):
+        return [
+            pltpu.make_async_copy(
+                full.at[4 * cut_blocks + BLOCKS * index + b],
+                feed_weight.at[:, :, :, :, pl.ds(b * CHUNK, CHUNK)],
+                weight_sems.at[b],
+            )
+            for b in range(BLOCKS)
+        ]
+
+    nothing = jnp.zeros((RANK, CHUNK), jnp.bfloat16)
+
+    def feed(index, carry):
+        @pl.when(index >= EXTRA_TICKS)
+        def _():
+            tick(index + HEAD_CHUNKS + line + 2)
+
+        for load in feed_load(index):
+            load.start()
+        for load in feed_load(index):
+            load.wait()
+        columns = pl.ds(pl.multiple_of(index * CHUNK, CHUNK), CHUNK)
+        weight = feed_weight[:, :, :, :, pl.ds(0, 2 * CHUNK)].reshape(width, 2 * CHUNK)
+        both = dot_nn(normed[...], weight)
+        gate, lifted = both[:tokens, :CHUNK], both[:tokens, CHUNK:]
+        gate_seen = both[tokens : tokens + RANK, :CHUNK]
+        lifted_seen = both[tokens + RANK :, CHUNK:]
+        funnel = feed_weight[:, :, :, :, pl.ds(2 * CHUNK, CHUNK)].reshape(width, CHUNK)
+        d_hidden = dot_nn(back[...], funnel)
+        sigmoid = 1.0 / (1.0 + jnp.exp(-gate))
+        silu = gate * sigmoid
+        hidden = (silu * lifted).astype(jnp.bfloat16)
+        d_gate = (d_hidden * lifted * (sigmoid * (1.0 + gate * (1.0 - sigmoid)))).astype(
+            jnp.bfloat16
+        )
+        d_lifted = (d_hidden * silu).astype(jnp.bfloat16)
+        gate_dots = jnp.sum(d_gate.astype(jnp.float32) * gate, axis=0, keepdims=True)
+        lifted_dots = jnp.sum(d_lifted.astype(jnp.float32) * lifted, axis=0, keepdims=True)
+        dots_out[0:1, columns] = gate_dots
+        dots_out[1:2, columns] = lifted_dots
+        gate_pull = (pull_lift_ref[0, :, columns] * gate_dots).astype(jnp.bfloat16)
+        lifted_pull = (pull_lift_ref[1, :, columns] * lifted_dots).astype(jnp.bfloat16)
+        up_out[0, :, columns] = ADAPTER_SCALE * (
+            dot_nn(reduced[pl.ds(0, RANK)], d_gate) * ratio_ref[0:1, columns]
+            - gate_seen * (pull_ref[0:1, columns] * gate_dots)
+        )
+        up_out[1, :, columns] = ADAPTER_SCALE * (
+            dot_nn(reduced[pl.ds(RANK, RANK)], d_lifted) * ratio_ref[1:2, columns]
+            - lifted_seen * (pull_ref[1:2, columns] * lifted_dots)
+        )
+        lowered[pl.ds(0, RANK)] += dot_nt(low_lift_ref[0, :, columns], d_gate)
+        lowered[pl.ds(RANK, RANK)] += dot_nt(low_lift_ref[1, :, columns], d_lifted)
+        funnel_down_out[:, columns] = ADAPTER_SCALE * dot_nn(funnel_lowered[...], hidden)
+        funnel_down = funnel_down_ref[:, columns]
+        funnel_reduced[...] += dot_nt(funnel_down, hidden)
+        sources = jnp.concatenate([hidden, funnel_down], axis=0)
+        gradients = jnp.concatenate(
+            [
+                jnp.concatenate([d_gate, d_lifted], axis=1),
+                jnp.concatenate([gate_pull, nothing], axis=1),
+                jnp.concatenate([nothing, lifted_pull], axis=1),
+            ],
+            axis=0,
+        )
+        per = 512 // (4 * feed_weight.shape[3])
+        for piece in range(width // 512):
+            near = pl.ds(piece * per, per)
+            funnel_rows = feed_weight[near, :, :, :, pl.ds(2 * CHUNK, CHUNK)]
+            gate_rows = feed_weight[near, :, :, :, pl.ds(0, 2 * CHUNK)]
+            lanes = pl.ds(piece * 512, 512)
+            funneled[:, lanes] += dot_nt(sources, funnel_rows.reshape(512, CHUNK))
+            d_normed[:, lanes] += dot_nt(
+                gradients, gate_rows.reshape(512, 2 * CHUNK)
+            )
+        return carry
+
+    lax.fori_loop(0, chunks - HEAD_CHUNKS, feed, 0)
+    outbox[...] = d_normed[pl.ds(0, tokens)].astype(jnp.bfloat16)
+    outs.append(pltpu.make_async_copy(outbox, d_normed_out, out_sems.at[4]))
+    outs[-1].start()
+    down_out[...] = ADAPTER_SCALE * (
+        dot_nn(lowered[...].astype(jnp.bfloat16), normed[pl.ds(0, tokens)])
+        - d_normed[pl.ds(tokens, 2 * RANK)]
+    )
+    floats[...] = funneled[pl.ds(0, tokens)].astype(jnp.bfloat16)
+    outs.append(pltpu.make_async_copy(floats, funneled_out, out_sems.at[5]))
+    outs[-1].start()
+    funnel_up_out[...] = dot_nn(funnel_reduced[...].astype(jnp.bfloat16), back[...])
+    funnel_seen_out[...] = funneled[pl.ds(tokens, RANK)]
+    finish(chunks - 1, 1 + BLOCKS * (chunks - 1), BLOCKS)
+    for out in outs:
+        out.wait()
+
+
+def run_block(shard, normed_one, rows, back, cosine, sine, keep, gain, small):
+    size = lax.axis_size("dp")
+    line = size // 4
+    tokens, width = rows.shape
+    blocks, height, _ = shard.shape
+    chunks = blocks // BLOCKS
+    cut_blocks = (BLOCKS * HEAD_CHUNKS + 1) // 4
+    wide = small[2].shape[2]
+    anywhere = pl.BlockSpec(memory_space=pl.ANY)
+    local = pl.BlockSpec(memory_space=pltpu.VMEM)
+    low = jnp.bfloat16
+    full = jnp.float32
+    out_shape = (
+        jax.ShapeDtypeStruct((blocks, line, 2, 2, height, CHUNK), low),
+        jax.ShapeDtypeStruct((3 * cut_blocks, tokens, CHUNK), low),
+        jax.ShapeDtypeStruct((2 * cut_blocks, tokens, CHUNK), low),
+        jax.ShapeDtypeStruct((cut_blocks, tokens, CHUNK), low),
+        jax.ShapeDtypeStruct((tokens, width), full),
+        jax.ShapeDtypeStruct((tokens, width), low),
+        jax.ShapeDtypeStruct((tokens, width), low),
+        jax.ShapeDtypeStruct((2, RANK, wide), full),
+        jax.ShapeDtypeStruct((2 * RANK, width), full),
+        jax.ShapeDtypeStruct((RANK, wide), full),
+        jax.ShapeDtypeStruct((RANK, width), full),
+        jax.ShapeDtypeStruct((RANK, width), full),
+        jax.ShapeDtypeStruct((2, wide), full),
+    )
+    scratch = [
+        pltpu.VMEM((tokens + 2 * RANK, width), low),
+        pltpu.VMEM((tokens, width), low),
+        pltpu.VMEM((tokens, width), low),
+        pltpu.VMEM((3 * cut_blocks, tokens, CHUNK), low),
+        pltpu.VMEM((3 * cut_blocks, tokens, CHUNK), low),
+        pltpu.VMEM((cut_blocks, tokens, CHUNK), low),
+        pltpu.VMEM((2, line, 2, 2, height, CHUNK), low),
+        pltpu.VMEM((line, 2, 2, height, 4 * CHUNK), low),
+        pltpu.VMEM((tokens, width), full),
+        pltpu.VMEM((tokens + 2 * RANK, width), full),
+        pltpu.VMEM((tokens + RANK, width), full),
+        pltpu.VMEM((tokens, width), low),
+        pltpu.VMEM((tokens, width), low),
+        pltpu.VMEM((2 * RANK, tokens), full),
+        pltpu.VMEM((2 * RANK, tokens), low),
+        pltpu.VMEM((RANK, tokens), low),
+        pltpu.VMEM((RANK, tokens), full),
+        pltpu.SemaphoreType.DMA((chunks + 1, 2 * (line - 1))),
+        pltpu.SemaphoreType.DMA((chunks + 1, 2 * (line - 1))),
+        pltpu.SemaphoreType.DMA((chunks + 1, 2 * (line - 1))),
+        pltpu.SemaphoreType.DMA((chunks + 1, 2 * (line - 1))),
+        pltpu.SemaphoreType.DMA((chunks + 1, 2)),
+        pltpu.SemaphoreType.DMA((chunks + 1, 2)),
+        pltpu.SemaphoreType.DMA((2, 2)),
+        pltpu.SemaphoreType.DMA((4,)),
+        pltpu.SemaphoreType.DMA((4,)),
+        pltpu.SemaphoreType.DMA((tokens // SEQ,)),
+        pltpu.SemaphoreType.DMA((tokens // SEQ,)),
+        pltpu.SemaphoreType.DMA((6,)),
+    ]
+    return pl.pallas_call(
+        functools.partial(block_kernel, size),
+        name="block",
+        out_shape=out_shape,
+        in_specs=[local] + [anywhere] * 3 + [local] * 11,
+        out_specs=[anywhere] * 7 + [local] * 6,
+        scratch_shapes=scratch,
+        compiler_params=pltpu.CompilerParams(
+            collective_id=1, has_side_effects=True, vmem_limit_bytes=60 * 1024 * 1024
+        ),
+    )(shard, normed_one, rows, back, cosine, sine, keep, gain, *small)
 
 
 def body(
@@ -367,7 +953,7 @@
         ]
     )
     magnitudes = jnp.pad(magnitudes, ((0, -magnitudes.shape[0] % 8), (0, 0)), constant_values=1.0)
-    attend_shard, feed_shard, squares = merge(
+    shard, squares = merge(
         (base_query, base_key, base_value, base_gate, base_widen, base_mixer, base_funnel),
         entry_rows,
         attend_value,
@@ -393,153 +979,152 @@
     split_magnitudes = jnp.concatenate([stature_value.reshape(-1), amplitude_value.reshape(-1)])
     split_ratio = split_magnitudes / split_norms
     shared_ratio = loudness_value / shared_norms
-    attend_all = lax.all_gather(attend_shard, "dp", axis=1, tiled=True)
-    feed_all = lax.all_gather(feed_shard, "dp", axis=1, tiled=True)
-    merged_attend = jnp.concatenate([attend_all[0], attend_all[1], attend_all[2]], axis=1)
-    merged_mixer = attend_all[3]
-    merged_gate, merged_widen, merged_funnel = feed_all
-
-    count = activations.shape[0] // SEQ
-    heads = cut // HEAD_DIM
-    scale = HEAD_DIM ** (-0.5)
     floats = activations.astype(jnp.float32)
     normed_one = low(root_norm(floats, norm_gains[0]))
-    projected = matmul(normed_one, merged_attend)
-    queries = projected[:, :cut]
-    keys = projected[:, cut : 2 * cut]
-    values = projected[:, 2 * cut :]
-    values_low = low(values).reshape(count, SEQ, heads, HEAD_DIM)
-    turned_queries = low(rotate(queries.reshape(-1, heads, HEAD_DIM), positions, 1.0))
-    turned_queries = turned_queries.reshape(count, SEQ, heads, HEAD_DIM)
-    turned_keys = low(rotate(keys.reshape(-1, heads, HEAD_DIM), positions, 1.0))
-    turned_keys = turned_keys.reshape(count, SEQ, heads, HEAD_DIM)
-    allowed = allowed_of(padding_mask, count)
-    scores = (
+    count = activations.shape[0] // SEQ
+    half = jnp.arange(HEAD_DIM // 2, dtype=jnp.float32)
+    angles = positions.astype(jnp.float32)[:, None] * (ROPE_BASE ** (-2.0 * half / HEAD_DIM))[None]
+    cosine = jnp.tile(jnp.cos(angles), (1, 2))
+    sine = jnp.sin(angles)
+    sine = jnp.concatenate([-sine, sine], axis=1)
+    keep = padding_mask.reshape(count, 1, SEQ)
+    feed_ratio = split_ratio[3 * cut :].reshape(2, wide)
+    feed_pull = 1.0 / (split_norms[3 * cut :] * split_magnitudes[3 * cut :]).reshape(2, wide)
+    entry_down = low(jnp.swapaxes(entry_value, 1, 2))
+    small = (
+        entry_down[3:].reshape(2 * RANK, width),
+        low(funnel_value.T),
+        low(widen_value * feed_ratio[:, None]),
+        widen_value * feed_pull[:, None],
+        feed_ratio,
+        feed_pull,
+        low(output_value[1] * shared_ratio[1]),
+    )
+    (
+        full,
+        turned,
+        plain,
+        mixed,
+        residual,
+        d_normed_two,
+        funneled,
+        feed_ups,
+        feed_downs,
+        funnel_down,
+        funnel_up,
+        funnel_seen,
+        feed_dots,
+    ) = run_block(
+        shard, normed_one, activations, cotangent, cosine, sine, keep, norm_gains[1:2], small
+    )
+    blocks = full.shape[0]
+    near = cut // CHUNK
+    heads = CHUNK // HEAD_DIM
+    scale = HEAD_DIM ** (-0.5)
+    full = full.reshape(blocks, width, CHUNK)
+    d_normed_two = swap(d_normed_two)
+    funneled = swap(funneled)
+    attended = residual - floats
+    block_output = low(residual + funneled)
+    back = cotangent.astype(jnp.float32)
+    unused, second_pull = jax.vjp(lambda v: root_norm(v, norm_gains[1]), residual)
+    d_residual = back + second_pull(d_normed_two)[0]
+    d_residual_low = low(d_residual)
+    d_mixed = low(
         jnp.einsum(
-            "bqhd,bkhd->bhqk", turned_queries, turned_keys, preferred_element_type=jnp.float32
-        )
-        * scale
-    )
+            "td,gdc->gtc", d_residual_low, full[3 * near : 4 * near], preferred_element_type=jnp.float32
+        )
+    )
+    split = (near, count, SEQ, heads, HEAD_DIM)
+    d_mixed = d_mixed.reshape(split)
+    turned_queries, turned_keys, values_low = (
+        turned[i * near : (i + 1) * near].reshape(split) for i in range(3)
+    )
+    allowed = allowed_of(padding_mask, count)[None]
+
+    def product(equation, left, right):
+        return jnp.einsum(equation, left, right, preferred_element_type=jnp.float32)
+
+    scores = product("gbqhd,gbkhd->gbhqk", turned_queries, turned_keys) * scale
     masked = jnp.where(allowed, scores, MASKED)
     top = jnp.max(masked, axis=-1, keepdims=True)
     log_total = top + jnp.log(jnp.sum(jnp.exp(masked - top), axis=-1, keepdims=True))
     attention = jnp.exp(masked - log_total)
     attention_low = low(attention)
-    mixed = jnp.einsum(
-        "bhqk,bkhd->bqhd", attention_low, values_low, preferred_element_type=jnp.float32
-    )
-    mixed = low(mixed.reshape(activations.shape[0], cut))
-    attended = swap(matmul_nt(mixed, merged_mixer))
-    residual = floats + attended
-    normed_two = low(root_norm(residual, norm_gains[1]))
-    gate = matmul(normed_two, merged_gate)
-    lifted = matmul(normed_two, merged_widen)
-    hidden = low(jax.nn.silu(gate) * lifted)
-    funneled = swap(matmul_nt(hidden, merged_funnel))
-    block_output = low(residual + funneled)
-
-    back = cotangent.astype(jnp.float32)
-    d_hidden = matmul(cotangent, merged_funnel)
-    unused, silu_pull = jax.vjp(lambda g, u: jax.nn.silu(g) * u, gate, lifted)
-    d_gate, d_lifted = silu_pull(d_hidden)
-    d_gate = low(d_gate)
-    d_lifted = low(d_lifted)
-    d_normed_two = swap(matmul_nt(d_gate, merged_gate) + matmul_nt(d_lifted, merged_widen))
-    unused, second_pull = jax.vjp(lambda v: root_norm(v, norm_gains[1]), residual)
-    d_residual = back + second_pull(d_normed_two)[0]
-    d_residual_low = low(d_residual)
-    d_mixed = low(matmul(d_residual_low, merged_mixer)).reshape(count, SEQ, heads, HEAD_DIM)
-    d_attention = jnp.einsum(
-        "bqhd,bkhd->bhqk", d_mixed, values_low, preferred_element_type=jnp.float32
-    )
-    d_values = jnp.einsum(
-        "bhqk,bqhd->bkhd", attention_low, d_mixed, preferred_element_type=jnp.float32
-    )
-    d_values = low(d_values).reshape(-1, cut)
+    d_attention = product("gbqhd,gbkhd->gbhqk", d_mixed, values_low)
+    d_values = low(product("gbhqk,gbqhd->gbkhd", attention_low, d_mixed))
     d_scores = attention * (d_attention - jnp.sum(attention * d_attention, axis=-1, keepdims=True))
     d_scores = low(d_scores)
-    d_turned_queries = (
-        jnp.einsum("bhqk,bkhd->bqhd", d_scores, turned_keys, preferred_element_type=jnp.float32)
-        * scale
-    )
-    d_turned_keys = (
-        jnp.einsum("bhqk,bqhd->bkhd", d_scores, turned_queries, preferred_element_type=jnp.float32)
-        * scale
-    )
-    d_queries = low(rotate(d_turned_queries.reshape(-1, heads, HEAD_DIM), positions, -1.0))
-    d_keys = low(rotate(d_turned_keys.reshape(-1, heads, HEAD_DIM), positions, -1.0))
-    d_queries = d_queries.reshape(-1, cut)
-    d_keys = d_keys.reshape(-1, cut)
-    d_projected = jnp.concatenate([d_queries, d_keys, d_values], axis=1)
-    d_normed_one = swap(matmul_nt(d_projected, merged_attend))
+    flat = (near, activations.shape[0], heads, HEAD_DIM)
+    d_turned_queries = product("gbhqk,gbkhd->gbqhd", d_scores, turned_keys).reshape(flat) * scale
+    d_turned_keys = product("gbhqk,gbqhd->gbkhd", d_scores, turned_queries).reshape(flat) * scale
+
+    def turn_back(values):
+        swapped = jnp.concatenate([values[..., HEAD_DIM // 2 :], values[..., : HEAD_DIM // 2]], -1)
+        return low(values * cosine[None, :, None] - swapped * sine[None, :, None])
+
+    d_heads = jnp.concatenate(
+        [
+            turn_back(d_turned_queries).reshape(near, -1, CHUNK),
+            turn_back(d_turned_keys).reshape(near, -1, CHUNK),
+            d_values.reshape(near, -1, CHUNK),
+        ]
+    )
+    d_normed_one = swap(product("gtc,gdc->td", d_heads, full[: 3 * near]))
     unused, first_pull = jax.vjp(lambda v: root_norm(v, norm_gains[0]), floats)
     input_gradient = d_residual + first_pull(d_normed_one)[0]
 
-    d_parts = (d_queries, d_keys, d_values, d_gate, d_lifted)
-    parts = (queries, keys, values, gate, lifted)
-    split_dots = jnp.concatenate(
-        [jnp.sum(d.astype(jnp.float32) * y, axis=0) for d, y in zip(d_parts, parts)]
-    )
+    heads_plain = jnp.concatenate([plain, turned[2 * near :]]).astype(jnp.float32)
+    head_dots = jnp.sum(d_heads.astype(jnp.float32) * heads_plain, axis=1).reshape(-1)
+    split_dots = jnp.concatenate([head_dots, feed_dots.reshape(-1)])
     shared_dots = jnp.stack(
         [
             jnp.sum(d_residual_low.astype(jnp.float32) * attended, axis=0),
             jnp.sum(back * funneled, axis=0),
         ]
     )
-    split_pull = split_dots / (split_norms * split_magnitudes)
     shared_pull = shared_dots / (shared_norms * loudness_value)
-
+    head_pull = split_dots[: 3 * cut] / (split_norms[: 3 * cut] * split_magnitudes[: 3 * cut])
     down_gradients = []
     up_gradients = []
-    inputs = (normed_one, normed_one, normed_one, normed_two, normed_two)
-    weights = (
-        attend_all[0],
-        attend_all[1],
-        attend_all[2],
-        merged_gate,
-        merged_widen,
-    )
-    offset = 0
-    for i in range(5):
-        out = weights[i].shape[1]
-        ratio = split_ratio[offset : offset + out]
-        pull = split_pull[offset : offset + out]
-        offset += out
-        low_lift = low(lifts[i] * ratio)
-        pull_lift = low(lifts[i] * pull)
-        lowered = low(matmul_nt(low_lift, d_parts[i]))
+    for i in range(3):
+        ratio = split_ratio[i * cut : (i + 1) * cut]
+        pull = head_pull[i * cut : (i + 1) * cut]
+        part = slice(i * near, (i + 1) * near)
+        low_lift = low(attend_value[i] * ratio).reshape(RANK, near, CHUNK)
+        pull_lift = low(attend_value[i] * pull).reshape(RANK, near, CHUNK)
+        lowered = low(product("rgc,gtc->rt", low_lift, d_heads[part]))
         down_gradients.append(
-            ADAPTER_SCALE * (matmul(lowered, inputs[i]) - matmul_nt(pull_lift, weights[i]))
-        )
-        low_down = low(entry_value[i])
-        reduced = low(matmul(inputs[i], low_down))
-        up_gradients.append(
             ADAPTER_SCALE
-            * (matmul_tn(reduced, d_parts[i]) * ratio - matmul_tn(low_down, weights[i]) * pull)
-        )
-    out_downs = []
-    out_ups = []
-    plan = (
-        (mixed, d_residual_low, mixer_value, merged_mixer),
-        (hidden, cotangent, funnel_value, merged_funnel),
-    )
-    for i, (source, d_out, down, weight) in enumerate(plan):
-        low_lift = low(output_value[i] * shared_ratio[i])
-        pull_lift = low(output_value[i] * shared_pull[i])
-        lowered = low(matmul_nt(low_lift, d_out))
-        out_downs.append(ADAPTER_SCALE * (matmul(lowered, source) - matmul(pull_lift, weight)))
-        low_down = low(down)
-        reduced = low(matmul(source, low_down))
-        out_ups.append(
-            ADAPTER_SCALE
-            * (
-                matmul_tn(reduced, d_out) * shared_ratio[i]
-                - jnp.einsum("ir,ji->rj", low_down, weight, preferred_element_type=jnp.float32)
-                * shared_pull[i]
-            )
-        )
-    shared_terms = jnp.concatenate(down_gradients + out_ups, axis=1)
-    split_terms = jnp.concatenate(up_gradients + out_downs, axis=1)
+            * (matmul(lowered, normed_one) - product("rgc,gdc->rd", pull_lift, full[part]))
+        )
+        reduced = low(matmul_nt(entry_down[i], normed_one))
+        main = product("rt,gtc->rgc", reduced, d_heads[part]).reshape(RANK, cut)
+        seen = product("rd,gdc->rgc", entry_down[i], full[part]).reshape(RANK, cut)
+        up_gradients.append(ADAPTER_SCALE * (main * ratio - seen * pull))
+    down_gradients += [feed_downs[:RANK], feed_downs[RANK:]]
+    up_gradients += [feed_ups[0], feed_ups[1]]
+    low_lift = low(output_value[0] * shared_ratio[0])
+    pull_lift = low(output_value[0] * shared_pull[0])
+    lowered = low(matmul_nt(low_lift, d_residual_low))
+    mixer_weight = full[3 * near : 4 * near]
+    mixer_down = ADAPTER_SCALE * (
+        product("rt,gtc->rgc", lowered, mixed) - product("rd,gdc->rgc", pull_lift, mixer_weight)
+    ).reshape(RANK, cut)
+    low_down = low(mixer_value.T).reshape(RANK, near, CHUNK)
+    reduced = low(product("rgc,gtc->rt", low_down, mixed))
+    mixer_up = ADAPTER_SCALE * (
+        matmul(reduced, d_residual_low) * shared_ratio[0]
+        - product("rgc,gdc->rd", low_down, mixer_weight) * shared_pull[0]
+    )
+    pull_lift = low(output_value[1] * shared_pull[1])
+    funnel_weight = full[4 * near :].reshape(-1, BLOCKS, width, CHUNK)[:, 2]
+    funnel_down = funnel_down - ADAPTER_SCALE * product(
+        "rd,gdc->rgc", pull_lift, funnel_weight
+    ).reshape(RANK, wide)
+    funnel_up = ADAPTER_SCALE * (funnel_up * shared_ratio[1] - funnel_seen * shared_pull[1])
+    shared_terms = jnp.concatenate(down_gradients + [mixer_up, funnel_up], axis=1)
+    split_terms = jnp.concatenate(up_gradients + [mixer_down, funnel_down], axis=1)
     shared_terms, split_terms, split_dots, shared_dots = lax.psum(
         (shared_terms, split_terms, split_dots, shared_dots), "dp"
     )

time: 935 us -> 893 us (0.955)
  Pallas kernels: 28.4 us -> 346 us
  waiting for transfers between devices: 427 us -> 120 us
  matrix products: 244 us -> 78.7 us
  local copies, waits for them, and re-layouts: 71.2 us -> 184 us
    pallas_call x0 -> x1, Pallas kernels: none -> 319 us  [run_block(): pl.pallas_call(functools.partial(block_kernel, size), name='block', out_s...]
    all_gather x2 -> x0, waiting for transfers between devices: 196 us -> none  [the longest x1 119 us: body(): attend_all = lax.all_gather(attend_shard, 'dp', axis=1, tiled=True)]
    ppermute x4 -> x3, waiting for transfers between devices: 122 us -> 0.01 us  [swap(): lax.ppermute(low, 'tensor', [(i, (i + step) % size) for i in range(size)])]
    dot_general x14 -> x4, matrix products: 93.5 us -> 8.77 us  [matmul(): return jnp.dot(left, right, preferred_element_type=jnp.float32)]
    dot_general x30 -> x20, matrix products: 150 us -> 69.9 us  [the longest x19 66.6 us: product(): return jnp.einsum(equation, left, right, preferred_element_type=jnp.float32)]
    slice x7 -> x22, local copies, waits for them, and re-layouts: 1.26 us -> 76.8 us  [the longest x2 33.8 us: body(): funnel_weight = full[4 * near:].reshape(-1, BLOCKS, width, CHUNK)[:, 2]]
    reshape x1 -> x14, local copies, waits for them, and re-layouts: 2.42 us -> 24 us  [the longest x5 11.5 us: body(): turned[i * near:(i + 1) * near].reshape(split)]
    psum x1, waiting for transfers between devices: 80.4 us -> 91.3 us  [body(): lax.psum((shared_terms, split_terms, split_dots, shared_dots), 'dp')]
  transfers between devices with their start and end apart: 8 -> 5, of which waited for: 7 -> 2; matrix products, arithmetic and copies ran while one was open for 12% -> 26% of each run, Pallas kernels for 0% -> 0%
where the time goes in v3:
time: 893 us; the launch traced here: 882 us
  Pallas kernels  346 us (39%)
  local copies, waits for them, and re-layouts  184 us (21%)
  waiting for transfers between devices  120 us (13%)
  matrix products  78.7 us (9%)
  other arithmetic  64 us (7%)
  blocking collectives  63.9 us (7%)
  between operations  20.9 us (2%)
    pallas_call x1, Pallas kernels, run_block(): pl.pallas_call(functools.partial(block_kernel, size), name='block', out_s...  319 us
    psum x1, waiting for transfers between devices, body(): lax.psum((shared_terms, split_terms, split_dots, shared_dots), 'dp')  91.3 us
    dot_general x19, matrix products, product(): return jnp.einsum(equation, left, right, preferred_element_type=jnp.float32)  66.6 us
    psum x1, blocking collectives, body(): lax.psum((shared_terms, split_terms, split_dots, shared_dots), 'dp')  58.3 us
    unnamed x242, local copies, waits for them, and re-layouts  45.2 us
    slice x2, local copies, waits for them, and re-layouts, body(): funnel_weight = full[4 * near:].reshape(-1, BLOCKS, width, CHUNK)[:, 2]  33.8 us
    psum x1, waiting for transfers between devices, body(): shared_terms, split_total = lax.psum((shared_terms, split_total), 'tensor')  29.1 us
    pallas_call x1, Pallas kernels, merge(): pl.pallas_call(functools.partial(merge_kernel, size, sides), name='merge'...  27.1 us
  transfers between devices with their start and end apart: 5, of which 2 were waited for; matrix products, arithmetic and copies ran while one was open for 26% of the time, Pallas kernels for 0%

profile of v3, /device:TPU:0, one launch (start us, length us, event | category | flops | bytes accessed | tf_op | source)
XLA Modules:
  0.0 882.2 jit_solution(16101716292260228638)
XLA Ops:
  24.4 27.1 %merge.1 = (bf16[49,128,256]{2,1,0:T(8,128)(2,1)}, f32[16,1024]{1,0:T(8,128)S(1)}) custom-call(bf16[128,1024]{1,0:T(8,128)(2,1)S(1)} %copy-done.8, bf16[128,1024]{1,0:T(8,128)(2,1)S(1)} %copy-done.9, bf16[128,1024]{1,0:T(8,128)(2,1)S(1)} %copy-done.10, bf16[128,2816]{1,0:T(8,128)(2,1)S(1)} %copy-done.5, bf16[128,2816]{1,0:T(8,128)(2,1)S(1)} %copy-done.6, ...), custom_call_target="tpu_custom_call" | custom-call | tf_op jit(solution)/shard_map/merge/pallas_call | solution.py:258
  67.4 319.1 %block.1 = (bf16[49,4,2,2,128,256]{5,4,3,2,1,0:T(8,128)(2,1)}, bf16[12,512,256]{2,1,0:T(8,128)(2,1)}, bf16[8,512,256]{2,1,0:T(8,128)(2,1)}, bf16[4,512,256]{2,1,...) custom-call(bf16[49,128,256]{2,1,0:T(8,128)(2,1)} %get-tuple-element, ...), custom_call_target="tpu_custom_call" | custom-call | tf_op jit(solution)/shard_map/block/pallas_call | solution.py:852
  389.3 12.2 %fusion.153 = (bf16[4,4,2,2,128,256]{5,4,3,2,1,0:T(8,128)(2,1)}, bf16[4,4,2,2,128,256]{5,4,3,2,1,0:T(8,128)(2,1)}, bf16[4,4,2,2,128,256]{5,4,3,2,1,0:T(8,128)(2,1)}, bf16[4,4,2,2,128,256]{5,4,3,2,1,0:T(8,128)(2,1)}) fusion(bf16[49,4,2,2,128,256]{5,4,3,2,1,0:T(8,128)(2,1)} %get-tuple-element.51), kind=kLoop, calls=%fused_computation.274 | loop fusion | bytes 33554432 | tf_op jit(solution)/shard_map/slice | solution.py:1103
  401.6 10.7 %slice.289 = bf16[12,4,2,2,128,256]{5,4,3,2,1,0:T(8,128)(2,1)} slice(bf16[49,4,2,2,128,256]{5,4,3,2,1,0:T(8,128)(2,1)} %get-tuple-element.51), slice={[0:12], [0:4], [0:2], [0:2], [0:128], [0:256]} | slice | bytes 25165824 | tf_op jit(solution)/shard_map/slice | solution.py:1073
  413.5 24.0 %slice.313 = bf16[33,4,2,2,128,256]{5,4,3,2,1,0:T(8,128)(2,1)} slice(bf16[49,4,2,2,128,256]{5,4,3,2,1,0:T(8,128)(2,1)} %get-tuple-element.51), slice={[16:49], [0:4], [0:2], [0:2], [0:128], [0:256]} | slice | bytes 69206016 | tf_op jit(solution)/shard_map/slice | solution.py:1121
  437.4 3.4 fusion.154
  441.9 2.4 copy.141
  444.3 2.2 reshape.392
  446.5 3.6 copy.147
  450.7 2.2 reshape.394
  457.2 3.0 convolution_bitcast_fusion.8
  469.7 2.9 convolution_bitcast_fusion.6
  473.2 9.8 %slice.369 = bf16[11,1,2048,256]{3,2,1,0:T(8,128)(2,1)} slice(bf16[11,3,2048,256]{3,2,1,0:T(8,128)(2,1)} %bitcast.298), slice={[0:11], [2:3], [0:2048], [0:256]} | slice | bytes 23068672 | tf_op jit(solution)/shard_map/slice | solution.py:1121
  483.0 15.5 %copy.176 = bf16[11,1,2048,256]{2,3,0,1:T(8,128)(2,1)} copy(bf16[11,1,2048,256]{3,2,1,0:T(8,128)(2,1)} %slice.369) | data formatting | bytes 23068672
  499.5 2.2 fusion.10
  501.8 2.1 copy-done.15
  512.0 3.4 fusion.44
  516.9 3.8 multiply_reduce_fusion.1
  522.0 2.8 broadcast_multiply_fusion
  524.8 2.5 broadcast_multiply_fusion.1
  530.5 2.6 fusion.156
  533.1 2.8 copy.149
  535.9 2.7 reshape.396
  540.5 2.7 fusion.155
  543.2 4.1 copy.143
  547.3 4.0 reshape.395
  555.1 5.8 fusion.31
  561.0 11.8 %bitcast_convert_fusion = bf16[512,2048]{1,0:T(8,128)(2,1)} fusion(bf16[12,2048,256]{2,1,0:T(8,128)(2,1)} %bitcast.314, bf16[4,512,256]{2,1,0:T(8,128)(2,1)S(1)} %reshape.397, bf16[4,512,256]{2,1,0:T(8,128)(2,1)S(1)} %get-tuple-element.114, bf16[4,512,256]{2,1,0:T(8,128)(2,1)S(1)} %get-tuple-element.113), kind=kOutput, calls=%fused_computation.18 | convolution fusion | flops 6446645248 | bytes 17825792 | tf_op jit(solution)/shard_map/gtc,gdc->td/dot_general | solution.py:1046
  579.6 2.3 copy.155
  581.9 2.3 copy.157
  585.5 2.7 fusion.68
  588.2 4.0 fusion.21
  592.2 2.6 fusion.67
  597.0 4.2 fusion.18
  603.7 2.5 fusion.58
  606.2 2.9 fusion.55
  609.2 2.9 fusion.52
  612.1 3.3 fusion.73
  620.3 6.1 fusion.7
  627.9 8.9 %fusion = (f32[2048]{0:T(1024)S(1)}, bf16[512,2048]{1,0:T(8,128)(2,1)}, f32[512,2048]{1,0:T(8,128)}) fusion(bf16[512,2048]{1,0:T(8,128)(2,1)S(1)} %copy-done.26, bf16[512,2048]{1,0:T(8,128)(2,1)} %collective-permute-done, bf16[512,2048]{1,0:T(8,128)(2,1)S(1)} %copy-done.44, f32[512,2048]{1,0:T(8,128)S(1)} %copy-done.14, f32[512]{0:T(512)S(1)} %multiply_multiply_fusion.9, ...), kind=kLoop, calls=%fused_computation.10 | loop fusion | flops 28309504 | bytes 27295744 | tf_op jit(solution)/shard_map/reduce_sum | solution.py:1083
  636.9 58.3 %all-reduce.2 = (f32[8704]{0:T(1024)}, f32[2,2048]{1,0:T(2,128)S(1)}) all-reduce(f32[8704]{0:T(1024)S(1)} %pad_maximum_fusion.4, f32[2,2048]{1,0:T(2,128)S(1)} %pad_maximum_fusion.5), channel_id=1, replica_groups=mesh['dp'=16,'tensor'=2] {'dp'}, use_global_device_ids=true, to_apply=%region_12.13 | all-reduce | flops 12800 | bytes 102400 | tf_op jit(solution)/shard_map/psum | solution.py:1128
  696.5 3.5 fusion.12
  706.8 8.0 fusion.9
  716.1 91.3 %all-reduce.9.cloned.1.call-done = (f32[16,12544]{1,0:T(8,128)}, f32[16,14336]{1,0:T(8,128)}) async-done(((f32[16,12544]{1,0:T(8,128)}, f32[16,14336]{1,0:T(8,128)}), (f32[16,12544]{1,0:T(8,128)}, f32[16,14336]{1,0:T(8,128)})) %all-reduce.9.cloned.1.call-update) | async-done | bytes 1720336 | tf_op jit(solution)/shard_map/psum | solution.py:1128
  810.7 5.6 psum.44
  818.3 29.1 %all-reduce.7.cloned.1.call-done = f32[16,14336]{1,0:T(8,128)} async-done(((f32[16,14336]{1,0:T(8,128)}), f32[16,14336]{1,0:T(8,128)}) %all-reduce.7.cloned.1.call-update) | async-done | bytes 917520 | tf_op jit(solution)/shard_map/psum | solution.py:1134
  861.2 2.1 multiply_subtract_fusion.2
  867.0 2.7 multiply_subtract_fusion
  (364 shorter events, 124.5 us)
Async XLA Ops:
  7.2 800.2 %all-reduce.9.cloned.1.call-start = ((), (), s32[]{:S(2)}) async-start(), calls=%async_computation.1 | async-start | bytes 3440640 | tf_op jit(solution)/shard_map/psum | solution.py:1128
  8.9 42.7 %copy-start.39 = (f32[5,2048,16]{1,2,0:T(8,128)S(1)}, f32[5,2048,16]{1,2,0:T(8,128)}, u32[]{:S(2)}) copy-start(f32[5,2048,16]{1,2,0:T(8,128)} %param.51) | copy-start | bytes 1966084
  10.4 42.0 %copy-start.45 = (f32[2816,16]{0,1:T(8,128)S(1)}, f32[2816,16]{0,1:T(8,128)}, u32[]{:S(2)}) copy-start(f32[2816,16]{0,1:T(8,128)} %param.55) | copy-start | bytes 540676
  11.5 42.3 %copy-start.54 = (f32[2,2816]{1,0:T(2,128)S(1)}, f32[2,2816]{1,0:T(2,128)}, u32[]{:S(2)}) copy-start(f32[2,2816]{1,0:T(2,128)} %param.58) | copy-start | bytes 67588
  13.1 40.8 %copy-start.61 = (f32[2,2048]{1,0:T(2,128)S(1)}, f32[2,2048]{1,0:T(2,128)}, u32[]{:S(2)}) copy-start(f32[2,2048]{1,0:T(2,128)} %param.59) | copy-start | bytes 49156
  14.6 40.0 %copy-start.81 = (f32[3072]{0:T(1024)}, f32[3072]{0:T(1024)S(1)}, u32[]{:S(2)}) copy-start(f32[3072]{0:T(1024)S(1)} %reshape.386) | copy-start | bytes 36868
  24.4 37.4 %copy-start.113 = (s32[512]{0:T(512)S(1)}, s32[512]{0:T(512)}, u32[]{:S(2)}) copy-start(s32[512]{0:T(512)} %param.42) | copy-start | bytes 6148
  51.5 12.3 %copy-start.1 = (f32[2,16,2816]{2,1,0:T(8,128)S(1)}, f32[2,16,2816]{2,1,0:T(8,128)}, u32[]{:S(2)}) copy-start(f32[2,16,2816]{2,1,0:T(8,128)} %lift_ref.1) | copy-start | bytes 1081348
  51.5 13.1 %copy-start.17 = (bf16[512,2048]{1,0:T(8,128)(2,1)S(1)}, bf16[512,2048]{1,0:T(8,128)(2,1)}, u32[]{:S(2)}) copy-start(bf16[512,2048]{1,0:T(8,128)(2,1)} %rows_ref.1) | copy-start | bytes 6291460
  53.1 9.7 %copy-start.69 = (f32[8704]{0:T(1024)}, f32[8704]{0:T(1024)S(1)}, u32[]{:S(2)}) copy-start(f32[8704]{0:T(1024)S(1)} %constant_dynamic-update-slice_fusion.2) | copy-start | bytes 104452
  53.8 12.7 %copy-start.76 = (f32[8704]{0:T(1024)}, f32[8704]{0:T(1024)S(1)}, u32[]{:S(2)}) copy-start(f32[8704]{0:T(1024)S(1)} %get-tuple-element.137) | copy-start | bytes 104452
  53.8 12.7 %copy-start.67 = (f32[2,2816]{1,0:T(2,128)}, f32[2,2816]{1,0:T(2,128)S(1)}, u32[]{:S(2)}) copy-start(f32[2,2816]{1,0:T(2,128)S(1)} %multiply_divide_fusion.pull_ref) | copy-start | bytes 67588
  53.9 12.6 %copy-start.68 = (f32[2,2816]{1,0:T(2,128)}, f32[2,2816]{1,0:T(2,128)S(1)}, u32[]{:S(2)}) copy-start(f32[2,2816]{1,0:T(2,128)S(1)} %mul.879.ratio_ref) | copy-start | bytes 67588
  53.9 12.6 %copy-start.74 = (f32[2,2048]{1,0:T(2,128)}, f32[2,2048]{1,0:T(2,128)S(1)}, u32[]{:S(2)}) copy-start(f32[2,2048]{1,0:T(2,128)S(1)} %sqrt.48) | copy-start | bytes 49156
  60.2 326.3 %copy-start.96 = (f32[512]{0:T(512)}, f32[512]{0:T(512)S(1)}, u32[]{:S(2)}) copy-start(f32[512]{0:T(512)S(1)} %fusion.2) | copy-start | bytes 6148
  60.2 326.3 %copy-start.98 = (f32[512]{0:T(512)}, f32[512]{0:T(512)S(1)}, u32[]{:S(2)}) copy-start(f32[512]{0:T(512)S(1)} %fusion.137) | copy-start | bytes 6148
  67.4 321.2 %copy-start.112 = (s32[512]{0:T(512)S(1)}, s32[512]{0:T(512)}, u32[]{:S(2)}) copy-start(s32[512]{0:T(512)} %param.41) | copy-start | bytes 6148
  386.5 120.4 %collective-permute-start.1 = (bf16[512,2048]{1,0:T(8,128)(2,1)}, bf16[512,2048]{1,0:T(8,128)(2,1)S(1)}, u32[]{:S(2)}, u32[]{:S(2)}) collective-permute-start(bf16[512,2048]{1,0:T(8,128)(2,1)} %get-tuple-element.49), channel_id=1, source_target_pairs={{0,1},{1,0},{2,3},{3,2},{4,5},{5,4},{6,7},{7,6},{8,9},{9,8},{10,11... | collective-permute-start | bytes 6291464 | tf_op jit(solution)/shard_map/ppermute | solution.py:79
  388.3 238.2 %collective-permute-start = (bf16[512,2048]{1,0:T(8,128)(2,1)}, bf16[512,2048]{1,0:T(8,128)(2,1)}, u32[]{:S(2)}, u32[]{:S(2)}) collective-permute-start(bf16[512,2048]{1,0:T(8,128)(2,1)} %get-tuple-element.48), channel_id=1, source_target_pairs={{0,1},{1,0},{2,3},{3,2},{4,5},{5,4},{6,7},{7,6},{8,9},{9,8},{10,11... | collective-permute-start | bytes 6291464 | tf_op jit(solution)/shard_map/ppermute | solution.py:79
  401.6 10.7 %copy-start.51 = (f32[1024,16]{0,1:T(8,128)S(1)}, f32[1024,16]{0,1:T(8,128)}, u32[]{:S(2)}) copy-start(f32[1024,16]{0,1:T(8,128)} %param.54) | copy-start | bytes 196612
  401.6 11.3 %copy-start.63 = (f32[3,1024]{1,0:T(4,128)S(1)}, f32[3,1024]{1,0:T(4,128)}, u32[]{:S(2)}) copy-start(f32[3,1024]{1,0:T(4,128)} %param.57) | copy-start | bytes 36868
  441.9 12.7 %copy-start.95 = (f32[2,2816]{1,0:T(2,128)S(1)}, f32[2,2816]{1,0:T(2,128)}, u32[]{:S(2)}) copy-start(f32[2,2816]{1,0:T(2,128)} %get-tuple-element.56) | copy-start | bytes 67588
  560.9 13.6 %copy-start.31 = (bf16[4,512,256]{2,1,0:T(8,128)(2,1)}, bf16[4,512,256]{2,1,0:T(8,128)(2,1)S(1)}, u32[]{:S(2)}) copy-start(bf16[4,512,256]{2,1,0:T(8,128)(2,1)S(1)} %get-tuple-element.114) | copy-start | bytes 3145732
  561.0 13.6 %copy-start.32 = (bf16[4,512,256]{2,1,0:T(8,128)(2,1)}, bf16[4,512,256]{2,1,0:T(8,128)(2,1)S(1)}, u32[]{:S(2)}) copy-start(bf16[4,512,256]{2,1,0:T(8,128)(2,1)S(1)} %get-tuple-element.113) | copy-start | bytes 3145732
  561.0 13.6 %copy-start.34 = (bf16[4,512,256]{2,1,0:T(8,128)(2,1)S(1)}, bf16[4,512,256]{2,1,0:T(8,128)(2,1)}, u32[]{:S(2)}) copy-start(bf16[4,512,256]{2,1,0:T(8,128)(2,1)} %get-tuple-element.106) | copy-start | bytes 3145732
  561.0 13.6 %copy-start.43 = (bf16[8,512,256]{2,1,0:T(8,128)(2,1)S(1)}, bf16[8,512,256]{2,1,0:T(8,128)(2,1)}, u32[]{:S(2)}) copy-start(bf16[8,512,256]{2,1,0:T(8,128)(2,1)} %get-tuple-element.52) | copy-start | bytes 6291460
  572.8 47.5 %collective-permute-start.2 = (bf16[512,2048]{1,0:T(8,128)(2,1)}, bf16[512,2048]{1,0:T(8,128)(2,1)}, u32[]{:S(2)}, u32[]{:S(2)}) collective-permute-start(bf16[512,2048]{1,0:T(8,128)(2,1)} %bitcast_convert_fusion), channel_id=1, source_target_pairs={{0,1},{1,0},{2,3},{3,2},{4,5},{5,4},{6,7},{7,6},{8,9},{9,8},{10,11... | collective-permute-start | bytes 6291464 | tf_op jit(solution)/shard_map/ppermute | solution.py:79
  575.4 10.1 %copy-start.12 = (bf16[512,2048]{1,0:T(8,128)(2,1)S(1)}, bf16[512,2048]{1,0:T(8,128)(2,1)}, u32[]{:S(2)}) copy-start(bf16[512,2048]{1,0:T(8,128)(2,1)} %fusion.4.normed_ref) | copy-start | bytes 6291460
  575.4 10.1 %copy-start.50 = (f32[16,4,256]{2,1,0:T(4,128)S(1)}, f32[16,4,256]{2,1,0:T(4,128)}, u32[]{:S(2)}) copy-start(f32[16,4,256]{2,1,0:T(4,128)} %squeeze.49) | copy-start | bytes 196612
  609.2 11.1 %copy-start.78 = (f32[1,2048]{1,0:T(1,128)S(1)}, f32[1,2048]{1,0:T(1,128)}, u32[]{:S(2)}) copy-start(f32[1,2048]{1,0:T(1,128)} %copy-done.77) | copy-start | bytes 24580
  626.4 68.8 %copy-start.75 = (f32[2,2048]{1,0:T(2,128)S(1)}, f32[2,2048]{1,0:T(2,128)}, u32[]{:S(2)}) copy-start(f32[2,2048]{1,0:T(2,128)} %copy-done.74) | copy-start | bytes 49156
  626.4 70.0 %copy-start.58 = (bf16[1024,16]{0,1:T(8,128)(2,1)S(1)}, bf16[1024,16]{0,1:T(8,128)(2,1)}, u32[]{:S(2)}) copy-start(bf16[1024,16]{0,1:T(8,128)(2,1)} %convert_element_type.212) | copy-start | bytes 98308
  714.8 146.3 %copy-start.41 = (f32[2,16,2048]{2,1,0:T(8,128)S(1)}, f32[2,16,2048]{2,1,0:T(8,128)}, u32[]{:S(2)}) copy-start(f32[2,16,2048]{2,1,0:T(8,128)} %param.56) | copy-start | bytes 786436
  714.8 148.5 %copy-start.46 = (f32[2816,16]{0,1:T(8,128)S(1)}, f32[2816,16]{0,1:T(8,128)}, u32[]{:S(2)}) copy-start(f32[2816,16]{0,1:T(8,128)} %param.55) | copy-start | bytes 540676
  714.8 132.5 %all-reduce.7.cloned.1.call-start = ((), (), s32[]{:S(2)}) async-start(), calls=%async_computation | async-start | bytes 1835008 | tf_op jit(solution)/shard_map/psum | solution.py:1134
  809.4 56.0 %copy-start.52 = (f32[1024,16]{0,1:T(8,128)S(1)}, f32[1024,16]{0,1:T(8,128)}, u32[]{:S(2)}) copy-start(f32[1024,16]{0,1:T(8,128)} %param.54) | copy-start | bytes 196612
  810.7 56.3 %copy-start.40 = (f32[5,2048,16]{1,2,0:T(8,128)S(1)}, f32[5,2048,16]{1,2,0:T(8,128)}, u32[]{:S(2)}) copy-start(f32[5,2048,16]{1,2,0:T(8,128)} %param.51) | copy-start | bytes 1966084
  810.7 56.3 %copy-start.48 = (f32[5,2048,16]{1,2,0:T(8,128)S(1)}, f32[5,2048,16]{1,2,0:T(8,128)}, u32[]{:S(2)}) copy-start(f32[5,2048,16]{1,2,0:T(8,128)} %param.60) | copy-start | bytes 1966084
  857.1 13.3 %copy-start.55 = (f32[2,2816]{1,0:T(2,128)S(1)}, f32[2,2816]{1,0:T(2,128)}, u32[]{:S(2)}) copy-start(f32[2,2816]{1,0:T(2,128)} %param.58) | copy-start | bytes 67588
  861.1 9.3 %copy-start.84 = (f32[2,2816]{1,0:T(2,128)S(1)}, f32[2,2816]{1,0:T(2,128)}, u32[]{:S(2)}) copy-start(f32[2,2816]{1,0:T(2,128)} %mul.1099) | copy-start | bytes 67588
  861.1 9.3 %copy-start.93 = (f32[2,2816]{1,0:T(2,128)S(1)}, f32[2,2816]{1,0:T(2,128)}, u32[]{:S(2)}) copy-start(f32[2,2816]{1,0:T(2,128)} %param.67) | copy-start | bytes 67588
  861.1 9.9 %copy-start.64 = (f32[3,1024]{1,0:T(4,128)S(1)}, f32[3,1024]{1,0:T(4,128)}, u32[]{:S(2)}) copy-start(f32[3,1024]{1,0:T(4,128)} %param.57) | copy-start | bytes 36868
  861.2 9.9 %copy-start.89 = (f32[3,1024]{1,0:T(4,128)S(1)}, f32[3,1024]{1,0:T(4,128)}, u32[]{:S(2)}) copy-start(f32[3,1024]{1,0:T(4,128)} %mul.1083) | copy-start | bytes 36868
  861.2 9.9 %copy-start.110 = (f32[3,1024]{1,0:T(4,128)S(1)}, f32[3,1024]{1,0:T(4,128)}, u32[]{:S(2)}) copy-start(f32[3,1024]{1,0:T(4,128)} %param.66) | copy-start | bytes 36868
  861.2 9.9 %copy-start.111 = (f32[3,1024]{1,0:T(4,128)S(1)}, f32[3,1024]{1,0:T(4,128)}, u32[]{:S(2)}) copy-start(f32[3,1024]{1,0:T(4,128)} %param.75) | copy-start | bytes 36868
  861.2 10.6 %copy-start.2 = (f32[2,16,2816]{2,1,0:T(8,128)S(1)}, f32[2,16,2816]{2,1,0:T(8,128)}, u32[]{:S(2)}) copy-start(f32[2,16,2816]{2,1,0:T(8,128)} %lift_ref.1) | copy-start | bytes 1081348
  861.2 10.6 %copy-start.56 = (f32[2,16,2816]{2,1,0:T(8,128)S(1)}, f32[2,16,2816]{2,1,0:T(8,128)}, u32[]{:S(2)}) copy-start(f32[2,16,2816]{2,1,0:T(8,128)} %param.62) | copy-start | bytes 1081348
  861.2 10.5 %copy-start.57 = (f32[2,16,2816]{2,1,0:T(8,128)S(1)}, f32[2,16,2816]{2,1,0:T(8,128)}, u32[]{:S(2)}) copy-start(f32[2,16,2816]{2,1,0:T(8,128)} %param.71) | copy-start | bytes 1081348
  (71 other events, 361.3 us)
Sparse Core Ops, SparseCore 0:
  715.0 92.4 all-reduce.8
  810.9 36.4 all-reduce.6

commit v4 on v3

--- a/solution.py
+++ b/solution.py
@@ -862,6 +862,667 @@
     )(shard, normed_one, rows, back, cosine, sine, keep, gain, *small)
 
 
+def tail_kernel(
+    full,
+    turned_ref,
+    plain_ref,
+    mixed_ref,
+    residual_ref,
+    d_normed_ref,
+    funneled_ref,
+    back_ref,
+    rows_ref,
+    normed_ref,
+    cosine_ref,
+    sine_ref,
+    keep_ref,
+    gain_ref,
+    entry_down_ref,
+    low_lift_ref,
+    pull_lift_ref,
+    ratio_ref,
+    pull_ref,
+    mixer_down_ref,
+    low_output_ref,
+    pull_output_ref,
+    output_ratio_ref,
+    output_pull_ref,
+    funnel_down_ref,
+    funnel_up_ref,
+    funnel_seen_ref,
+    feed_dots_ref,
+    partial_out,
+    d_residual_out,
+    funneled_out,
+    down_out,
+    up_out,
+    mixer_down_out,
+    mixer_up_out,
+    funnel_down_out,
+    funnel_up_out,
+    dots_out,
+    weights,
+    residual,
+    floats,
+    back,
+    normed,
+    turned,
+    plain,
+    mixed,
+    own,
+    inbox,
+    funneled,
+    attention,
+    d_low,
+    d_heads,
+    funnel_weight,
+    dots_box,
+    mixer_dots,
+    load_sems,
+    weight_sems,
+    funnel_sems,
+    side_sends,
+    side_gets,
+    out_sems,
+):
+    tokens, width = back.shape
+    count = tokens // SEQ
+    cut = d_heads.shape[2]
+    near = cut // CHUNK
+    wide = funnel_down_ref.shape[1]
+    scale = HEAD_DIM ** (-0.5)
+    other = {"tensor": 1 - lax.axis_index("tensor")}
+    halves = CHUNK // HEAD_DIM
+
+    loads = [
+        pltpu.make_async_copy(source, target, load_sems.at[i])
+        for i, (source, target) in enumerate(
+            (
+                (funneled_ref, funneled),
+                (back_ref, back),
+                (turned_ref, turned),
+                (normed_ref, normed),
+                (d_normed_ref, own),
+                (residual_ref, residual),
+                (rows_ref, floats),
+                (mixed_ref, mixed),
+                (plain_ref, plain),
+            )
+        )
+    ]
+    weight_loads = [
+        pltpu.make_async_copy(
+            full.at[near * i + b],
+            weights.at[i, :, :, :, :, pl.ds(b * CHUNK, CHUNK)],
+            weight_sems.at[near * i + b],
+        )
+        for i in range(4)
+        for b in range(near)
+    ]
+    for load in loads[:3]:
+        load.start()
+    barrier = pltpu.get_barrier_semaphore()
+    pl.semaphore_signal(barrier, inc=1, device_id=other, device_id_type=MESH)
+    pl.semaphore_wait(barrier, 1)
+
+    def remote(source, target, index):
+        return pltpu.make_async_remote_copy(
+            src_ref=source,
+            dst_ref=target,
+            send_sem=side_sends.at[index],
+            recv_sem=side_gets.at[index],
+            device_id=other,
+            device_id_type=MESH,
+        )
+
+    def rows_of(part):
+        return pl.ds(part * SEQ, SEQ)
+
+    part_copies = [
+        remote(d_normed_ref.at[rows_of(part)], inbox.at[rows_of(part)], part)
+        for part in range(count)
+    ]
+    part_copies[0].start()
+    for load in loads[3:] + weight_loads:
+        load.start()
+    dots_copy = remote(dots_box.at[0], dots_box.at[1], count)
+    funneled_copy = remote(funneled_ref, funneled_out, count + 1)
+
+    def weight_of(i):
+        return weights[i].reshape(width, cut)
+
+    loads[0].wait()
+    loads[1].wait()
+    tile = 64
+
+    def count_dots(index, total):
+        place = pl.ds(pl.multiple_of(index * tile, tile), tile)
+        return total + jnp.sum(
+            back[place].astype(jnp.float32) * funneled[place].astype(jnp.float32),
+            axis=0,
+            keepdims=True,
+        )
+
+    funnel_dots = lax.fori_loop(
+        0, tokens // tile, count_dots, jnp.zeros((1, width), jnp.float32)
+    )
+    dots_box[0] = jnp.broadcast_to(funnel_dots, dots_box.shape[1:])
+    dots_copy.start()
+    loads[2].wait()
+    line_up = lax.broadcasted_iota(jnp.int32, (SEQ, SEQ), 0)
+    line_on = lax.broadcasted_iota(jnp.int32, (SEQ, SEQ), 1)
+
+    def attend(block, carry):
+        for part in range(count):
+            place = rows_of(part)
+            allowed = ((line_up >= line_on) & (keep_ref[part] > 0)) | (line_up == line_on)
+            for half in range(halves):
+                lanes = slice(half * HEAD_DIM, (half + 1) * HEAD_DIM)
+                scores = dot_nt(
+                    turned[block, place, lanes], turned[near + block, place, lanes]
+                ) * scale
+                masked = jnp.where(allowed, scores, MASKED)
+                top = jnp.max(masked, axis=1, keepdims=True)
+                weight = jnp.exp(masked - top)
+                attention[part, halves * block + half] = weight / jnp.sum(
+                    weight, axis=1, keepdims=True
+                )
+        return carry
+
+    lax.fori_loop(0, near, attend, 0)
+    for copy in part_copies[1:]:
+        copy.start()
+
+    def funnel_load(block, slot):
+        return pltpu.make_async_copy(
+            full.at[4 * near + BLOCKS * block + 2], funnel_weight.at[slot], funnel_sems.at[slot]
+        )
+
+    funnel_load(0, 0).start()
+    for load in loads[3:] + weight_loads:
+        load.wait()
+    head_seen = [
+        dot_nn(entry_down_ref[pl.ds(RANK * i, RANK)], weight_of(i)) for i in range(3)
+    ]
+    mixer_seen = dot_nt(mixer_down_ref[...], weight_of(3))
+    reduced = dot_nt(entry_down_ref[...], normed[...]).astype(jnp.bfloat16)
+    dots_copy.wait()
+    funnel_dots = dots_box[0, 0:1] + dots_box[1, 0:1]
+    funnel_pull = (pull_output_ref[1] * funnel_dots).astype(jnp.bfloat16)
+
+    def correct(block, carry):
+        slot = lax.rem(block, 2)
+
+        @pl.when(block < wide // CHUNK - 1)
+        def _():
+            funnel_load(block + 1, 1 - slot).start()
+
+        funnel_load(block, slot).wait()
+        columns = pl.ds(pl.multiple_of(block * CHUNK, CHUNK), CHUNK)
+        funnel_down_out[:, columns] = funnel_down_ref[:, columns] - ADAPTER_SCALE * dot_nn(
+            funnel_pull, funnel_weight[slot].reshape(width, CHUNK)
+        )
+        return carry
+
+    lax.fori_loop(0, wide // CHUNK, correct, 0)
+    funnel_up_out[...] = ADAPTER_SCALE * (
+        funnel_up_ref[...] * output_ratio_ref[1:2]
+        - funnel_seen_ref[...] * (output_pull_ref[1:2] * funnel_dots)
+    )
+    mixer_dots[...] = jnp.zeros_like(mixer_dots)
+    small = 32
+    for part in range(count):
+        part_copies[part].wait()
+        if part == count - 1:
+            funneled_copy.start()
+
+        def pull_back(index, carry, part=part):
+            place = pl.ds(pl.multiple_of(part * SEQ + index * small, small), small)
+            value = residual[place]
+            weighted = gain_ref[...] * (
+                own[place].astype(jnp.float32) + inbox[place].astype(jnp.float32)
+            )
+            root = lax.rsqrt(jnp.mean(value * value, axis=1, keepdims=True) + NORM_EPS)
+            along = jnp.mean(value * weighted, axis=1, keepdims=True)
+            gradient = back[place].astype(jnp.float32) + (
+                root * weighted - value * (root * root * root * along)
+            )
+            rounded = gradient.astype(jnp.bfloat16)
+            d_low[place] = rounded
+            attended = value - floats[place].astype(jnp.float32)
+            mixer_dots[...] += jnp.sum(
+                (rounded.astype(jnp.float32) * attended).reshape(small // 8, 8, width), axis=0
+            )
+            residual[place] = gradient
+            return carry
+
+        lax.fori_loop(0, SEQ // small, pull_back, 0)
+        place = rows_of(part)
+
+        def attend_back(block, carry, part=part, place=place):
+            columns = pl.ds(pl.multiple_of(block * CHUNK, CHUNK), CHUNK)
+            mixer = weights[3, :, :, :, :, columns].reshape(width, CHUNK)
+            d_mixed = dot_nn(d_low[place], mixer).astype(jnp.bfloat16)
+            for half in range(halves):
+                lanes = slice(half * HEAD_DIM, (half + 1) * HEAD_DIM)
+                spot = pl.ds(
+                    pl.multiple_of(block * CHUNK + half * HEAD_DIM, HEAD_DIM), HEAD_DIM
+                )
+                weight = attention[part, halves * block + half]
+                d_head = d_mixed[:, lanes]
+                d_attention = dot_nt(d_head, turned[2 * near + block, place, lanes])
+                d_heads[2, place, spot] = dot_nn(
+                    weight.astype(jnp.bfloat16).T, d_head
+                ).astype(jnp.bfloat16)
+                inner = jnp.sum(weight * d_attention, axis=1, keepdims=True)
+                d_scores = (weight * (d_attention - inner)).astype(jnp.bfloat16)
+                d_query = dot_nn(d_scores, turned[near + block, place, lanes]) * scale
+                d_key = dot_nn(d_scores.T, turned[block, place, lanes]) * scale
+                for i, value in ((0, d_query), (1, d_key)):
+                    d_heads[i, place, spot] = (
+                        value * cosine_ref[place]
+                        - pltpu.roll(value, HEAD_DIM // 2, 1) * sine_ref[place]
+                    ).astype(jnp.bfloat16)
+            return carry
+
+        lax.fori_loop(0, near, attend_back, 0)
+    d_residual_copy = pltpu.make_async_copy(residual, d_residual_out, out_sems.at[0])
+    d_residual_copy.start()
+    per = 512 // (4 * weights.shape[4])
+    for i in range(3):
+        dots = []
+        for block in range(near):
+            lanes = slice(block * CHUNK, (block + 1) * CHUNK)
+            source = plain if i < 2 else turned
+            dots.append(
+                jnp.sum(
+                    d_heads[i, :tokens, lanes].astype(jnp.float32)
+                    * source[near * i + block].astype(jnp.float32),
+                    axis=0,
+                    keepdims=True,
+                )
+            )
+        dots = jnp.concatenate(dots, axis=1)
+        dots_out[4 + i : 5 + i] = dots
+        pulled = (pull_lift_ref[i] * dots).astype(jnp.bfloat16)
+        up_out[i] = ADAPTER_SCALE * (
+            dot_nn(reduced[RANK * i : RANK * (i + 1)], d_heads[i, :tokens]) * ratio_ref[i : i + 1]
+            - head_seen[i] * (pull_ref[i : i + 1] * dots)
+        )
+        lowered = dot_nt(low_lift_ref[i], d_heads[i, :tokens]).astype(jnp.bfloat16)
+        down_out[pl.ds(RANK * i, RANK)] = ADAPTER_SCALE * dot_nn(lowered, normed[...])
+        d_heads[i, tokens:] = pulled
+    for piece in range(width // 512):
+        lanes = slice(piece * 512, (piece + 1) * 512)
+        results = [
+            dot_nt(d_heads[i], weights[i, pl.ds(piece * per, per)].reshape(512, cut))
+            for i in range(3)
+        ]
+        own[:, lanes] = (
+            results[0][:tokens] + results[1][:tokens] + results[2][:tokens]
+        ).astype(jnp.bfloat16)
+        for i in range(3):
+            down_out[pl.ds(RANK * i, RANK), lanes] -= ADAPTER_SCALE * results[i][tokens:]
+    partial_copy = pltpu.make_async_copy(own, partial_out, out_sems.at[1])
+    partial_copy.start()
+    mixer_total = jnp.sum(mixer_dots[...], axis=0, keepdims=True)
+    joined = jnp.concatenate([mixed[b] for b in range(near)], axis=1)
+    lowered = dot_nt(low_output_ref[...], d_low[...]).astype(jnp.bfloat16)
+    pulled = (pull_output_ref[0] * mixer_total).astype(jnp.bfloat16)
+    mixer_down_out[...] = ADAPTER_SCALE * (
+        dot_nn(lowered, joined) - dot_nn(pulled, weight_of(3))
+    )
+    reduced_mixed = dot_nt(mixer_down_ref[...], joined).astype(jnp.bfloat16)
+    mixer_up_out[...] = ADAPTER_SCALE * (
+        dot_nn(reduced_mixed, d_low[...]) * output_ratio_ref[0:1]
+        - mixer_seen * (output_pull_ref[0:1] * mixer_total)
+    )
+    for i, value in enumerate((mixer_total, funnel_dots)):
+        for r in range(2):
+            dots_out[2 * i + r : 2 * i + r + 1] = value[:, r * LANES : (r + 1) * LANES]
+    row = 7
+    for i in range(2):
+        for start in range(0, wide, LANES):
+            size = min(LANES, wide - start)
+            dots_out[row : row + 1, pl.ds(0, size)] = feed_dots_ref[
+                i : i + 1, pl.ds(start, size)
+            ]
+            if size < LANES:
+                dots_out[row : row + 1, pl.ds(size, LANES - size)] = jnp.zeros(
+                    (1, LANES - size), jnp.float32
+                )
+            row += 1
+    if row < dots_out.shape[0]:
+        dots_out[row:] = jnp.zeros((dots_out.shape[0] - row, LANES), jnp.float32)
+    d_residual_copy.wait()
+    partial_copy.wait()
+    funneled_copy.wait()
+
+
+def run_tail(big, small, lines):
+    full, turned, plain, mixed, residual = big[:5]
+    tokens, width = residual.shape
+    line, height = full.shape[1], full.shape[4]
+    near = mixed.shape[0]
+    cut = near * CHUNK
+    wide = small[14].shape[1]
+    count = tokens // SEQ
+    anywhere = pl.BlockSpec(memory_space=pl.ANY)
+    local = pl.BlockSpec(memory_space=pltpu.VMEM)
+    low, full_type = jnp.bfloat16, jnp.float32
+    heads = cut // HEAD_DIM
+    return pl.pallas_call(
+        tail_kernel,
+        name="tail",
+        out_shape=(
+            jax.ShapeDtypeStruct((tokens, width), low),
+            jax.ShapeDtypeStruct((tokens, width), full_type),
+            jax.ShapeDtypeStruct((tokens, width), low),
+            jax.ShapeDtypeStruct((3 * RANK, width), full_type),
+            jax.ShapeDtypeStruct((3, RANK, cut), full_type),
+            jax.ShapeDtypeStruct((RANK, cut), full_type),
+            jax.ShapeDtypeStruct((RANK, width), full_type),
+            jax.ShapeDtypeStruct((RANK, wide), full_type),
+            jax.ShapeDtypeStruct((RANK, width), full_type),
+            jax.ShapeDtypeStruct((lines, LANES), full_type),
+        ),
+        in_specs=[anywhere] * 10 + [local] * 18,
+        out_specs=[anywhere] * 3 + [local] * 7,
+        scratch_shapes=[
+            pltpu.VMEM((4, line, 2, 2, height, cut), low),
+            pltpu.VMEM((tokens, width), full_type),
+            pltpu.VMEM((tokens, width), low),
+            pltpu.VMEM((tokens, width), low),
+            pltpu.VMEM((tokens, width), low),
+            pltpu.VMEM(turned.shape, low),
+            pltpu.VMEM(plain.shape, low),
+            pltpu.VMEM(mixed.shape, low),
+            pltpu.VMEM((tokens, width), low),
+            pltpu.VMEM((tokens, width), low),
+            pltpu.VMEM((tokens, width), low),
+            pltpu.VMEM((count, heads, SEQ, SEQ), full_type),
+            pltpu.VMEM((tokens, width), low),
+            pltpu.VMEM((3, tokens + RANK, cut), low),
+            pltpu.VMEM((2, line, 2, 2, height, CHUNK), low),
+            pltpu.VMEM((2, 8, width), full_type),
+            pltpu.VMEM((8, width), full_type),
+            pltpu.SemaphoreType.DMA((9,)),
+            pltpu.SemaphoreType.DMA((4 * near,)),
+            pltpu.SemaphoreType.DMA((2,)),
+            pltpu.SemaphoreType.DMA((count + 2,)),
+            pltpu.SemaphoreType.DMA((count + 2,)),
+            pltpu.SemaphoreType.DMA((2,)),
+        ],
+        compiler_params=pltpu.CompilerParams(
+            collective_id=2, has_side_effects=True, vmem_limit_bytes=62 * 1024 * 1024
+        ),
+    )(*big, *small)
+
+
+def place_in(target, base, offset, value):
+    width = target.shape[1]
+    start = 0
+    while start < value.shape[1]:
+        group, lane = divmod(offset + start, width)
+        size = min(value.shape[1] - start, width - lane)
+        target[pl.ds(base + RANK * group, RANK), pl.ds(lane, size)] = value[
+            :, start : start + size
+        ].astype(target.dtype)
+        start += size
+
+
+def take_from(source, base, offset, size):
+    width = source.shape[1]
+    pieces = []
+    start = 0
+    while start < size:
+        group, lane = divmod(offset + start, width)
+        count = min(size - start, width - lane)
+        pieces.append(
+            source[pl.ds(base + RANK * group, RANK), pl.ds(lane, count)].astype(jnp.float32)
+        )
+        start += count
+    return pieces[0] if len(pieces) == 1 else jnp.concatenate(pieces, axis=1)
+
+
+def sum_kernel(
+    size,
+    sides,
+    widths,
+    down_ref,
+    feed_down_ref,
+    mixer_up_ref,
+    funnel_up_ref,
+    up_ref,
+    feed_up_ref,
+    mixer_down_ref,
+    funnel_down_ref,
+    dots_ref,
+    magnitude_ref,
+    total,
+    norm_out,
+    gathered,
+    side_box,
+    norm_box,
+    *rest,
+):
+    bits = len(widths)
+    outboxes, inboxes = rest[:bits], rest[bits : 2 * bits]
+    sends, receives = rest[2 * bits :]
+    half = gathered.shape[0] // 2
+    me = lax.axis_index("dp")
+    side = lax.axis_index("tensor")
+    partners = partners_of(size)
+    greet_sum(size, sides)
+
+    def remote(source, target, index, where):
+        return pltpu.make_async_remote_copy(
+            src_ref=source,
+            dst_ref=target,
+            send_sem=sends.at[index],
+            recv_sem=receives.at[index],
+            device_id=where,
+            device_id_type=MESH,
+        )
+
+    row = 0
+    for ref in (down_ref, feed_down_ref, mixer_up_ref, funnel_up_ref):
+        gathered[pl.ds(row, ref.shape[0])] = ref[...]
+        row += ref.shape[0]
+    offset = 0
+    split = [up_ref[i] for i in range(3)] + [feed_up_ref[i] for i in range(2)]
+    split += [mixer_down_ref[...], funnel_down_ref[...], dots_ref[...]]
+    for value in split:
+        place_in(gathered, half, offset, value)
+        offset += value.shape[1]
+    rest_columns = half // RANK * gathered.shape[1] - offset
+    place_in(gathered, half, offset, jnp.zeros((RANK, rest_columns), jnp.float32))
+
+    start = 0
+    width = gathered.shape[1]
+    marks = []
+    for step in range(bits):
+        bit = lax.rem(lax.div(me, 2**step), 2)
+        where = {"dp": partners[step]}
+        if widths[step] < width:
+            width = widths[step]
+            marks.append((step, bit, width))
+            mine = pl.ds(pl.multiple_of(start + bit * width, 128), width)
+            theirs = pl.ds(pl.multiple_of(start + (1 - bit) * width, 128), width)
+            outboxes[step][...] = gathered[:, theirs].astype(jnp.bfloat16)
+            copy = remote(outboxes[step], inboxes[step], step, where)
+            copy.start()
+            copy.wait()
+            gathered[:, mine] += inboxes[step][...].astype(jnp.float32)
+            start = start + bit * width
+        else:
+            mine = pl.ds(pl.multiple_of(start, 128), width)
+            outboxes[step][...] = gathered[:, mine].astype(jnp.bfloat16)
+            copy = remote(outboxes[step], inboxes[step], step, where)
+            copy.start()
+            copy.wait()
+            gathered[:, mine] = outboxes[step][...].astype(jnp.float32) + inboxes[step][
+                ...
+            ].astype(jnp.float32)
+    mine = pl.ds(pl.multiple_of(start, 128), width)
+    side_box[0] = gathered[pl.ds(0, half), mine].astype(jnp.bfloat16)
+    shared = side_box[0].astype(jnp.float32)
+    for step in range(1, sides):
+        copy = remote(
+            side_box.at[0],
+            side_box.at[step],
+            bits + step - 1,
+            {"tensor": lax.rem(side + step, sides)},
+        )
+        copy.start()
+        copy.wait()
+        shared += side_box[step].astype(jnp.float32)
+    total[pl.ds(0, half), mine] = shared.astype(jnp.bfloat16)
+    total[pl.ds(half, half), mine] = gathered[pl.ds(half, half), mine].astype(jnp.bfloat16)
+    index = bits + sides - 1
+    for step, bit, width in reversed(marks):
+        mine = pl.ds(pl.multiple_of(start, 128), width)
+        copy = remote(
+            total.at[:, mine], total.at[:, mine], index, {"dp": partners[step]}
+        )
+        copy.start()
+        copy.wait()
+        index += 1
+        start = start - bit * width
+    squares = jnp.zeros((RANK, 1), jnp.float32)
+    for row in range(0, half, RANK):
+        value = total[pl.ds(row, RANK)].astype(jnp.float32)
+        squares += jnp.sum(value * value, axis=1, keepdims=True)
+    lines = dots_ref.shape[1]
+    dots_offset = offset - lines
+    dots = take_from(total, half, dots_offset, lines) / magnitude_ref[...]
+    dots = jnp.sum(dots * dots, axis=1, keepdims=True)
+    shared_total = jnp.sum(squares) + jnp.sum(dots[:4])
+    split_squares = jnp.zeros((RANK, 1), jnp.float32)
+    start = 0
+    while start < dots_offset:
+        count = min(dots_offset - start, gathered.shape[1])
+        value = take_from(total, half, start, count)
+        split_squares += jnp.sum(value * value, axis=1, keepdims=True)
+        start += count
+    split_total = jnp.sum(split_squares) + jnp.sum(dots[4:])
+    norm_box[0] = jnp.full(norm_box.shape[1:], split_total, jnp.float32)
+    for step in range(1, sides):
+        copy = remote(
+            norm_box.at[0],
+            norm_box.at[step],
+            index + step - 1,
+            {"tensor": lax.rem(side + step, sides)},
+        )
+        copy.start()
+        copy.wait()
+    split_sum = norm_box[0]
+    for step in range(1, sides):
+        split_sum = split_sum + norm_box[step]
+    norm_out[...] = jnp.sqrt(split_sum + shared_total)
+
+
+def sum_all(parts, magnitudes):
+    size = lax.axis_size("dp")
+    sides = lax.axis_size("tensor")
+    width = parts[0].shape[1]
+    rows = sum(part.shape[0] for part in parts[:4])
+    bits = len(bin(size)) - 3
+    widths = [max(width >> (step + 1), 128) for step in range(bits)]
+    halvings = sum(1 for step in range(bits) if width >> (step + 1) >= 128)
+    boxes = [pltpu.VMEM((2 * rows, w), jnp.bfloat16) for w in widths]
+    copies = bits + halvings + 2 * (sides - 1)
+    return pl.pallas_call(
+        functools.partial(sum_kernel, size, sides, widths),
+        name="sum",
+        out_shape=(
+            jax.ShapeDtypeStruct((2 * rows, width), jnp.bfloat16),
+            jax.ShapeDtypeStruct((8, 128), jnp.float32),
+        ),
+        in_specs=[pl.BlockSpec(memory_space=pltpu.VMEM)] * 10,
+        out_specs=[pl.BlockSpec(memory_space=pltpu.VMEM)] * 2,
+        scratch_shapes=[
+            pltpu.VMEM((2 * rows, width), jnp.float32),
+            pltpu.VMEM((sides, rows, widths[-1]), jnp.bfloat16),
+            pltpu.VMEM((sides, 8, 128), jnp.float32),
+            *boxes,
+            *boxes,
+            pltpu.SemaphoreType.DMA((copies,)),
+            pltpu.SemaphoreType.DMA((copies,)),
+        ],
+        compiler_params=pltpu.CompilerParams(
+            collective_id=3, has_side_effects=True, vmem_limit_bytes=32 * 1024 * 1024
+        ),
+    )(*parts, magnitudes)
+
+
+def update_kernel(*refs):
+    total, norm_ref = refs[:2]
+    values, firsts, seconds = refs[2:11], refs[11:20], refs[20:29]
+    fresh, momenta, variances = refs[29:38], refs[38:47], refs[47:56]
+    factor = jnp.minimum(1.0, CLIP / (norm_ref[0:1, 0:1] + 1e-06))
+    half = total.shape[0] // 2
+    cut, wide = values[1].shape[2], values[2].shape[2]
+
+    def update(index, rate, piece, gradient):
+        value, momentum, variance = decoupled_update(
+            values[index][piece], gradient * factor, firsts[index][piece], seconds[index][piece], rate
+        )
+        fresh[index][piece] = value
+        momenta[index][piece] = momentum
+        variances[index][piece] = variance
+
+    def shared(group):
+        return total[pl.ds(RANK * group, RANK)].astype(jnp.float32)
+
+    for i in range(5):
+        update(0, RATE_FACTOR, i, shared(i))
+    for i in range(2):
+        update(5, RATE_LIFT, i, shared(5 + i))
+    offset = 0
+    for i in range(3):
+        update(1, RATE_LIFT, i, take_from(total, half, offset, cut))
+        offset += cut
+    for i in range(2):
+        update(2, RATE_LIFT, i, take_from(total, half, offset, wide))
+        offset += wide
+    update(3, RATE_FACTOR, Ellipsis, take_from(total, half, offset, cut))
+    offset += cut
+    update(4, RATE_FACTOR, Ellipsis, take_from(total, half, offset, wide))
+    offset += wide
+    dots = take_from(total, half, offset, LANES)
+
+    def long(row, size):
+        count = -(-size // LANES)
+        return jnp.concatenate([dots[row + r : row + r + 1] for r in range(count)], axis=1)[
+            :, :size
+        ]
+
+    width = total.shape[1]
+    for i in range(2):
+        piece = slice(i, i + 1)
+        update(8, RATE_LOUD, piece, long(2 * i, width) / values[8][piece])
+    for i in range(3):
+        piece = slice(i, i + 1)
+        update(6, RATE_SCALE, piece, long(4 + i, cut) / values[6][piece])
+    lines = -(-wide // LANES)
+    for i in range(2):
+        piece = slice(i, i + 1)
+        update(7, RATE_SCALE, piece, long(7 + lines * i, wide) / values[7][piece])
+
+
+def update_all(total, norm, params, firsts, seconds):
+    shapes = tuple(jax.ShapeDtypeStruct(p.shape, p.dtype) for p in params)
+    return pl.pallas_call(
+        update_kernel,
+        name="update",
+        out_shape=shapes * 3,
+        in_specs=[pl.BlockSpec(memory_space=pltpu.VMEM)] * 29,
+        out_specs=[pl.BlockSpec(memory_space=pltpu.VMEM)] * 27,
+        compiler_params=pltpu.CompilerParams(vmem_limit_bytes=48 * 1024 * 1024),
+    )(total, norm, *params, *firsts, *seconds)
+
+
 def body(
     activations,
     cotangent,
@@ -1017,155 +1678,82 @@
     ) = run_block(
         shard, normed_one, activations, cotangent, cosine, sine, keep, norm_gains[1:2], small
     )
-    blocks = full.shape[0]
-    near = cut // CHUNK
-    heads = CHUNK // HEAD_DIM
-    scale = HEAD_DIM ** (-0.5)
-    full = full.reshape(blocks, width, CHUNK)
-    d_normed_two = swap(d_normed_two)
-    funneled = swap(funneled)
-    attended = residual - floats
-    block_output = low(residual + funneled)
-    back = cotangent.astype(jnp.float32)
-    unused, second_pull = jax.vjp(lambda v: root_norm(v, norm_gains[1]), residual)
-    d_residual = back + second_pull(d_normed_two)[0]
-    d_residual_low = low(d_residual)
-    d_mixed = low(
-        jnp.einsum(
-            "td,gdc->gtc", d_residual_low, full[3 * near : 4 * near], preferred_element_type=jnp.float32
-        )
-    )
-    split = (near, count, SEQ, heads, HEAD_DIM)
-    d_mixed = d_mixed.reshape(split)
-    turned_queries, turned_keys, values_low = (
-        turned[i * near : (i + 1) * near].reshape(split) for i in range(3)
-    )
-    allowed = allowed_of(padding_mask, count)[None]
-
-    def product(equation, left, right):
-        return jnp.einsum(equation, left, right, preferred_element_type=jnp.float32)
-
-    scores = product("gbqhd,gbkhd->gbhqk", turned_queries, turned_keys) * scale
-    masked = jnp.where(allowed, scores, MASKED)
-    top = jnp.max(masked, axis=-1, keepdims=True)
-    log_total = top + jnp.log(jnp.sum(jnp.exp(masked - top), axis=-1, keepdims=True))
-    attention = jnp.exp(masked - log_total)
-    attention_low = low(attention)
-    d_attention = product("gbqhd,gbkhd->gbhqk", d_mixed, values_low)
-    d_values = low(product("gbhqk,gbqhd->gbkhd", attention_low, d_mixed))
-    d_scores = attention * (d_attention - jnp.sum(attention * d_attention, axis=-1, keepdims=True))
-    d_scores = low(d_scores)
-    flat = (near, activations.shape[0], heads, HEAD_DIM)
-    d_turned_queries = product("gbhqk,gbkhd->gbqhd", d_scores, turned_keys).reshape(flat) * scale
-    d_turned_keys = product("gbhqk,gbqhd->gbkhd", d_scores, turned_queries).reshape(flat) * scale
-
-    def turn_back(values):
-        swapped = jnp.concatenate([values[..., HEAD_DIM // 2 :], values[..., : HEAD_DIM // 2]], -1)
-        return low(values * cosine[None, :, None] - swapped * sine[None, :, None])
-
-    d_heads = jnp.concatenate(
-        [
-            turn_back(d_turned_queries).reshape(near, -1, CHUNK),
-            turn_back(d_turned_keys).reshape(near, -1, CHUNK),
-            d_values.reshape(near, -1, CHUNK),
+    head_pull = 1.0 / (split_norms[: 3 * cut] * split_magnitudes[: 3 * cut]).reshape(3, cut)
+    head_ratio = split_ratio[: 3 * cut].reshape(3, cut)
+    shared_pull = 1.0 / (shared_norms * loudness_value)
+    small = (
+        cosine,
+        sine,
+        keep,
+        norm_gains[1:2],
+        entry_down[:3].reshape(3 * RANK, width),
+        low(attend_value * head_ratio[:, None]),
+        attend_value * head_pull[:, None],
+        head_ratio,
+        head_pull,
+        low(mixer_value.T),
+        low(output_value[0] * shared_ratio[0]),
+        output_value * shared_pull[:, None],
+        shared_ratio,
+        shared_pull,
+        funnel_down,
+        funnel_up,
+        funnel_seen,
+        feed_dots,
+    )
+    big = (
+        full,
+        turned,
+        plain,
+        mixed,
+        residual,
+        d_normed_two,
+        funneled,
+        cotangent,
+        activations,
+        normed_one,
+    )
+    (
+        partial,
+        d_residual,
+        funneled_other,
+        head_downs,
+        head_ups,
+        mixer_down,
+        mixer_up,
+        funnel_down,
+        funnel_up,
+        dots,
+    ) = run_tail(big, small, squares.shape[0])
+    d_normed_one = swap(partial)
+    total, norm = sum_all(
+        (
+            head_downs,
+            feed_downs,
+            mixer_up,
+            funnel_up,
+            head_ups,
+            feed_ups,
+            mixer_down,
+            funnel_down,
+            dots,
+        ),
+        magnitudes,
+    )
+
+    def turned_over(items):
+        return [
+            jnp.swapaxes(item, -1, -2) if i in (0, 3, 4) else item for i, item in enumerate(items)
         ]
-    )
-    d_normed_one = swap(product("gtc,gdc->td", d_heads, full[: 3 * near]))
+
+    results = update_all(total, norm, turned_over(params), turned_over(firsts), turned_over(seconds))
+    updated, momenta, variances = (turned_over(results[i : i + 9]) for i in (0, 9, 18))
+    gradient_norm = norm[0, 0]
+    block_output = low(
+        residual + (funneled.astype(jnp.float32) + funneled_other.astype(jnp.float32))
+    )
     unused, first_pull = jax.vjp(lambda v: root_norm(v, norm_gains[0]), floats)
     input_gradient = d_residual + first_pull(d_normed_one)[0]
-
-    heads_plain = jnp.concatenate([plain, turned[2 * near :]]).astype(jnp.float32)
-    head_dots = jnp.sum(d_heads.astype(jnp.float32) * heads_plain, axis=1).reshape(-1)
-    split_dots = jnp.concatenate([head_dots, feed_dots.reshape(-1)])
-    shared_dots = jnp.stack(
-        [
-            jnp.sum(d_residual_low.astype(jnp.float32) * attended, axis=0),
-            jnp.sum(back * funneled, axis=0),
-        ]
-    )
-    shared_pull = shared_dots / (shared_norms * loudness_value)
-    head_pull = split_dots[: 3 * cut] / (split_norms[: 3 * cut] * split_magnitudes[: 3 * cut])
-    down_gradients = []
-    up_gradients = []
-    for i in range(3):
-        ratio = split_ratio[i * cut : (i + 1) * cut]
-        pull = head_pull[i * cut : (i + 1) * cut]
-        part = slice(i * near, (i + 1) * near)
-        low_lift = low(attend_value[i] * ratio).reshape(RANK, near, CHUNK)
-        pull_lift = low(attend_value[i] * pull).reshape(RANK, near, CHUNK)
-        lowered = low(product("rgc,gtc->rt", low_lift, d_heads[part]))
-        down_gradients.append(
-            ADAPTER_SCALE
-            * (matmul(lowered, normed_one) - product("rgc,gdc->rd", pull_lift, full[part]))
-        )
-        reduced = low(matmul_nt(entry_down[i], normed_one))
-        main = product("rt,gtc->rgc", reduced, d_heads[part]).reshape(RANK, cut)
-        seen = product("rd,gdc->rgc", entry_down[i], full[part]).reshape(RANK, cut)
-        up_gradients.append(ADAPTER_SCALE * (main * ratio - seen * pull))
-    down_gradients += [feed_downs[:RANK], feed_downs[RANK:]]
-    up_gradients += [feed_ups[0], feed_ups[1]]
-    low_lift = low(output_value[0] * shared_ratio[0])
-    pull_lift = low(output_value[0] * shared_pull[0])
-    lowered = low(matmul_nt(low_lift, d_residual_low))
-    mixer_weight = full[3 * near : 4 * near]
-    mixer_down = ADAPTER_SCALE * (
-        product("rt,gtc->rgc", lowered, mixed) - product("rd,gdc->rgc", pull_lift, mixer_weight)
-    ).reshape(RANK, cut)
-    low_down = low(mixer_value.T).reshape(RANK, near, CHUNK)
-    reduced = low(product("rgc,gtc->rt", low_down, mixed))
-    mixer_up = ADAPTER_SCALE * (
-        matmul(reduced, d_residual_low) * shared_ratio[0]
-        - product("rgc,gdc->rd", low_down, mixer_weight) * shared_pull[0]
-    )
-    pull_lift = low(output_value[1] * shared_pull[1])
-    funnel_weight = full[4 * near :].reshape(-1, BLOCKS, width, CHUNK)[:, 2]
-    funnel_down = funnel_down - ADAPTER_SCALE * product(
-        "rd,gdc->rgc", pull_lift, funnel_weight
-    ).reshape(RANK, wide)
-    funnel_up = ADAPTER_SCALE * (funnel_up * shared_ratio[1] - funnel_seen * shared_pull[1])
-    shared_terms = jnp.concatenate(down_gradients + [mixer_up, funnel_up], axis=1)
-    split_terms = jnp.concatenate(up_gradients + [mixer_down, funnel_down], axis=1)
-    shared_terms, split_terms, split_dots, shared_dots = lax.psum(
-        (shared_terms, split_terms, split_dots, shared_dots), "dp"
-    )
-    split_scale = split_dots / split_magnitudes
-    shared_scale = shared_dots / loudness_value
-    split_total = jnp.sum(split_terms * split_terms) + jnp.sum(split_scale * split_scale)
-    shared_terms, split_total = lax.psum((shared_terms, split_total), "tensor")
-    totals = (
-        jnp.stack([shared_terms[:, i * width : (i + 1) * width].T for i in range(5)]),
-        jnp.stack([split_terms[:, i * cut : (i + 1) * cut] for i in range(3)]),
-        jnp.stack([split_terms[:, 3 * cut + i * wide : 3 * cut + (i + 1) * wide] for i in range(2)]),
-        split_terms[:, split_wide : split_wide + cut].T,
-        split_terms[:, split_wide + cut :].T,
-        jnp.stack([shared_terms[:, (5 + i) * width : (6 + i) * width] for i in range(2)]),
-        split_scale[: 3 * cut].reshape(3, cut),
-        split_scale[3 * cut :].reshape(2, wide),
-        shared_scale,
-    )
-    gradient_norm = jnp.sqrt(split_total + squares_of((totals[0], totals[5], totals[8])))
-    down_factor = jnp.minimum(1.0, CLIP / (gradient_norm + 1e-06))
-    rates = (
-        RATE_FACTOR,
-        RATE_LIFT,
-        RATE_LIFT,
-        RATE_FACTOR,
-        RATE_FACTOR,
-        RATE_LIFT,
-        RATE_SCALE,
-        RATE_SCALE,
-        RATE_LOUD,
-    )
-    updated = []
-    momenta = []
-    variances = []
-    for value, gradient, first, second, rate in zip(params, totals, firsts, seconds, rates):
-        fresh, momentum, variance = decoupled_update(
-            value, gradient * down_factor, first, second, rate
-        )
-        updated.append(fresh)
-        momenta.append(momentum)
-        variances.append(variance)
     return (
         block_output,
         input_gradient,

time: 893 us -> 584 us (0.65)
  Pallas kernels: 346 us -> 500 us
  local copies, waits for them, and re-layouts: 184 us -> 46.1 us
  waiting for transfers between devices: 120 us -> 0.01 us
  matrix products: 78.7 us -> 0 us
  blocking collectives: 63.9 us -> 0 us
  other arithmetic: 64 us -> 25.4 us
  between operations: 20.9 us -> 1.49 us
    pallas_call x0 -> x3, Pallas kernels: none -> 153 us  [the longest x1 94 us: run_tail(): pl.pallas_call(tail_kernel, name='tail', out_shape=(jax.ShapeDtypeStruct(...]
    psum x2 -> x0, waiting for transfers between devices: 120 us -> none  [the longest x1 91.3 us: body(): lax.psum((shared_terms, split_terms, split_dots, shared_dots), 'dp')]
    dot_general x24 -> x0, matrix products: 78.7 us -> none  [the longest x19 66.6 us: product(): return jnp.einsum(equation, left, right, preferred_element_type=jnp.float32)]
    slice x16 -> x4, local copies, waits for them, and re-layouts: 73.1 us -> 1.22 us  [the longest x1 0.69 us: body(): entry_down[:3].reshape(3 * RANK, width)]
    psum x2 -> x0, blocking collectives: 63.9 us -> none  [the longest x1 58.3 us: body(): lax.psum((shared_terms, split_terms, split_dots, shared_dots), 'dp')]
    reshape x14 -> x0, local copies, waits for them, and re-layouts: 24 us -> none  [the longest x5 11.5 us: body(): turned[i * near:(i + 1) * near].reshape(split)]
    reduce_sum x9 -> x1, other arithmetic: 22.7 us -> 1.09 us  [root_norm(): values * lax.rsqrt(jnp.mean(values * values, axis=-1, keepdims=True) + NO...]
    sub x9 -> x0, other arithmetic: 12.5 us -> none  [decoupled_update(): value - rate * (corrected / (spread + ADAM_EPS) + DECAY * value)]
  transfers between devices with their start and end apart: 5 -> 1, of which waited for: 2 -> 0; matrix products, arithmetic and copies ran while one was open for 26% -> 1% of each run, Pallas kernels for 0% -> 10%
where the time goes in v4:
time: 584 us; the launch traced here: 575 us
  Pallas kernels  500 us (86%)
  local copies, waits for them, and re-layouts  46.1 us (8%)
  other arithmetic  25.4 us (4%)
    pallas_call x1, Pallas kernels, run_block(): pl.pallas_call(functools.partial(block_kernel, size), name='block', out_s...  319 us
    pallas_call x1, Pallas kernels, run_tail(): pl.pallas_call(tail_kernel, name='tail', out_shape=(jax.ShapeDtypeStruct(...  94 us
    pallas_call x1, Pallas kernels, sum_all(): pl.pallas_call(functools.partial(sum_kernel, size, sides, widths), name='...  54.5 us
    unnamed x131, local copies, waits for them, and re-layouts  38.5 us
    pallas_call x1, Pallas kernels, merge(): pl.pallas_call(functools.partial(merge_kernel, size, sides), name='merge'...  27.1 us
    convert_element_type x6, other arithmetic, low(): return values.astype(jnp.bfloat16)  11.8 us
  transfers between devices with their start and end apart: 1, of which 0 were waited for; matrix products, arithmetic and copies ran while one was open for 1% of the time, Pallas kernels for 10%

profile of v4, /device:TPU:0, one launch (start us, length us, event | category | flops | bytes accessed | tf_op | source)
XLA Modules:
  0.0 574.5 jit_solution(9395498350065358115)
XLA Ops:
  1.3 1.1 bitcast_convert_fusion.2
  3.8 1.5 bitcast_convert_fusion.mixer_down_ref
  5.2 1.0 copy.79.mixer_down_ref
  6.3 1.6 bitcast_convert_fusion.1.funnel_down_ref
  7.8 1.3 copy.80.funnel_down_ref
  12.4 0.9 copy.85.entry_ref
  14.1 1.0 copy-done.5
  15.0 1.1 copy-done.7
  16.1 1.1 copy-done.8
  17.3 1.1 copy-done.9
  18.4 0.9 copy-done.19
  19.3 0.9 copy-done.20
  20.3 0.9 copy-done.21
  21.2 0.9 copy-done.22
  22.9 27.1 %merge.1 = (bf16[49,128,256]{2,1,0:T(8,128)(2,1)}, f32[16,1024]{1,0:T(8,128)S(1)}) custom-call(bf16[128,1024]{1,0:T(8,128)(2,1)S(1)} %copy-done.19, bf16[128,1024]{1,0:T(8,128)(2,1)S(1)} %copy-done.20, bf16[128,1024]{1,0:T(8,128)(2,1)S(1)} %copy-done.21, bf16[128,2816]{1,0:T(8,128)(2,1)S(1)} %copy-done.7, bf16[128,2816]{1,0:T(8,128)(2,1)S(1)} %copy-done.8, ...), custom_call_target="tpu_custom_call" | custom-call | tf_op jit(solution)/shard_map/merge/pallas_call | solution.py:258
  50.9 2.1 fusion.1
  53.6 1.4 fusion.12
  55.0 1.6 fusion.7
  58.7 0.8 pad_maximum_fusion.sine_ref
  61.7 1.9 fusion.3.normed_ref
  63.6 319.5 %block.1 = (bf16[49,4,2,2,128,256]{5,4,3,2,1,0:T(8,128)(2,1)}, bf16[12,512,256]{2,1,0:T(8,128)(2,1)}, bf16[8,512,256]{2,1,0:T(8,128)(2,1)}, bf16[4,512,256]{2,1,...) custom-call(bf16[49,128,256]{2,1,0:T(8,128)(2,1)} %get-tuple-element, ...), custom_call_target="tpu_custom_call" | custom-call | tf_op jit(solution)/shard_map/block/pallas_call | solution.py:852
  383.2 94.0 %tail.1 = (bf16[512,2048]{1,0:T(8,128)(2,1)}, f32[512,2048]{1,0:T(8,128)}, bf16[512,2048]{1,0:T(8,128)(2,1)}, f32[48,2048]{1,0:T(8,128)}, f32[3,16,1024]{2,1,0:T...) custom-call(bf16[49,4,2,2,128,256]{5,4,3,2,1,0:T(8,128)(2,1)} %get-t, ...), custom_call_target="tpu_custom_call" | custom-call | tf_op jit(solution)/shard_map/tail/pallas_call | solution.py:1214
  477.2 1.8 collective-permute-start
  479.0 1.0 copy-done.13
  480.0 1.0 copy-done.15
  481.0 0.9 copy-done.25
  482.0 0.9 copy-done.28
  482.9 0.9 copy-done.31
  483.8 0.9 copy-done.35
  484.7 0.9 copy-done.36
  485.6 0.8 copy-done.40
  486.4 0.8 copy-done.41
  487.3 54.5 %sum.1 = (bf16[224,2048]{1,0:T(8,128)(2,1)S(1)}, f32[8,128]{1,0:T(8,128)S(1)}) custom-call(f32[48,2048]{1,0:T(8,128)S(1)} %copy-done.13, f32[32,2048]{1,0:T(8,128)S(1)} %copy-done.25, f32[16,2048]{1,0:T(8,128)S(1)} %copy-done.35, f32[16,2048]{1,0:T(8,128)S(1)} %copy-done.36, f32[3,16,1024]{2,1,0:T(8,128)S(1)} %copy-done.28, f32[2,16,2816]{2,1,0:T(8,128)S(1)} %copy-done.15, ...), custom_call_target="tpu_custom_call" | custom-call | tf_op jit(solution)/shard_map/sum/pallas_call | solution.py:1435
  541.8 0.9 copy-done.6
  543.2 1.1 copy-done.10
  544.3 1.1 copy-done.11
  545.4 1.0 copy-done.16
  546.4 1.0 copy-done.17
  547.4 0.9 copy-done.23
  548.3 0.9 copy-done.24
  549.3 0.9 copy-done.27
  550.2 0.9 copy-done.29
  551.1 0.9 copy-done.30
  558.8 4.7 update.1
  563.5 5.1 add_convert_fusion
  568.7 1.1 fusion.4
  569.8 1.1 copy-done.52
  570.8 3.5 fusion
  (142 shorter events, 19.4 us)
Async XLA Ops:
  0.7 9.8 %copy-start.1 = (f32[5,2048,16]{1,2,0:T(8,128)S(1)}, f32[5,2048,16]{1,2,0:T(8,128)}, u32[]{:S(2)}) copy-start(f32[5,2048,16]{1,2,0:T(8,128)} %param.51) | copy-start | bytes 1966084
  0.7 8.5 %copy-start.18 = (f32[3,1024]{1,0:T(4,128)S(1)}, f32[3,1024]{1,0:T(4,128)}, u32[]{:S(2)}) copy-start(f32[3,1024]{1,0:T(4,128)} %refs_8_.1) | copy-start | bytes 36868
  0.7 9.1 %copy-start.32 = (f32[2,2048]{1,0:T(2,128)S(1)}, f32[2,2048]{1,0:T(2,128)}, u32[]{:S(2)}) copy-start(f32[2,2048]{1,0:T(2,128)} %refs_10_.1) | copy-start | bytes 49156
  0.7 9.8 %copy-start.2 = (f32[2,16,2048]{2,1,0:T(8,128)S(1)}, f32[2,16,2048]{2,1,0:T(8,128)}, u32[]{:S(2)}) copy-start(f32[2,16,2048]{2,1,0:T(8,128)} %refs_7_.1) | copy-start | bytes 786436
  0.7 10.4 %copy-start.14 = (f32[2,2816]{1,0:T(2,128)S(1)}, f32[2,2816]{1,0:T(2,128)}, u32[]{:S(2)}) copy-start(f32[2,2816]{1,0:T(2,128)} %refs_9_.1) | copy-start | bytes 67588
  0.7 13.3 %copy-start = (f32[2,16,2816]{2,1,0:T(8,128)S(1)}, f32[2,16,2816]{2,1,0:T(8,128)}, u32[]{:S(2)}) copy-start(f32[2,16,2816]{2,1,0:T(8,128)} %refs_4_.1) | copy-start | bytes 1081348
  0.7 13.3 %copy-start.3 = (f32[3,16,1024]{2,1,0:T(8,128)S(1)}, f32[3,16,1024]{2,1,0:T(8,128)}, u32[]{:S(2)}) copy-start(f32[3,16,1024]{2,1,0:T(8,128)} %refs_3_.1) | copy-start | bytes 589828
  14.1 1.0 copy-start.5
  15.0 1.1 copy-start.7
  16.1 1.1 copy-start.8
  17.3 1.1 copy-start.9
  18.4 0.9 copy-start.19
  19.3 0.9 copy-start.20
  20.3 0.9 copy-start.21
  21.2 0.9 copy-start.22
  22.9 30.1 %copy-start.63 = (s32[512]{0:T(512)S(1)}, s32[512]{0:T(512)}, u32[]{:S(2)}) copy-start(s32[512]{0:T(512)} %param.42) | copy-start | bytes 6148
  50.0 7.8 %copy-start.33 = (f32[2,2048]{1,0:T(2,128)S(1)}, f32[2,2048]{1,0:T(2,128)}, u32[]{:S(2)}) copy-start(f32[2,2048]{1,0:T(2,128)} %refs_10_.1) | copy-start | bytes 49156
  53.0 10.6 %copy-start.61 = (f32[512]{0:T(512)}, f32[512]{0:T(512)S(1)}, u32[]{:S(2)}) copy-start(f32[512]{0:T(512)S(1)} %fusion.9) | copy-start | bytes 6148
  57.7 5.9 %copy-start.53 = (f32[2,2816]{1,0:T(2,128)}, f32[2,2816]{1,0:T(2,128)S(1)}, u32[]{:S(2)}) copy-start(f32[2,2816]{1,0:T(2,128)S(1)} %multiply_divide_fusion.pull_ref) | copy-start | bytes 67588
  57.8 325.3 %copy-start.55 = (f32[3,1024]{1,0:T(4,128)}, f32[3,1024]{1,0:T(4,128)S(1)}, u32[]{:S(2)}) copy-start(f32[3,1024]{1,0:T(4,128)S(1)} %multiply_divide_fusion.2.pull_ref) | copy-start | bytes 36868
  57.8 5.8 %copy-start.54 = (f32[2,2816]{1,0:T(2,128)}, f32[2,2816]{1,0:T(2,128)S(1)}, u32[]{:S(2)}) copy-start(f32[2,2816]{1,0:T(2,128)S(1)} %mul.164.ratio_ref) | copy-start | bytes 67588
  57.8 325.3 %copy-start.56 = (f32[3,1024]{1,0:T(4,128)}, f32[3,1024]{1,0:T(4,128)S(1)}, u32[]{:S(2)}) copy-start(f32[3,1024]{1,0:T(4,128)S(1)} %mul.173.ratio_ref) | copy-start | bytes 36868
  57.8 3.9 copy-start.48
  57.9 325.2 %copy-start.57 = (f32[2,2048]{1,0:T(2,128)}, f32[2,2048]{1,0:T(2,128)S(1)}, u32[]{:S(2)}) copy-start(f32[2,2048]{1,0:T(2,128)S(1)} %get-tuple-element.149.output_pull_ref) | copy-start | bytes 49156
  57.9 325.2 %copy-start.58 = (f32[2,2048]{1,0:T(2,128)}, f32[2,2048]{1,0:T(2,128)S(1)}, u32[]{:S(2)}) copy-start(f32[2,2048]{1,0:T(2,128)S(1)} %get-tuple-element.150.output_ratio_ref) | copy-start | bytes 49156
  383.1 160.1 %copy-start.4 = (f32[2816,16]{0,1:T(8,128)S(1)}, f32[2816,16]{0,1:T(8,128)}, u32[]{:S(2)}) copy-start(f32[2816,16]{0,1:T(8,128)} %param.55) | copy-start | bytes 540676
  383.2 160.1 %copy-start.12 = (f32[1024,16]{0,1:T(8,128)S(1)}, f32[1024,16]{0,1:T(8,128)}, u32[]{:S(2)}) copy-start(f32[1024,16]{0,1:T(8,128)} %param.54) | copy-start | bytes 196612
  383.2 160.0 %copy-start.26 = (f32[3,16,1024]{2,1,0:T(8,128)S(1)}, f32[3,16,1024]{2,1,0:T(8,128)}, u32[]{:S(2)}) copy-start(f32[3,16,1024]{2,1,0:T(8,128)} %refs_12_.1) | copy-start | bytes 589828
  477.2 91.4 %collective-permute-start = (bf16[512,2048]{1,0:T(8,128)(2,1)}, bf16[512,2048]{1,0:T(8,128)(2,1)S(1)}, u32[]{:S(2)}, u32[]{:S(2)}) collective-permute-start(bf16[512,2048]{1,0:T(8,128)(2,1)} %get-tuple-element.99), channel_id=1, source_target_pairs={{0,1},{1,0},{2,3},{3,2},{4,5},{5,4},{6,7},{7,6},{8,9},{9,8},{10,11... | collective-permute-start | bytes 6291464 | tf_op jit(solution)/shard_map/ppermute | solution.py:79
  479.0 1.0 copy-start.13
  480.0 1.0 copy-start.15
  481.0 0.9 copy-start.25
  481.9 0.9 copy-start.28
  482.9 0.9 copy-start.31
  541.8 0.9 copy-start.6
  543.2 1.1 copy-start.10
  544.3 1.1 copy-start.11
  545.4 1.0 copy-start.16
  546.4 1.0 copy-start.17
  547.4 0.9 copy-start.23
  548.3 0.9 copy-start.24
  549.3 0.9 copy-start.27
  558.8 4.7 copy-start.50
  563.5 5.1 copy-start.49
  563.5 5.1 copy-start.51
  568.6 1.1 copy-start.60
  568.6 2.2 copy-start.52
  568.6 2.2 copy-start.62
  (17 other events, 13.4 us)

commit v5 on v4

--- a/solution.py
+++ b/solution.py
@@ -34,35 +34,6 @@
     return values * lax.rsqrt(jnp.mean(values * values, axis=-1, keepdims=True) + NORM_EPS) * gain
 
 
-def rotate(values, places, sign):
-    half = values.shape[-1] // 2
-    steps = jnp.arange(half, dtype=jnp.float32)
-    frequency = ROPE_BASE ** (-2.0 * steps / values.shape[-1])
-    angles = places.astype(jnp.float32)[:, None] * frequency[None, :]
-    cosine = jnp.cos(angles)[:, None, :]
-    sine = sign * jnp.sin(angles)[:, None, :]
-    first = values[..., :half]
-    second = values[..., half:]
-    return jnp.concatenate(
-        [first * cosine - second * sine, second * cosine + first * sine], axis=-1
-    )
-
-
-def allowed_of(padding, count):
-    valid = padding.reshape(count, SEQ) > 0
-    index = jnp.arange(SEQ)
-    causal = index[:, None] >= index[None, :]
-    itself = index[:, None] == index[None, :]
-    return (causal[None] & valid[:, None, :] | itself[None])[:, None]
-
-
-def squares_of(items):
-    total = jnp.zeros((), jnp.float32)
-    for param_entry in items:
-        total = total + jnp.sum(param_entry * param_entry)
-    return total
-
-
 def decoupled_update(value, gradient, first, second, rate):
     momentum = BETA_ONE * first + (1.0 - BETA_ONE) * gradient
     variance = BETA_TWO * second + (1.0 - BETA_TWO) * gradient * gradient
@@ -71,34 +42,13 @@
     return (value - rate * (corrected / (spread + ADAM_EPS) + DECAY * value), momentum, variance)
 
 
-def swap(partial):
-    low = partial.astype(jnp.bfloat16)
-    size = lax.axis_size("tensor")
-    total = low.astype(jnp.float32)
-    for step in range(1, size):
-        other = lax.ppermute(low, "tensor", [(i, (i + step) % size) for i in range(size)])
-        total = total + other.astype(jnp.float32)
-    return total
-
-
-def matmul(left, right):
-    return jnp.dot(left, right, preferred_element_type=jnp.float32)
-
-
-def matmul_nt(left, right):
-    return jnp.einsum("ik,jk->ij", left, right, preferred_element_type=jnp.float32)
-
-
-def matmul_tn(left, right):
-    return jnp.einsum("ki,kj->ij", left, right, preferred_element_type=jnp.float32)
-
-
 def low(values):
     return values.astype(jnp.bfloat16)
 
 
 MESH = pl.DeviceIdType.MESH
 LANES = 1024
+VMEM = 62 * 1024 * 1024
 CHUNK = 256
 
 
@@ -160,9 +110,12 @@
     mixer_down_ref,
     funnel_down_ref,
     output_ref,
-    magnitude_ref,
+    stature_ref,
+    amplitude_ref,
+    loudness_ref,
     shard_out,
     squares_out,
+    magnitudes_out,
     total,
     inbox,
     direction_cut,
@@ -179,9 +132,28 @@
     total[...] = jnp.zeros_like(total)
 
     def direction(base, down, up):
-        return base.astype(jnp.float32) + ADAPTER_SCALE * jnp.dot(
-            down, up, precision=HIGH_PRECISION, preferred_element_type=jnp.float32
-        )
+        return base.astype(jnp.float32) + ADAPTER_SCALE * lax.dot_general(
+            down,
+            up,
+            (((0,), (0,)), ((), ())),
+            precision=HIGH_PRECISION,
+            preferred_element_type=jnp.float32,
+        )
+
+    magnitudes_out[...] = jnp.ones_like(magnitudes_out)
+    for i in range(2):
+        for r in range(2):
+            magnitudes_out[2 * i + r : 2 * i + r + 1, :] = loudness_ref[
+                i : i + 1, r * LANES : (r + 1) * LANES
+            ]
+    for i in range(3):
+        magnitudes_out[4 + i : 5 + i, :] = stature_ref[i : i + 1, :]
+    for i in range(2):
+        for start in range(0, wide, CHUNK):
+            row = 7 + 3 * i + start // LANES
+            magnitudes_out[row : row + 1, pl.ds(start % LANES, CHUNK)] = amplitude_ref[
+                i : i + 1, pl.ds(start, CHUNK)
+            ]
 
     group = LANES // rows
     lane_group = lax.broadcasted_iota(jnp.int32, (1, LANES), 1) // rows
@@ -192,7 +164,7 @@
         sums = jnp.zeros((1, rows), jnp.float32)
         for start in range(0, base.shape[0], CHUNK):
             piece = pl.ds(start, CHUNK)
-            part = direction(base[piece], down[piece], output_ref[i])
+            part = direction(base[piece], down[:, piece], output_ref[i])
             held[piece] = part
             sums += jnp.sum(part * part, axis=0, keepdims=True)
         spread = jnp.concatenate([sums] * group, axis=1)
@@ -216,7 +188,7 @@
             )
     double_sum(total, inbox, sends, receives, size, sides, 4)
     squares_out[...] = total[...]
-    ratio = magnitude_ref[...] / jnp.sqrt(total[...] + COLUMN_EPS)
+    ratio = magnitudes_out[...] / jnp.sqrt(total[...] + COLUMN_EPS)
     near = LANES // CHUNK
     for i in range(3):
         for b in range(near):
@@ -248,22 +220,23 @@
                 shard_out[4 * near + 3 * (start // CHUNK) + 2] = part
 
 
-def merge(bases, entry_rows, attend, widen, mixer_down, funnel_down, output_columns, magnitudes):
+def merge(bases, entry_rows, attend, widen, mixer_down, funnel_down, output_columns, scales):
     size = lax.axis_size("dp")
     sides = lax.axis_size("tensor")
     rows, cut = bases[0].shape
     wide = bases[3].shape[1]
     steps = len(bin(size)) - 3 + sides - 1
-    lines = magnitudes.shape[0]
+    lines = 16
     return pl.pallas_call(
         functools.partial(merge_kernel, size, sides),
         name="merge",
         out_shape=(
             jax.ShapeDtypeStruct(((4 * cut + 3 * wide) // CHUNK, rows, CHUNK), jnp.bfloat16),
             jax.ShapeDtypeStruct((lines, LANES), jnp.float32),
+            jax.ShapeDtypeStruct((lines, LANES), jnp.float32),
         ),
-        in_specs=[pl.BlockSpec(memory_space=pltpu.VMEM)] * 14,
-        out_specs=[pl.BlockSpec(memory_space=pltpu.VMEM)] * 2,
+        in_specs=[pl.BlockSpec(memory_space=pltpu.VMEM)] * 16,
+        out_specs=[pl.BlockSpec(memory_space=pltpu.VMEM)] * 3,
         scratch_shapes=[
             pltpu.VMEM((lines, LANES), jnp.float32),
             pltpu.VMEM((steps, lines, LANES), jnp.float32),
@@ -275,9 +248,9 @@
             pltpu.SemaphoreType.DMA((steps,)),
         ],
         compiler_params=pltpu.CompilerParams(
-            collective_id=0, has_side_effects=True, vmem_limit_bytes=48 * 1024 * 1024
+            collective_id=0, has_side_effects=True, vmem_limit_bytes=VMEM
         ),
-    )(*bases, entry_rows, attend, widen, mixer_down, funnel_down, output_columns, magnitudes)
+    )(*bases, entry_rows, attend, widen, mixer_down, funnel_down, output_columns, *scales)
 
 
 def dot_nn(left, right):
@@ -288,6 +261,11 @@
     return lax.dot_general(
         left, right, (((1,), (1,)), ((), ())), preferred_element_type=jnp.float32
     )
+
+
+def long_row(lines, row, size):
+    count = -(-size // LANES)
+    return jnp.concatenate([lines[row + r : row + r + 1] for r in range(count)], axis=1)[:, :size]
 
 
 BLOCKS = 3
@@ -454,21 +432,20 @@
 def block_kernel(
     size,
     shard,
-    normed_ref,
     rows_ref,
     back_ref,
     cosine_ref,
     sine_ref,
     keep_ref,
     gain_ref,
-    entry_down_ref,
-    funnel_down_ref,
-    low_lift_ref,
-    pull_lift_ref,
-    ratio_ref,
-    pull_ref,
-    low_output_ref,
+    entry_ref,
+    funnel_ref,
+    lift_ref,
+    output_ref,
+    squares_ref,
+    magnitudes_ref,
     full,
+    normed_out,
     turned_out,
     plain_out,
     mixed_out,
@@ -498,6 +475,11 @@
     reduced,
     funnel_lowered,
     funnel_reduced,
+    low_lift_ref,
+    pull_lift_ref,
+    ratio_ref,
+    pull_ref,
+    funnel_down_ref,
     right_sends,
     left_sends,
     right_gets,
@@ -538,9 +520,8 @@
     own = pltpu.make_async_copy(shard, full.at[:, spot, column, core], local_sems.at[0])
     own.start()
     loads = [
-        pltpu.make_async_copy(normed_ref, normed.at[pl.ds(0, tokens)], local_sems.at[1]),
+        pltpu.make_async_copy(rows_ref, floats, local_sems.at[1]),
         pltpu.make_async_copy(back_ref, back, local_sems.at[2]),
-        pltpu.make_async_copy(rows_ref, floats, local_sems.at[3]),
     ]
     for load in loads:
         load.start()
@@ -551,13 +532,48 @@
     step(0, chunks, 0, 1)
     tick(0)
     early_wait(1)
+    for load in loads:
+        load.wait()
+    tile = 32
+
+    def norm_rows(index, carry):
+        place = pl.ds(pl.multiple_of(index * tile, tile), tile)
+        value = floats[place].astype(jnp.float32)
+        root = lax.rsqrt(jnp.mean(value * value, axis=1, keepdims=True) + NORM_EPS)
+        normed[place] = (value * root * gain_ref[0:1]).astype(jnp.bfloat16)
+        return carry
+
+    def prepare():
+        lax.fori_loop(0, tokens // tile, norm_rows, 0)
+        norms = jnp.sqrt(squares_ref[...] + COLUMN_EPS)
+        ratios = magnitudes_ref[...] / norms
+        pulls = 1.0 / (norms * magnitudes_ref[...])
+        wide = funnel_down_ref.shape[1]
+        lines = -(-wide // LANES)
+        for i in range(2):
+            ratio = long_row(ratios, 7 + lines * i, wide)
+            pull = long_row(pulls, 7 + lines * i, wide)
+            ratio_ref[i : i + 1] = ratio
+            pull_ref[i : i + 1] = pull
+            low_lift_ref[i] = (lift_ref[i] * ratio).astype(jnp.bfloat16)
+            pull_lift_ref[i] = lift_ref[i] * pull
+        funnel_down_ref[...] = funnel_ref[...].astype(jnp.bfloat16)
+        low_output = (output_ref[1] * long_row(ratios, 2, width)).astype(jnp.bfloat16)
+        funnel_lowered[...] = dot_nt(low_output, back[...]).astype(jnp.bfloat16)
+        for i in range(2):
+            normed[pl.ds(tokens + RANK * i, RANK)] = entry_ref[3 + i].astype(jnp.bfloat16)
+
     for now in range(1, line + 4):
         step(now, chunks, 0, 1)
         tick(now)
+        if now == 1:
+            prepare()
+    normed_copy = pltpu.make_async_copy(
+        normed.at[pl.ds(0, tokens)], normed_out, local_sems.at[3]
+    )
+    normed_copy.start()
     ready = HEAD_CHUNKS - 2 + line + 2
     lax.fori_loop(line + 4, ready + 1, lambda now, carry: (tick(now), carry)[1], 0)
-    for load in loads:
-        load.wait()
 
     def head_load(block, slot):
         return pltpu.make_async_copy(
@@ -670,7 +686,7 @@
         side_copy(part).start()
     tick(ready + 3)
 
-    tile = 32
+    normed_copy.wait()
     for part in range(count):
         side_copy(part).wait()
 
@@ -681,7 +697,7 @@
             )
             residual[place] = value
             root = lax.rsqrt(jnp.mean(value * value, axis=1, keepdims=True) + NORM_EPS)
-            normed[place] = (value * root * gain_ref[...]).astype(jnp.bfloat16)
+            normed[place] = (value * root * gain_ref[1:2]).astype(jnp.bfloat16)
             return carry
 
         lax.fori_loop(0, SEQ // tile, add_up, 0)
@@ -689,9 +705,9 @@
             tick(ready + 4)
     outs.append(pltpu.make_async_copy(residual, residual_out, out_sems.at[3]))
     outs[-1].start()
-    normed[pl.ds(tokens, 2 * RANK)] = entry_down_ref[...]
-    reduced[...] = dot_nt(entry_down_ref[...], normed[pl.ds(0, tokens)]).astype(jnp.bfloat16)
-    funnel_lowered[...] = dot_nt(low_output_ref[...], back[...]).astype(jnp.bfloat16)
+    reduced[...] = dot_nt(normed[pl.ds(tokens, 2 * RANK)], normed[pl.ds(0, tokens)]).astype(
+        jnp.bfloat16
+    )
     d_normed[...] = jnp.zeros_like(d_normed)
     funneled[...] = jnp.zeros_like(funneled)
     lowered[...] = jnp.zeros_like(lowered)
@@ -791,20 +807,21 @@
         out.wait()
 
 
-def run_block(shard, normed_one, rows, back, cosine, sine, keep, gain, small):
+def run_block(shard, rows, back, small):
     size = lax.axis_size("dp")
     line = size // 4
     tokens, width = rows.shape
     blocks, height, _ = shard.shape
     chunks = blocks // BLOCKS
     cut_blocks = (BLOCKS * HEAD_CHUNKS + 1) // 4
-    wide = small[2].shape[2]
+    wide = small[6].shape[2]
     anywhere = pl.BlockSpec(memory_space=pl.ANY)
     local = pl.BlockSpec(memory_space=pltpu.VMEM)
     low = jnp.bfloat16
     full = jnp.float32
     out_shape = (
         jax.ShapeDtypeStruct((blocks, line, 2, 2, height, CHUNK), low),
+        jax.ShapeDtypeStruct((tokens, width), low),
         jax.ShapeDtypeStruct((3 * cut_blocks, tokens, CHUNK), low),
         jax.ShapeDtypeStruct((2 * cut_blocks, tokens, CHUNK), low),
         jax.ShapeDtypeStruct((cut_blocks, tokens, CHUNK), low),
@@ -836,6 +853,11 @@
         pltpu.VMEM((2 * RANK, tokens), low),
         pltpu.VMEM((RANK, tokens), low),
         pltpu.VMEM((RANK, tokens), full),
+        pltpu.VMEM((2, RANK, wide), low),
+        pltpu.VMEM((2, RANK, wide), full),
+        pltpu.VMEM((2, wide), full),
+        pltpu.VMEM((2, wide), full),
+        pltpu.VMEM((RANK, wide), low),
         pltpu.SemaphoreType.DMA((chunks + 1, 2 * (line - 1))),
         pltpu.SemaphoreType.DMA((chunks + 1, 2 * (line - 1))),
         pltpu.SemaphoreType.DMA((chunks + 1, 2 * (line - 1))),
@@ -853,16 +875,19 @@
         functools.partial(block_kernel, size),
         name="block",
         out_shape=out_shape,
-        in_specs=[local] + [anywhere] * 3 + [local] * 11,
-        out_specs=[anywhere] * 7 + [local] * 6,
+        in_specs=[local] + [anywhere] * 2 + [local] * 10,
+        out_specs=[anywhere] * 8 + [local] * 6,
         scratch_shapes=scratch,
         compiler_params=pltpu.CompilerParams(
-            collective_id=1, has_side_effects=True, vmem_limit_bytes=60 * 1024 * 1024
+            collective_id=1, has_side_effects=True, vmem_limit_bytes=VMEM
         ),
-    )(shard, normed_one, rows, back, cosine, sine, keep, gain, *small)
+    )(shard, rows, back, *small)
 
 
 def tail_kernel(
+    size,
+    sides,
+    widths,
     full,
     turned_ref,
     plain_ref,
@@ -877,30 +902,24 @@
     sine_ref,
     keep_ref,
     gain_ref,
-    entry_down_ref,
-    low_lift_ref,
-    pull_lift_ref,
-    ratio_ref,
-    pull_ref,
-    mixer_down_ref,
-    low_output_ref,
-    pull_output_ref,
-    output_ratio_ref,
-    output_pull_ref,
+    entry_ref,
+    attend_ref,
+    mixer_ref,
+    output_ref,
+    squares_ref,
+    magnitudes_ref,
     funnel_down_ref,
     funnel_up_ref,
     funnel_seen_ref,
     feed_dots_ref,
+    feed_down_ref,
+    feed_up_ref,
     partial_out,
+    partial_other,
     d_residual_out,
     funneled_out,
-    down_out,
-    up_out,
-    mixer_down_out,
-    mixer_up_out,
-    funnel_down_out,
-    funnel_up_out,
-    dots_out,
+    total,
+    norm_out,
     weights,
     residual,
     floats,
@@ -918,12 +937,19 @@
     funnel_weight,
     dots_box,
     mixer_dots,
+    entry_down_ref,
+    funnel_down,
+    gathered,
+    dots_out,
+    side_box,
+    norm_box,
     load_sems,
     weight_sems,
     funnel_sems,
     side_sends,
     side_gets,
     out_sems,
+    *sum_refs,
 ):
     tokens, width = back.shape
     count = tokens // SEQ
@@ -931,8 +957,9 @@
     near = cut // CHUNK
     wide = funnel_down_ref.shape[1]
     scale = HEAD_DIM ** (-0.5)
-    other = {"tensor": 1 - lax.axis_index("tensor")}
+    other = {"tensor": lax.rem(lax.axis_index("tensor") + 1, sides)}
     halves = CHUNK // HEAD_DIM
+    half_rows = gathered.shape[0] // 2
 
     loads = [
         pltpu.make_async_copy(source, target, load_sems.at[i])
@@ -961,9 +988,7 @@
     ]
     for load in loads[:3]:
         load.start()
-    barrier = pltpu.get_barrier_semaphore()
-    pl.semaphore_signal(barrier, inc=1, device_id=other, device_id_type=MESH)
-    pl.semaphore_wait(barrier, 1)
+    greet_sum(size, sides)
 
     def remote(source, target, index):
         return pltpu.make_async_remote_copy(
@@ -987,6 +1012,15 @@
         load.start()
     dots_copy = remote(dots_box.at[0], dots_box.at[1], count)
     funneled_copy = remote(funneled_ref, funneled_out, count + 1)
+    partial_copy = remote(own, partial_other, count + 2)
+    norms = jnp.sqrt(squares_ref[...] + COLUMN_EPS)
+    ratios = magnitudes_ref[...] / norms
+    pulls = 1.0 / (norms * magnitudes_ref[...])
+    for i in range(3):
+        entry_down_ref[pl.ds(RANK * i, RANK)] = entry_ref[i].astype(jnp.bfloat16)
+    mixer_low = mixer_ref[...].astype(jnp.bfloat16)
+    output_ratio = [long_row(ratios, 2 * i, width) for i in range(2)]
+    output_pull = [long_row(pulls, 2 * i, width) for i in range(2)]
 
     def weight_of(i):
         return weights[i].reshape(width, cut)
@@ -1044,11 +1078,11 @@
     head_seen = [
         dot_nn(entry_down_ref[pl.ds(RANK * i, RANK)], weight_of(i)) for i in range(3)
     ]
-    mixer_seen = dot_nt(mixer_down_ref[...], weight_of(3))
+    mixer_seen = dot_nt(mixer_low, weight_of(3))
     reduced = dot_nt(entry_down_ref[...], normed[...]).astype(jnp.bfloat16)
     dots_copy.wait()
     funnel_dots = dots_box[0, 0:1] + dots_box[1, 0:1]
-    funnel_pull = (pull_output_ref[1] * funnel_dots).astype(jnp.bfloat16)
+    funnel_pull = (output_ref[1] * (output_pull[1] * funnel_dots)).astype(jnp.bfloat16)
 
     def correct(block, carry):
         slot = lax.rem(block, 2)
@@ -1059,16 +1093,17 @@
 
         funnel_load(block, slot).wait()
         columns = pl.ds(pl.multiple_of(block * CHUNK, CHUNK), CHUNK)
-        funnel_down_out[:, columns] = funnel_down_ref[:, columns] - ADAPTER_SCALE * dot_nn(
+        funnel_down[:, columns] = funnel_down_ref[:, columns] - ADAPTER_SCALE * dot_nn(
             funnel_pull, funnel_weight[slot].reshape(width, CHUNK)
         )
         return carry
 
     lax.fori_loop(0, wide // CHUNK, correct, 0)
-    funnel_up_out[...] = ADAPTER_SCALE * (
-        funnel_up_ref[...] * output_ratio_ref[1:2]
-        - funnel_seen_ref[...] * (output_pull_ref[1:2] * funnel_dots)
+    gathered[pl.ds(6 * RANK, RANK)] = ADAPTER_SCALE * (
+        funnel_up_ref[...] * output_ratio[1]
+        - funnel_seen_ref[...] * (output_pull[1] * funnel_dots)
     )
+    gathered[pl.ds(3 * RANK, 2 * RANK)] = feed_down_ref[...]
     mixer_dots[...] = jnp.zeros_like(mixer_dots)
     small = 32
     for part in range(count):
@@ -1079,7 +1114,7 @@
         def pull_back(index, carry, part=part):
             place = pl.ds(pl.multiple_of(part * SEQ + index * small, small), small)
             value = residual[place]
-            weighted = gain_ref[...] * (
+            weighted = gain_ref[1:2] * (
                 own[place].astype(jnp.float32) + inbox[place].astype(jnp.float32)
             )
             root = lax.rsqrt(jnp.mean(value * value, axis=1, keepdims=True) + NORM_EPS)
@@ -1144,13 +1179,21 @@
             )
         dots = jnp.concatenate(dots, axis=1)
         dots_out[4 + i : 5 + i] = dots
-        pulled = (pull_lift_ref[i] * dots).astype(jnp.bfloat16)
-        up_out[i] = ADAPTER_SCALE * (
-            dot_nn(reduced[RANK * i : RANK * (i + 1)], d_heads[i, :tokens]) * ratio_ref[i : i + 1]
-            - head_seen[i] * (pull_ref[i : i + 1] * dots)
-        )
-        lowered = dot_nt(low_lift_ref[i], d_heads[i, :tokens]).astype(jnp.bfloat16)
-        down_out[pl.ds(RANK * i, RANK)] = ADAPTER_SCALE * dot_nn(lowered, normed[...])
+        head_ratio = ratios[4 + i : 5 + i]
+        pulled = (attend_ref[i] * (pulls[4 + i : 5 + i] * dots)).astype(jnp.bfloat16)
+        place_in(
+            gathered,
+            half_rows,
+            cut * i,
+            ADAPTER_SCALE
+            * (
+                dot_nn(reduced[RANK * i : RANK * (i + 1)], d_heads[i, :tokens]) * head_ratio
+                - head_seen[i] * (pulls[4 + i : 5 + i] * dots)
+            ),
+        )
+        low_lift = (attend_ref[i] * head_ratio).astype(jnp.bfloat16)
+        lowered = dot_nt(low_lift, d_heads[i, :tokens]).astype(jnp.bfloat16)
+        gathered[pl.ds(RANK * i, RANK)] = ADAPTER_SCALE * dot_nn(lowered, normed[...])
         d_heads[i, tokens:] = pulled
     for piece in range(width // 512):
         lanes = slice(piece * 512, (piece + 1) * 512)
@@ -1162,20 +1205,20 @@
             results[0][:tokens] + results[1][:tokens] + results[2][:tokens]
         ).astype(jnp.bfloat16)
         for i in range(3):
-            down_out[pl.ds(RANK * i, RANK), lanes] -= ADAPTER_SCALE * results[i][tokens:]
-    partial_copy = pltpu.make_async_copy(own, partial_out, out_sems.at[1])
+            gathered[pl.ds(RANK * i, RANK), lanes] -= ADAPTER_SCALE * results[i][tokens:]
     partial_copy.start()
+    partial_save = pltpu.make_async_copy(own, partial_out, out_sems.at[1])
+    partial_save.start()
     mixer_total = jnp.sum(mixer_dots[...], axis=0, keepdims=True)
     joined = jnp.concatenate([mixed[b] for b in range(near)], axis=1)
-    lowered = dot_nt(low_output_ref[...], d_low[...]).astype(jnp.bfloat16)
-    pulled = (pull_output_ref[0] * mixer_total).astype(jnp.bfloat16)
-    mixer_down_out[...] = ADAPTER_SCALE * (
-        dot_nn(lowered, joined) - dot_nn(pulled, weight_of(3))
-    )
-    reduced_mixed = dot_nt(mixer_down_ref[...], joined).astype(jnp.bfloat16)
-    mixer_up_out[...] = ADAPTER_SCALE * (
-        dot_nn(reduced_mixed, d_low[...]) * output_ratio_ref[0:1]
-        - mixer_seen * (output_pull_ref[0:1] * mixer_total)
+    low_output = (output_ref[0] * output_ratio[0]).astype(jnp.bfloat16)
+    lowered = dot_nt(low_output, d_low[...]).astype(jnp.bfloat16)
+    pulled = (output_ref[0] * (output_pull[0] * mixer_total)).astype(jnp.bfloat16)
+    mixer_down = ADAPTER_SCALE * (dot_nn(lowered, joined) - dot_nn(pulled, weight_of(3)))
+    reduced_mixed = dot_nt(mixer_low, joined).astype(jnp.bfloat16)
+    gathered[pl.ds(5 * RANK, RANK)] = ADAPTER_SCALE * (
+        dot_nn(reduced_mixed, d_low[...]) * output_ratio[0]
+        - mixer_seen * (output_pull[0] * mixer_total)
     )
     for i, value in enumerate((mixer_total, funnel_dots)):
         for r in range(2):
@@ -1194,40 +1237,56 @@
             row += 1
     if row < dots_out.shape[0]:
         dots_out[row:] = jnp.zeros((dots_out.shape[0] - row, LANES), jnp.float32)
+    offset = 3 * cut
+    for value in (feed_up_ref[0], feed_up_ref[1], mixer_down, funnel_down[...], dots_out[...]):
+        place_in(gathered, half_rows, offset, value)
+        offset += value.shape[1]
+    rest_columns = half_rows // RANK * width - offset
+    place_in(gathered, half_rows, offset, jnp.zeros((RANK, rest_columns), jnp.float32))
+    sum_up(
+        size, sides, widths, offset, magnitudes_ref, total, norm_out, gathered, side_box, norm_box,
+        *sum_refs,
+    )
     d_residual_copy.wait()
+    partial_save.wait()
+    funneled_copy.wait()
     partial_copy.wait()
-    funneled_copy.wait()
-
-
-def run_tail(big, small, lines):
+
+
+def run_tail(big, small):
+    size = lax.axis_size("dp")
+    sides = lax.axis_size("tensor")
     full, turned, plain, mixed, residual = big[:5]
     tokens, width = residual.shape
     line, height = full.shape[1], full.shape[4]
     near = mixed.shape[0]
     cut = near * CHUNK
-    wide = small[14].shape[1]
+    wide = small[10].shape[1]
+    lines = small[8].shape[0]
     count = tokens // SEQ
     anywhere = pl.BlockSpec(memory_space=pl.ANY)
     local = pl.BlockSpec(memory_space=pltpu.VMEM)
     low, full_type = jnp.bfloat16, jnp.float32
     heads = cut // HEAD_DIM
+    rows = 7 * RANK
+    bits = len(bin(size)) - 3
+    widths = [max(width >> (step + 1), 128) for step in range(bits)]
+    halvings = sum(1 for step in range(bits) if width >> (step + 1) >= 128)
+    boxes = [pltpu.VMEM((2 * rows, w), low) for w in widths]
+    copies = bits + halvings + 2 * (sides - 1)
     return pl.pallas_call(
-        tail_kernel,
+        functools.partial(tail_kernel, size, sides, widths),
         name="tail",
         out_shape=(
             jax.ShapeDtypeStruct((tokens, width), low),
+            jax.ShapeDtypeStruct((tokens, width), low),
             jax.ShapeDtypeStruct((tokens, width), full_type),
             jax.ShapeDtypeStruct((tokens, width), low),
-            jax.ShapeDtypeStruct((3 * RANK, width), full_type),
-            jax.ShapeDtypeStruct((3, RANK, cut), full_type),
-            jax.ShapeDtypeStruct((RANK, cut), full_type),
-            jax.ShapeDtypeStruct((RANK, width), full_type),
-            jax.ShapeDtypeStruct((RANK, wide), full_type),
-            jax.ShapeDtypeStruct((RANK, width), full_type),
-            jax.ShapeDtypeStruct((lines, LANES), full_type),
+            jax.ShapeDtypeStruct((2 * rows, width), low),
+            jax.ShapeDtypeStruct((8, 128), full_type),
         ),
-        in_specs=[anywhere] * 10 + [local] * 18,
-        out_specs=[anywhere] * 3 + [local] * 7,
+        in_specs=[anywhere] * 10 + [local] * 16,
+        out_specs=[anywhere] * 4 + [local] * 2,
         scratch_shapes=[
             pltpu.VMEM((4, line, 2, 2, height, cut), low),
             pltpu.VMEM((tokens, width), full_type),
@@ -1246,15 +1305,25 @@
             pltpu.VMEM((2, line, 2, 2, height, CHUNK), low),
             pltpu.VMEM((2, 8, width), full_type),
             pltpu.VMEM((8, width), full_type),
+            pltpu.VMEM((3 * RANK, width), low),
+            pltpu.VMEM((RANK, wide), full_type),
+            pltpu.VMEM((2 * rows, width), full_type),
+            pltpu.VMEM((lines, LANES), full_type),
+            pltpu.VMEM((sides, rows, widths[-1]), low),
+            pltpu.VMEM((sides, 8, 128), full_type),
             pltpu.SemaphoreType.DMA((9,)),
             pltpu.SemaphoreType.DMA((4 * near,)),
             pltpu.SemaphoreType.DMA((2,)),
-            pltpu.SemaphoreType.DMA((count + 2,)),
-            pltpu.SemaphoreType.DMA((count + 2,)),
+            pltpu.SemaphoreType.DMA((count + 3,)),
+            pltpu.SemaphoreType.DMA((count + 3,)),
             pltpu.SemaphoreType.DMA((2,)),
+            *boxes,
+            *boxes,
+            pltpu.SemaphoreType.DMA((copies,)),
+            pltpu.SemaphoreType.DMA((copies,)),
         ],
         compiler_params=pltpu.CompilerParams(
-            collective_id=2, has_side_effects=True, vmem_limit_bytes=62 * 1024 * 1024
+            collective_id=2, has_side_effects=True, vmem_limit_bytes=VMEM
         ),
     )(*big, *small)
 
@@ -1285,19 +1354,11 @@
     return pieces[0] if len(pieces) == 1 else jnp.concatenate(pieces, axis=1)
 
 
-def sum_kernel(
+def sum_up(
     size,
     sides,
     widths,
-    down_ref,
-    feed_down_ref,
-    mixer_up_ref,
-    funnel_up_ref,
-    up_ref,
-    feed_up_ref,
-    mixer_down_ref,
-    funnel_down_ref,
-    dots_ref,
+    offset,
     magnitude_ref,
     total,
     norm_out,
@@ -1313,7 +1374,6 @@
     me = lax.axis_index("dp")
     side = lax.axis_index("tensor")
     partners = partners_of(size)
-    greet_sum(size, sides)
 
     def remote(source, target, index, where):
         return pltpu.make_async_remote_copy(
@@ -1324,19 +1384,6 @@
             device_id=where,
             device_id_type=MESH,
         )
-
-    row = 0
-    for ref in (down_ref, feed_down_ref, mixer_up_ref, funnel_up_ref):
-        gathered[pl.ds(row, ref.shape[0])] = ref[...]
-        row += ref.shape[0]
-    offset = 0
-    split = [up_ref[i] for i in range(3)] + [feed_up_ref[i] for i in range(2)]
-    split += [mixer_down_ref[...], funnel_down_ref[...], dots_ref[...]]
-    for value in split:
-        place_in(gathered, half, offset, value)
-        offset += value.shape[1]
-    rest_columns = half // RANK * gathered.shape[1] - offset
-    place_in(gathered, half, offset, jnp.zeros((RANK, rest_columns), jnp.float32))
 
     start = 0
     width = gathered.shape[1]
@@ -1393,9 +1440,8 @@
     for row in range(0, half, RANK):
         value = total[pl.ds(row, RANK)].astype(jnp.float32)
         squares += jnp.sum(value * value, axis=1, keepdims=True)
-    lines = dots_ref.shape[1]
-    dots_offset = offset - lines
-    dots = take_from(total, half, dots_offset, lines) / magnitude_ref[...]
+    dots_offset = offset - LANES
+    dots = take_from(total, half, dots_offset, LANES) / magnitude_ref[...]
     dots = jnp.sum(dots * dots, axis=1, keepdims=True)
     shared_total = jnp.sum(squares) + jnp.sum(dots[:4])
     split_squares = jnp.zeros((RANK, 1), jnp.float32)
@@ -1422,40 +1468,6 @@
     norm_out[...] = jnp.sqrt(split_sum + shared_total)
 
 
-def sum_all(parts, magnitudes):
-    size = lax.axis_size("dp")
-    sides = lax.axis_size("tensor")
-    width = parts[0].shape[1]
-    rows = sum(part.shape[0] for part in parts[:4])
-    bits = len(bin(size)) - 3
-    widths = [max(width >> (step + 1), 128) for step in range(bits)]
-    halvings = sum(1 for step in range(bits) if width >> (step + 1) >= 128)
-    boxes = [pltpu.VMEM((2 * rows, w), jnp.bfloat16) for w in widths]
-    copies = bits + halvings + 2 * (sides - 1)
-    return pl.pallas_call(
-        functools.partial(sum_kernel, size, sides, widths),
-        name="sum",
-        out_shape=(
-            jax.ShapeDtypeStruct((2 * rows, width), jnp.bfloat16),
-            jax.ShapeDtypeStruct((8, 128), jnp.float32),
-        ),
-        in_specs=[pl.BlockSpec(memory_space=pltpu.VMEM)] * 10,
-        out_specs=[pl.BlockSpec(memory_space=pltpu.VMEM)] * 2,
-        scratch_shapes=[
-            pltpu.VMEM((2 * rows, width), jnp.float32),
-            pltpu.VMEM((sides, rows, widths[-1]), jnp.bfloat16),
-            pltpu.VMEM((sides, 8, 128), jnp.float32),
-            *boxes,
-            *boxes,
-            pltpu.SemaphoreType.DMA((copies,)),
-            pltpu.SemaphoreType.DMA((copies,)),
-        ],
-        compiler_params=pltpu.CompilerParams(
-            collective_id=3, has_side_effects=True, vmem_limit_bytes=32 * 1024 * 1024
-        ),
-    )(*parts, magnitudes)
-
-
 def update_kernel(*refs):
     total, norm_ref = refs[:2]
     values, firsts, seconds = refs[2:11], refs[11:20], refs[20:29]
@@ -1519,7 +1531,7 @@
         out_shape=shapes * 3,
         in_specs=[pl.BlockSpec(memory_space=pltpu.VMEM)] * 29,
         out_specs=[pl.BlockSpec(memory_space=pltpu.VMEM)] * 27,
-        compiler_params=pltpu.CompilerParams(vmem_limit_bytes=48 * 1024 * 1024),
+        compiler_params=pltpu.CompilerParams(vmem_limit_bytes=VMEM),
     )(total, norm, *params, *firsts, *seconds)
 
 
@@ -1597,72 +1609,31 @@
         amplitude_second,
         loudness_second,
     )
-    rows = base_query.shape[0]
+    rows, cut = base_query.shape
     width = activations.shape[1]
     place = lax.axis_index("dp") * rows
-    cut = base_query.shape[1]
-    wide = base_gate.shape[1]
-    entry_rows = lax.dynamic_slice_in_dim(entry_value, place, rows, 1)
-    output_columns = lax.dynamic_slice_in_dim(output_value, place, rows, 2)
-    lifts = [attend_value[0], attend_value[1], attend_value[2], widen_value[0], widen_value[1]]
-    pad = -wide % LANES
-    magnitudes = jnp.concatenate(
-        [
-            loudness_value.reshape(-1, LANES),
-            stature_value.reshape(-1, LANES),
-            jnp.pad(amplitude_value, ((0, 0), (0, pad)), constant_values=1.0).reshape(-1, LANES),
-        ]
-    )
-    magnitudes = jnp.pad(magnitudes, ((0, -magnitudes.shape[0] % 8), (0, 0)), constant_values=1.0)
-    shard, squares = merge(
+    entry_down = jnp.swapaxes(entry_value, 1, 2)
+    shard, squares, magnitudes = merge(
         (base_query, base_key, base_value, base_gate, base_widen, base_mixer, base_funnel),
-        entry_rows,
+        lax.dynamic_slice_in_dim(entry_down, place, rows, 2),
         attend_value,
         widen_value,
-        mixer_value,
-        funnel_value,
-        output_columns,
-        magnitudes,
+        mixer_value.T,
+        funnel_value.T,
+        lax.dynamic_slice_in_dim(output_value, place, rows, 2),
+        (stature_value, amplitude_value, loudness_value),
     )
-    lines = (wide + pad) // LANES
-    shared_norms = jnp.sqrt(squares[:4].reshape(2, width) + COLUMN_EPS)
-    split_norms = jnp.sqrt(
-        jnp.concatenate(
-            [squares[4:7].reshape(-1)]
-            + [
-                squares[7 + i * lines : 7 + (i + 1) * lines].reshape(-1)[:wide]
-                for i in range(2)
-            ]
-        )
-        + COLUMN_EPS
-    )
-    split_wide = split_norms.shape[0]
-    split_magnitudes = jnp.concatenate([stature_value.reshape(-1), amplitude_value.reshape(-1)])
-    split_ratio = split_magnitudes / split_norms
-    shared_ratio = loudness_value / shared_norms
-    floats = activations.astype(jnp.float32)
-    normed_one = low(root_norm(floats, norm_gains[0]))
     count = activations.shape[0] // SEQ
-    half = jnp.arange(HEAD_DIM // 2, dtype=jnp.float32)
-    angles = positions.astype(jnp.float32)[:, None] * (ROPE_BASE ** (-2.0 * half / HEAD_DIM))[None]
-    cosine = jnp.tile(jnp.cos(angles), (1, 2))
-    sine = jnp.sin(angles)
-    sine = jnp.concatenate([-sine, sine], axis=1)
+    half = HEAD_DIM // 2
+    lane = jnp.arange(HEAD_DIM)
+    frequency = ROPE_BASE ** (-2.0 * (lane % half).astype(jnp.float32) / HEAD_DIM)
+    angles = positions.astype(jnp.float32)[:, None] * frequency[None]
+    cosine = jnp.cos(angles)
+    sine = jnp.sin(angles) * jnp.where(lane < half, -1.0, 1.0)[None]
     keep = padding_mask.reshape(count, 1, SEQ)
-    feed_ratio = split_ratio[3 * cut :].reshape(2, wide)
-    feed_pull = 1.0 / (split_norms[3 * cut :] * split_magnitudes[3 * cut :]).reshape(2, wide)
-    entry_down = low(jnp.swapaxes(entry_value, 1, 2))
-    small = (
-        entry_down[3:].reshape(2 * RANK, width),
-        low(funnel_value.T),
-        low(widen_value * feed_ratio[:, None]),
-        widen_value * feed_pull[:, None],
-        feed_ratio,
-        feed_pull,
-        low(output_value[1] * shared_ratio[1]),
-    )
     (
         full,
+        normed_one,
         turned,
         plain,
         mixed,
@@ -1676,69 +1647,53 @@
         funnel_seen,
         feed_dots,
     ) = run_block(
-        shard, normed_one, activations, cotangent, cosine, sine, keep, norm_gains[1:2], small
+        shard,
+        activations,
+        cotangent,
+        (
+            cosine,
+            sine,
+            keep,
+            norm_gains,
+            entry_down,
+            funnel_value.T,
+            widen_value,
+            output_value,
+            squares,
+            magnitudes,
+        ),
     )
-    head_pull = 1.0 / (split_norms[: 3 * cut] * split_magnitudes[: 3 * cut]).reshape(3, cut)
-    head_ratio = split_ratio[: 3 * cut].reshape(3, cut)
-    shared_pull = 1.0 / (shared_norms * loudness_value)
-    small = (
-        cosine,
-        sine,
-        keep,
-        norm_gains[1:2],
-        entry_down[:3].reshape(3 * RANK, width),
-        low(attend_value * head_ratio[:, None]),
-        attend_value * head_pull[:, None],
-        head_ratio,
-        head_pull,
-        low(mixer_value.T),
-        low(output_value[0] * shared_ratio[0]),
-        output_value * shared_pull[:, None],
-        shared_ratio,
-        shared_pull,
-        funnel_down,
-        funnel_up,
-        funnel_seen,
-        feed_dots,
-    )
-    big = (
-        full,
-        turned,
-        plain,
-        mixed,
-        residual,
-        d_normed_two,
-        funneled,
-        cotangent,
-        activations,
-        normed_one,
-    )
-    (
-        partial,
-        d_residual,
-        funneled_other,
-        head_downs,
-        head_ups,
-        mixer_down,
-        mixer_up,
-        funnel_down,
-        funnel_up,
-        dots,
-    ) = run_tail(big, small, squares.shape[0])
-    d_normed_one = swap(partial)
-    total, norm = sum_all(
+    partial, partial_other, d_residual, funneled_other, total, norm = run_tail(
         (
-            head_downs,
+            full,
+            turned,
+            plain,
+            mixed,
+            residual,
+            d_normed_two,
+            funneled,
+            cotangent,
+            activations,
+            normed_one,
+        ),
+        (
+            cosine,
+            sine,
+            keep,
+            norm_gains,
+            entry_down,
+            attend_value,
+            mixer_value.T,
+            output_value,
+            squares,
+            magnitudes,
+            funnel_down,
+            funnel_up,
+            funnel_seen,
+            feed_dots,
             feed_downs,
-            mixer_up,
-            funnel_up,
-            head_ups,
             feed_ups,
-            mixer_down,
-            funnel_down,
-            dots,
         ),
-        magnitudes,
     )
 
     def turned_over(items):
@@ -1752,6 +1707,8 @@
     block_output = low(
         residual + (funneled.astype(jnp.float32) + funneled_other.astype(jnp.float32))
     )
+    floats = activations.astype(jnp.float32)
+    d_normed_one = partial.astype(jnp.float32) + partial_other.astype(jnp.float32)
     unused, first_pull = jax.vjp(lambda v: root_norm(v, norm_gains[0]), floats)
     input_gradient = d_residual + first_pull(d_normed_one)[0]
     return (

time: 584 us -> 545 us (0.933)
  local copies, waits for them, and re-layouts: 46.1 us -> 3.98 us
  Pallas kernels: 500 us -> 520 us
  other arithmetic: 25.4 us -> 14.6 us
    unnamed x131 -> x16, local copies, waits for them, and re-layouts: 38.5 us -> 0.07 us
    pallas_call x2 -> x1, Pallas kernels: 148 us -> 165 us  [run_tail(): pl.pallas_call(functools.partial(tail_kernel, size, sides, widths), name=...]
    convert_element_type x6 -> x1, other arithmetic: 11.8 us -> 2.43 us  [low(): return values.astype(jnp.bfloat16)]
  transfers between devices with their start and end apart: 1 -> 0, of which waited for: 0 -> 0; matrix products, arithmetic and copies ran while one was open for 1% -> 0% of each run, Pallas kernels for 10% -> 0%
where the time goes in v5:
time: 545 us; the launch traced here: 539 us
  Pallas kernels  520 us (95%)
  other arithmetic  14.6 us (3%)
    pallas_call x1, Pallas kernels, run_block(): pl.pallas_call(functools.partial(block_kernel, size), name='block', out_s...  319 us
    pallas_call x1, Pallas kernels, run_tail(): pl.pallas_call(functools.partial(tail_kernel, size, sides, widths), name=...  165 us
    pallas_call x1, Pallas kernels, merge(): pl.pallas_call(functools.partial(merge_kernel, size, sides), name='merge'...  29.3 us

profile of v5, /device:TPU:0, one launch (start us, length us, event | category | flops | bytes accessed | tf_op | source)
XLA Modules:
  0.0 539.5 jit_solution(16876115677974219645)
XLA Ops:
  0.7 0.0 copy-start.7
  0.7 1.4 dynamic-slice_bitcast_fusion.entry_ref
  2.1 1.3 constant_dynamic-slice_fusion.output_ref
  3.4 29.3 %merge.1 = (bf16[49,128,256]{2,1,0:T(8,128)(2,1)}, f32[16,1024]{1,0:T(8,128)}, f32[16,1024]{1,0:T(8,128)}) custom-call(bf16[128,1024]{1,0:T(8,128)(2,1)} %query_ref.1, bf16[128,1024]{1,0:T(8,128)(2,1)} %key_ref.1, bf16[128,1024]{1,0:T(8,128)(2,1)} %value_ref.1, bf16[128,2816]{1,0:T(8,128)(2,1)} %gate_ref.1, bf16[128,2816]{1,0:T(8,128)(2,1)} %widen_ref.1, ...), custom_call_target="tpu_custom_call" | custom-call | tf_op jit(solution)/shard_map/merge/pallas_call | solution.py:230
  32.7 0.0 copy-done.7
  32.8 1.8 fusion.3
  34.6 318.8 %block.1 = (bf16[49,4,2,2,128,256]{5,4,3,2,1,0:T(8,128)(2,1)}, bf16[512,2048]{1,0:T(8,128)(2,1)}, bf16[12,512,256]{2,1,0:T(8,128)(2,1)}, bf16[8,512,256]{2,1,0:T...) custom-call(bf16[49,128,256]{2,1,0:T(8,128)(2,1)} %get-tuple-element, ...), custom_call_target="tpu_custom_call" | custom-call | tf_op jit(solution)/shard_map/block/pallas_call | solution.py:874
  353.4 165.4 %tail.1 = (bf16[512,2048]{1,0:T(8,128)(2,1)}, bf16[512,2048]{1,0:T(8,128)(2,1)}, f32[512,2048]{1,0:T(8,128)}, bf16[512,2048]{1,0:T(8,128)(2,1)}, bf16[224,2048]{1,0:T(8,128)(2,1)}, /*index=5*/f32[8,128]{1,0:T(8,128)}) custom-call(bf16[49,4,2,2,128,256]{5,4,3,2,1,0:T(8,128)(2,1)} %get-tuple-element.85.full, ...), custom_call_target="tpu_custom_call" | custom-call | tf_op jit(solution)/shard_map/tail/pallas_call | solution.py:1277
  518.8 0.0 copy-start.6
  518.8 6.0 %update.1 = (f32[5,16,2048]{2,1,0:T(8,128)}, f32[3,16,1024]{2,1,0:T(8,128)}, f32[2,16,2816]{2,1,0:T(8,128)}, f32[16,1024]{1,0:T(8,128)}, f32[16,2816]{1,0:T(8,12...) custom-call(bf16[224,2048]{1,0:T(8,128)(2,1)} %get-tuple-element.102, ...), custom_call_target="tpu_custom_call" | custom-call | tf_op jit(solution)/shard_map/update/pallas_call | solution.py:1528
  524.9 0.0 copy-start
  524.9 0.0 copy-start.3
  524.9 0.0 copy-start.4
  524.9 0.0 copy-done.6
  524.9 4.6 fusion
  529.6 0.0 copy-done
  529.6 0.0 copy-done.3
  529.6 0.0 copy-done.4
  529.6 0.0 copy-start.1
  529.6 0.0 copy-start.2
  529.6 0.0 copy-start.5
  529.6 5.7 %fusion.2 = f32[512,2048]{1,0:T(8,128)} fusion(f32[512,2048]{1,0:T(8,128)} %get-tuple-element.98, bf16[512,2048]{1,0:T(8,128)(2,1)S(1)} %copy-done, bf16[512,2048]{1,0:T(8,128)(2,1)S(1)} %copy-done.4, bf16[512,2048]{1,0:T(8,128)(2,1)S(1)} %copy-done.3, f32[512]{0:T(512)S(1)} %get-tuple-element.135, f32[512]{0:T(512)S(1)} %get-tuple-element.134, ...), kind=kLoop, calls=%fused_computation.6 | loop fusion | flops 10485760 | bytes 14692352 | tf_op jit(solution)/shard_map/add | solution.py:1713
  535.4 0.0 copy-done.1
  535.4 0.0 copy-done.2
  535.4 0.0 copy-done.5
  535.4 2.4 add_convert_fusion
  537.8 1.2 slice.7
  (4 shorter events, 0.0 us)
Async XLA Ops:
  0.7 32.1 %copy-start.7 = (s32[512]{0:T(512)S(1)}, s32[512]{0:T(512)}, u32[]{:S(2)}) copy-start(s32[512]{0:T(512)} %param.42) | copy-start | bytes 6148
  518.8 6.1 %copy-start.6 = (f32[2,2048]{1,0:T(2,128)S(1)}, f32[2,2048]{1,0:T(2,128)}, u32[]{:S(2)}) copy-start(f32[2,2048]{1,0:T(2,128)} %gain_ref.3) | copy-start | bytes 49156
  524.9 4.7 copy-start
  524.9 4.7 copy-start.3
  524.9 4.7 copy-start.4
  529.6 5.7 %copy-start.1 = (f32[512,2048]{1,0:T(8,128)S(1)}, f32[512,2048]{1,0:T(8,128)}, u32[]{:S(2)}) copy-start(f32[512,2048]{1,0:T(8,128)} %get-tuple-element.83.residual_ref) | copy-start | bytes 12582916
  529.6 5.7 %copy-start.2 = (bf16[512,2048]{1,0:T(8,128)(2,1)S(1)}, bf16[512,2048]{1,0:T(8,128)(2,1)}, u32[]{:S(2)}) copy-start(bf16[512,2048]{1,0:T(8,128)(2,1)} %get-tuple-element.84.funneled_ref) | copy-start | bytes 6291460
  529.6 5.7 %copy-start.5 = (bf16[512,2048]{1,0:T(8,128)(2,1)S(1)}, bf16[512,2048]{1,0:T(8,128)(2,1)}, u32[]{:S(2)}) copy-start(bf16[512,2048]{1,0:T(8,128)(2,1)} %get-tuple-element.97) | copy-start | bytes 6291460

commit v6 on v5

--- a/solution.py
+++ b/solution.py
@@ -30,20 +30,12 @@
 MASKED = -1e30
 
 
-def root_norm(values, gain):
-    return values * lax.rsqrt(jnp.mean(values * values, axis=-1, keepdims=True) + NORM_EPS) * gain
-
-
 def decoupled_update(value, gradient, first, second, rate):
     momentum = BETA_ONE * first + (1.0 - BETA_ONE) * gradient
     variance = BETA_TWO * second + (1.0 - BETA_TWO) * gradient * gradient
     corrected = momentum / (1.0 - BETA_ONE**STEP)
     spread = jnp.sqrt(variance / (1.0 - BETA_TWO**STEP))
     return (value - rate * (corrected / (spread + ADAM_EPS) + DECAY * value), momentum, variance)
-
-
-def low(values):
-    return values.astype(jnp.bfloat16)
 
 
 MESH = pl.DeviceIdType.MESH
@@ -270,7 +262,7 @@
 
 BLOCKS = 3
 HEAD_CHUNKS = 5
-EXTRA_TICKS = 3
+EXTRA_TICKS = 2
 
 
 def gather_parts(size, shard, full, sems):
@@ -291,19 +283,16 @@
 
     def greet():
         barrier = pltpu.get_barrier_semaphore()
-        ahead, behind = spot < line - 1, spot > 0
-
-        @pl.when(ahead)
-        def _():
-            pl.semaphore_signal(barrier, inc=1, device_id=right, device_id_type=MESH)
-
-        @pl.when(behind)
-        def _():
-            pl.semaphore_signal(barrier, inc=1, device_id=left, device_id_type=MESH)
-
+        peers = jnp.int32(3)
+        for near, target in ((spot < line - 1, right), (spot > 0, left)):
+
+            @pl.when(near)
+            def _(target=target):
+                pl.semaphore_signal(barrier, inc=1, device_id=target, device_id_type=MESH)
+
+            peers += near.astype(jnp.int32)
         for target in (across, twin, {"tensor": 1 - lax.axis_index("tensor")}):
             pl.semaphore_signal(barrier, inc=1, device_id=target, device_id_type=MESH)
-        peers = 3 + ahead.astype(jnp.int32) + behind.astype(jnp.int32)
         pl.semaphore_wait(barrier, peers)
 
     def remote(source, target, send, get, where):
@@ -340,33 +329,31 @@
             return full.at[blocks, origin, column, core, pl.ds(early, late)]
         return full.at[blocks, origin, :, core, pl.ds(0, early)]
 
-    def moves(to_right, hop, chunk, start, count):
+    def move(to_right, part, distance, chunk, start, count):
         sends, gets = (right_sends, right_gets) if to_right else (left_sends, left_gets)
+        hop = distance - 1
         blocks = pl.ds(start, count)
-        found = []
-        for part in range(2):
-            place = place_of(part, spot - hop if to_right else spot + hop, blocks)
-            source = shard.at[blocks, pl.ds(early, late)] if hop == 0 and part == 0 else place
-            found.append(
-                remote(
-                    source,
-                    place,
-                    sends.at[chunk, 2 * hop + part],
-                    gets.at[chunk, 2 * hop + part],
-                    right if to_right else left,
-                )
-            )
-        return found
-
-    def arrivals(to_right, hop, chunk, start, count):
+        place = place_of(part, spot - hop if to_right else spot + hop, blocks)
+        source = shard.at[blocks, pl.ds(early, late)] if hop == 0 and part == 0 else place
+        kept = 2 * hop + part
+        where = right if to_right else left
+        return remote(source, place, sends.at[chunk, kept], gets.at[chunk, kept], where)
+
+    def arrivals(to_right, distance, chunk, start, count):
         gets = right_gets if to_right else left_gets
         for part in range(2):
-            place = place_of(part, spot - hop if to_right else spot + hop, pl.ds(start, count))
-            kept = 2 * (hop - 1) + part
+            origin = spot - distance if to_right else spot + distance
+            place = place_of(part, origin, pl.ds(start, count))
+            kept = 2 * (distance - 1) + part
             remote(
                 place, place, right_sends.at[chunk, kept], gets.at[chunk, kept], right
             ).wait_recv()
 
+    def reaches(to_right, distance):
+        if to_right:
+            return (spot >= distance - 1) & (spot < line - 1)
+        return (spot <= line - distance) & (spot > 0)
+
     def pair_copy(chunk, start, count, owner):
         place = full.at[pl.ds(start, count), :, owner, core, pl.ds(early, late)]
         return remote(place, place, pair_sems.at[chunk, 0], pair_sems.at[chunk, 1], across)
@@ -375,58 +362,64 @@
         place = full.at[pl.ds(start, count), :, :, owner]
         return remote(place, place, core_sems.at[chunk, 0], core_sems.at[chunk, 1], twin)
 
-    def send_on(hop, chunk, start, count):
-        @pl.when((spot >= hop) & (spot < line - 1))
+    def send(distances, parts, chunk, start, count):
+        for to_right in (True, False):
+            for distance in distances:
+
+                @pl.when(reaches(to_right, distance))
+                def _(to_right=to_right, distance=distance):
+                    for part in parts:
+                        move(to_right, part, distance, chunk, start, count).start()
+
+    def take_in(distance, chunk, start, count):
+        @pl.when(spot >= distance)
         def _():
-            for copy in moves(True, hop, chunk, start, count):
-                copy.start()
-
-        @pl.when((spot < line - hop) & (spot > 0))
+            arrivals(True, distance, chunk, start, count)
+
+        @pl.when(spot < line - distance)
         def _():
-            for copy in moves(False, hop, chunk, start, count):
-                copy.start()
-
-    def take_in(hop, chunk, start, count):
-        @pl.when(spot >= hop)
-        def _():
-            arrivals(True, hop, chunk, start, count)
-
-        @pl.when(spot < line - hop)
-        def _():
-            arrivals(False, hop, chunk, start, count)
-
-    def step(phase, chunk, start, count):
-        if 1 <= phase < line:
-            take_in(phase, chunk, start, count)
-        if phase < line - 1:
-            send_on(phase, chunk, start, count)
-        if phase == line - 1:
+            arrivals(False, distance, chunk, start, count)
+
+    def own(parts, chunk, start, count):
+        send((1,), parts, chunk, start, count)
+
+    def turn(distance, chunk, start, count):
+        take_in(distance, chunk, start, count)
+        if distance < line - 1:
+            send((distance + 1,), (0, 1), chunk, start, count)
+        else:
             pair_copy(chunk, start, count, column).start()
-        elif phase == line + 1:
-            pair_copy(chunk, start, count, 1 - column).wait_recv()
-            core_copy(chunk, start, count, core).start()
-        elif phase == line + 2:
-            core_copy(chunk, start, count, 1 - core).wait_recv()
-        elif phase == line + 3:
-            finish(chunk, start, count)
+
+    def pair_done(chunk, start, count):
+        pair_copy(chunk, start, count, 1 - column).wait_recv()
+        core_copy(chunk, start, count, core).start()
+
+    def core_done(chunk, start, count):
+        core_copy(chunk, start, count, 1 - core).wait_recv()
 
     def finish(chunk, start, count):
-        for hop in range(line - 1):
-
-            @pl.when((spot >= hop) & (spot < line - 1))
-            def _(hop=hop):
-                for copy in moves(True, hop, chunk, start, count):
-                    copy.wait_send()
-
-            @pl.when((spot < line - hop) & (spot > 0))
-            def _(hop=hop):
-                for copy in moves(False, hop, chunk, start, count):
-                    copy.wait_send()
+        for to_right in (True, False):
+            for distance in range(1, line):
+
+                @pl.when(reaches(to_right, distance))
+                def _(to_right=to_right, distance=distance):
+                    for part in range(2):
+                        move(to_right, part, distance, chunk, start, count).wait_send()
 
         pair_copy(chunk, start, count, column).wait_send()
         core_copy(chunk, start, count, core).wait_send()
 
-    return greet, step, early_start, early_wait, finish
+    def stages(pace):
+        found = {0: functools.partial(own, (0, 1))}
+        for distance in range(1, line):
+            found[pace * distance] = functools.partial(turn, distance)
+        last = pace * (line - 1)
+        found[last + 2] = pair_done
+        found[last + 3] = core_done
+        found[last + 4] = finish
+        return found
+
+    return greet, own, stages, early_start, early_wait, finish
 
 
 def block_kernel(
@@ -489,6 +482,7 @@
     early_sems,
     local_sems,
     weight_sems,
+    feed_sems,
     side_sends,
     side_gets,
     out_sems,
@@ -500,22 +494,34 @@
     count = tokens // SEQ
     sides = {"tensor": 1 - lax.axis_index("tensor")}
     sems = (right_sends, left_sends, right_gets, left_gets, pair_sems, core_sems, early_sems)
-    greet, step, early_start, early_wait, finish = gather_parts(size, shard, full, sems)
+    greet, send_own, stages, early_start, early_wait, finish = gather_parts(
+        size, shard, full, sems
+    )
     me = lax.axis_index("dp")
     core, column, spot = lax.rem(me, 2), lax.rem(lax.div(me, 2), 2), lax.div(me, 4)
 
-    def tick(now):
-        for phase in range(line + 4):
+    slow, fast = stages(1), stages(1)
+    lag = (line - 1) + 3
+
+    def tick(now, sends=True):
+        for phase, stage in slow.items():
             chunk = now - phase
+            if phase == 0 and not sends:
+                continue
             start = 1 + BLOCKS * chunk
             if isinstance(now, int):
-                if 0 <= chunk < chunks:
-                    step(phase, chunk, start, BLOCKS)
+                if 1 <= chunk < chunks:
+                    stage(chunk, start, BLOCKS)
             else:
 
-                @pl.when((chunk >= 0) & (chunk < chunks))
-                def _(phase=phase, chunk=chunk, start=start):
-                    step(phase, chunk, start, BLOCKS)
+                @pl.when((chunk >= 1) & (chunk < chunks))
+                def _(stage=stage, chunk=chunk, start=start):
+                    stage(chunk, start, BLOCKS)
+
+    def first_ticks(now):
+        if now in fast:
+            fast[now](chunks, 0, 1)
+            fast[now](0, 1, BLOCKS)
 
     own = pltpu.make_async_copy(shard, full.at[:, spot, column, core], local_sems.at[0])
     own.start()
@@ -527,10 +533,12 @@
         load.start()
     greet()
     early_start()
+    send_own((0,), chunks, 0, 1)
+    send_own((0,), 0, 1, BLOCKS)
     own.wait()
     early_wait(0)
-    step(0, chunks, 0, 1)
-    tick(0)
+    send_own((1,), chunks, 0, 1)
+    send_own((1,), 0, 1, BLOCKS)
     early_wait(1)
     for load in loads:
         load.wait()
@@ -563,8 +571,9 @@
         for i in range(2):
             normed[pl.ds(tokens + RANK * i, RANK)] = entry_ref[3 + i].astype(jnp.bfloat16)
 
-    for now in range(1, line + 4):
-        step(now, chunks, 0, 1)
+    head_ticks = max(fast) + 1
+    for now in range(1, head_ticks):
+        first_ticks(now)
         tick(now)
         if now == 1:
             prepare()
@@ -572,8 +581,8 @@
         normed.at[pl.ds(0, tokens)], normed_out, local_sems.at[3]
     )
     normed_copy.start()
-    ready = HEAD_CHUNKS - 2 + line + 2
-    lax.fori_loop(line + 4, ready + 1, lambda now, carry: (tick(now), carry)[1], 0)
+    ready = HEAD_CHUNKS - 2 + lag
+    lax.fori_loop(head_ticks, ready + 1, lambda now, carry: (tick(now), carry)[1], 0)
 
     def head_load(block, slot):
         return pltpu.make_async_copy(
@@ -627,7 +636,7 @@
     mixer_loads = [
         pltpu.make_async_copy(
             full.at[3 * cut_blocks + b],
-            feed_weight.at[:, :, :, :, pl.ds(b * CHUNK, CHUNK)],
+            feed_weight.at[0, :, :, :, :, pl.ds(b * CHUNK, CHUNK)],
             weight_sems.at[b],
         )
         for b in range(cut_blocks)
@@ -677,9 +686,9 @@
     for part in range(count):
         place = pl.ds(part * SEQ, SEQ)
         joined = jnp.concatenate([mixed[b, place] for b in range(cut_blocks)], axis=1)
-        per = 512 // (4 * feed_weight.shape[3])
+        per = 512 // (4 * feed_weight.shape[4])
         for piece in range(width // 512):
-            weight = feed_weight[pl.ds(piece * per, per), :, :, :, pl.ds(0, cut_blocks * CHUNK)]
+            weight = feed_weight[0, pl.ds(piece * per, per), :, :, :, pl.ds(0, cut_blocks * CHUNK)]
             outbox[place, pl.ds(piece * 512, 512)] = dot_nt(
                 joined, weight.reshape(512, cut_blocks * CHUNK)
             ).astype(jnp.bfloat16)
@@ -713,34 +722,52 @@
     lowered[...] = jnp.zeros_like(lowered)
     funnel_reduced[...] = jnp.zeros_like(funnel_reduced)
 
-    def feed_load(index):
+    def feed_load(index, slot, owner):
         return [
             pltpu.make_async_copy(
-                full.at[4 * cut_blocks + BLOCKS * index + b],
-                feed_weight.at[:, :, :, :, pl.ds(b * CHUNK, CHUNK)],
-                weight_sems.at[b],
+                full.at[4 * cut_blocks + BLOCKS * index + b, :, :, owner],
+                feed_weight.at[slot, :, :, owner, :, pl.ds(b * CHUNK, CHUNK)],
+                feed_sems.at[slot, owner, b],
             )
             for b in range(BLOCKS)
         ]
 
+    for load in feed_load(0, 0, core):
+        load.start()
     nothing = jnp.zeros((RANK, CHUNK), jnp.bfloat16)
 
     def feed(index, carry):
-        @pl.when(index >= EXTRA_TICKS)
+        now = index + HEAD_CHUNKS + lag
+        first = ready + 5
+        for early_step in range(EXTRA_TICKS):
+
+            @pl.when(index == 2 * early_step + 1)
+            def _(early_step=early_step):
+                tick(first + early_step)
+
+        @pl.when(now >= first + EXTRA_TICKS)
         def _():
-            tick(index + HEAD_CHUNKS + line + 2)
-
-        for load in feed_load(index):
+            tick(now)
+
+        slot = lax.rem(index, 2)
+        for load in feed_load(index, slot, 1 - core):
             load.start()
-        for load in feed_load(index):
-            load.wait()
+
+        @pl.when(index < chunks - HEAD_CHUNKS - 1)
+        def _():
+            for load in feed_load(index + 1, 1 - slot, core):
+                load.start()
+
+        for owner in (core, 1 - core):
+            for load in feed_load(index, slot, owner):
+                load.wait()
         columns = pl.ds(pl.multiple_of(index * CHUNK, CHUNK), CHUNK)
-        weight = feed_weight[:, :, :, :, pl.ds(0, 2 * CHUNK)].reshape(width, 2 * CHUNK)
+        weight = feed_weight[slot, :, :, :, :, pl.ds(0, 2 * CHUNK)].reshape(width, 2 * CHUNK)
         both = dot_nn(normed[...], weight)
         gate, lifted = both[:tokens, :CHUNK], both[:tokens, CHUNK:]
         gate_seen = both[tokens : tokens + RANK, :CHUNK]
         lifted_seen = both[tokens + RANK :, CHUNK:]
-        funnel = feed_weight[:, :, :, :, pl.ds(2 * CHUNK, CHUNK)].reshape(width, CHUNK)
+        funnel = feed_weight[slot, :, :, :, :, pl.ds(2 * CHUNK, CHUNK)].reshape(width, CHUNK)
         d_hidden = dot_nn(back[...], funnel)
         sigmoid = 1.0 / (1.0 + jnp.exp(-gate))
         silu = gate * sigmoid
@@ -777,11 +804,11 @@
             ],
             axis=0,
         )
-        per = 512 // (4 * feed_weight.shape[3])
+        per = 512 // (4 * feed_weight.shape[4])
         for piece in range(width // 512):
             near = pl.ds(piece * per, per)
-            funnel_rows = feed_weight[near, :, :, :, pl.ds(2 * CHUNK, CHUNK)]
-            gate_rows = feed_weight[near, :, :, :, pl.ds(0, 2 * CHUNK)]
+            funnel_rows = feed_weight[slot, near, :, :, :, pl.ds(2 * CHUNK, CHUNK)]
+            gate_rows = feed_weight[slot, near, :, :, :, pl.ds(0, 2 * CHUNK)]
             lanes = pl.ds(piece * 512, 512)
             funneled[:, lanes] += dot_nt(sources, funnel_rows.reshape(512, CHUNK))
             d_normed[:, lanes] += dot_nt(
@@ -843,7 +870,7 @@
         pltpu.VMEM((3 * cut_blocks, tokens, CHUNK), low),
         pltpu.VMEM((cut_blocks, tokens, CHUNK), low),
         pltpu.VMEM((2, line, 2, 2, height, CHUNK), low),
-        pltpu.VMEM((line, 2, 2, height, 4 * CHUNK), low),
+        pltpu.VMEM((2, line, 2, 2, height, 4 * CHUNK), low),
         pltpu.VMEM((tokens, width), full),
         pltpu.VMEM((tokens + 2 * RANK, width), full),
         pltpu.VMEM((tokens + RANK, width), full),
@@ -867,6 +894,7 @@
         pltpu.SemaphoreType.DMA((2, 2)),
         pltpu.SemaphoreType.DMA((4,)),
         pltpu.SemaphoreType.DMA((4,)),
+        pltpu.SemaphoreType.DMA((2, 2, BLOCKS)),
         pltpu.SemaphoreType.DMA((tokens // SEQ,)),
         pltpu.SemaphoreType.DMA((tokens // SEQ,)),
         pltpu.SemaphoreType.DMA((6,)),
@@ -914,9 +942,8 @@
     feed_dots_ref,
     feed_down_ref,
     feed_up_ref,
-    partial_out,
-    partial_other,
-    d_residual_out,
+    gradient_out,
+    block_out,
     funneled_out,
     total,
     norm_out,
@@ -930,6 +957,7 @@
     mixed,
     own,
     inbox,
+    last_inbox,
     funneled,
     attention,
     d_low,
@@ -943,12 +971,15 @@
     dots_out,
     side_box,
     norm_box,
+    kept_rows,
+    other_rows,
     load_sems,
     weight_sems,
     funnel_sems,
     side_sends,
     side_gets,
     out_sems,
+    kept_sems,
     *sum_refs,
 ):
     tokens, width = back.shape
@@ -1011,8 +1042,14 @@
     for load in loads[3:] + weight_loads:
         load.start()
     dots_copy = remote(dots_box.at[0], dots_box.at[1], count)
-    funneled_copy = remote(funneled_ref, funneled_out, count + 1)
-    partial_copy = remote(own, partial_other, count + 2)
+    funneled_copies = [
+        remote(funneled_ref.at[rows_of(part)], funneled_out.at[rows_of(part)], count + 1 + part)
+        for part in range(count)
+    ]
+    last_copies = [
+        remote(own.at[rows_of(part)], last_inbox.at[rows_of(part)], 2 * count + 1 + part)
+        for part in range(count)
+    ]
     norms = jnp.sqrt(squares_ref[...] + COLUMN_EPS)
     ratios = magnitudes_ref[...] / norms
     pulls = 1.0 / (norms * magnitudes_ref[...])
@@ -1067,9 +1104,15 @@
     for copy in part_copies[1:]:
         copy.start()
 
+    def funnel_lanes(block):
+        half = 0 if isinstance(block, int) else lax.rem(block, 2) * (CHUNK // 2)
+        return pl.ds(pl.multiple_of(half, CHUNK // 2), CHUNK // 2)
+
     def funnel_load(block, slot):
         return pltpu.make_async_copy(
-            full.at[4 * near + BLOCKS * block + 2], funnel_weight.at[slot], funnel_sems.at[slot]
+            full.at[4 * near + BLOCKS * lax.div(block, 2) + 2, :, :, :, :, funnel_lanes(block)],
+            funnel_weight.at[slot],
+            funnel_sems.at[slot],
         )
 
     funnel_load(0, 0).start()
@@ -1087,18 +1130,18 @@
     def correct(block, carry):
         slot = lax.rem(block, 2)
 
-        @pl.when(block < wide // CHUNK - 1)
+        @pl.when(block < 2 * wide // CHUNK - 1)
         def _():
             funnel_load(block + 1, 1 - slot).start()
 
         funnel_load(block, slot).wait()
-        columns = pl.ds(pl.multiple_of(block * CHUNK, CHUNK), CHUNK)
+        columns = pl.ds(pl.multiple_of(block * (CHUNK // 2), CHUNK // 2), CHUNK // 2)
         funnel_down[:, columns] = funnel_down_ref[:, columns] - ADAPTER_SCALE * dot_nn(
-            funnel_pull, funnel_weight[slot].reshape(width, CHUNK)
+            funnel_pull, funnel_weight[slot].reshape(width, CHUNK // 2)
         )
         return carry
 
-    lax.fori_loop(0, wide // CHUNK, correct, 0)
+    lax.fori_loop(0, 2 * wide // CHUNK, correct, 0)
     gathered[pl.ds(6 * RANK, RANK)] = ADAPTER_SCALE * (
         funnel_up_ref[...] * output_ratio[1]
         - funnel_seen_ref[...] * (output_pull[1] * funnel_dots)
@@ -1109,7 +1152,7 @@
     for part in range(count):
         part_copies[part].wait()
         if part == count - 1:
-            funneled_copy.start()
+            funneled_copies[0].start()
 
         def pull_back(index, carry, part=part):
             place = pl.ds(pl.multiple_of(part * SEQ + index * small, small), small)
@@ -1161,8 +1204,6 @@
             return carry
 
         lax.fori_loop(0, near, attend_back, 0)
-    d_residual_copy = pltpu.make_async_copy(residual, d_residual_out, out_sems.at[0])
-    d_residual_copy.start()
     per = 512 // (4 * weights.shape[4])
     for i in range(3):
         dots = []
@@ -1206,9 +1247,7 @@
         ).astype(jnp.bfloat16)
         for i in range(3):
             gathered[pl.ds(RANK * i, RANK), lanes] -= ADAPTER_SCALE * results[i][tokens:]
-    partial_copy.start()
-    partial_save = pltpu.make_async_copy(own, partial_out, out_sems.at[1])
-    partial_save.start()
+    last_copies[0].start()
     mixer_total = jnp.sum(mixer_dots[...], axis=0, keepdims=True)
     joined = jnp.concatenate([mixed[b] for b in range(near)], axis=1)
     low_output = (output_ref[0] * output_ratio[0]).astype(jnp.bfloat16)
@@ -1238,19 +1277,83 @@
     if row < dots_out.shape[0]:
         dots_out[row:] = jnp.zeros((dots_out.shape[0] - row, LANES), jnp.float32)
     offset = 3 * cut
-    for value in (feed_up_ref[0], feed_up_ref[1], mixer_down, funnel_down[...], dots_out[...]):
+    scales = dots_out[...] / magnitudes_ref[...]
+    for value in (feed_up_ref[0], feed_up_ref[1], mixer_down, funnel_down[...], scales):
         place_in(gathered, half_rows, offset, value)
         offset += value.shape[1]
     rest_columns = half_rows // RANK * width - offset
     place_in(gathered, half_rows, offset, jnp.zeros((RANK, rest_columns), jnp.float32))
+    def meanwhile():
+        for copy in last_copies[1:] + funneled_copies[1:]:
+            copy.start()
+
     sum_up(
-        size, sides, widths, offset, magnitudes_ref, total, norm_out, gathered, side_box, norm_box,
-        *sum_refs,
+        size, sides, widths, offset - LANES, total, norm_out, gathered, side_box, norm_box,
+        meanwhile, *sum_refs,
     )
-    d_residual_copy.wait()
-    partial_save.wait()
-    funneled_copy.wait()
-    partial_copy.wait()
+    tile = kept_rows.shape[1]
+    steps = SEQ // tile
+
+    def kept_loads(part, index, slot):
+        place = pl.ds(pl.multiple_of(part * SEQ + index * tile, tile), tile)
+        return [
+            pltpu.make_async_copy(residual_ref.at[place], kept_rows.at[slot], kept_sems.at[0, slot]),
+            pltpu.make_async_copy(funneled_out.at[place], other_rows.at[slot], kept_sems.at[1, slot]),
+        ]
+
+    gradient_copies = []
+    for part in range(count):
+        last_copies[part].wait()
+
+        def pull_rows(index, carry, part=part):
+            place = pl.ds(pl.multiple_of(part * SEQ + index * small, small), small)
+            value = floats[place].astype(jnp.float32)
+            weighted = gain_ref[0:1] * (
+                own[place].astype(jnp.float32) + last_inbox[place].astype(jnp.float32)
+            )
+            root = lax.rsqrt(jnp.mean(value * value, axis=1, keepdims=True) + NORM_EPS)
+            along = jnp.mean(value * weighted, axis=1, keepdims=True)
+            residual[place] += root * weighted - value * (root * root * root * along)
+            return carry
+
+        lax.fori_loop(0, SEQ // small, pull_rows, 0)
+        gradient_copies.append(
+            pltpu.make_async_copy(
+                residual.at[rows_of(part)], gradient_out.at[rows_of(part)], out_sems.at[part]
+            )
+        )
+        gradient_copies[-1].start()
+    for part in range(count):
+        funneled_copies[part].wait()
+        for load in kept_loads(part, 0, 0):
+            load.start()
+
+        def end_rows(index, carry, part=part):
+            slot = lax.rem(index, 2)
+
+            @pl.when(index < steps - 1)
+            def _():
+                for load in kept_loads(part, index + 1, 1 - slot):
+                    load.start()
+
+            for load in kept_loads(part, index, slot):
+                load.wait()
+            place = pl.ds(pl.multiple_of(part * SEQ + index * tile, tile), tile)
+            d_low[place] = (
+                kept_rows[slot]
+                + (funneled[place].astype(jnp.float32) + other_rows[slot].astype(jnp.float32))
+            ).astype(jnp.bfloat16)
+            return carry
+
+        lax.fori_loop(0, steps, end_rows, 0)
+        gradient_copies.append(
+            pltpu.make_async_copy(
+                d_low.at[rows_of(part)], block_out.at[rows_of(part)], out_sems.at[count + part]
+            )
+        )
+        gradient_copies[-1].start()
+    for copy in gradient_copies:
+        copy.wait()
 
 
 def run_tail(big, small):
@@ -1278,15 +1381,14 @@
         functools.partial(tail_kernel, size, sides, widths),
         name="tail",
         out_shape=(
+            jax.ShapeDtypeStruct((tokens, width), full_type),
             jax.ShapeDtypeStruct((tokens, width), low),
             jax.ShapeDtypeStruct((tokens, width), low),
-            jax.ShapeDtypeStruct((tokens, width), full_type),
-            jax.ShapeDtypeStruct((tokens, width), low),
-            jax.ShapeDtypeStruct((2 * rows, width), low),
+            jax.ShapeDtypeStruct((2 * rows + RANK, width), low),
             jax.ShapeDtypeStruct((8, 128), full_type),
         ),
         in_specs=[anywhere] * 10 + [local] * 16,
-        out_specs=[anywhere] * 4 + [local] * 2,
+        out_specs=[anywhere] * 3 + [local] * 2,
         scratch_shapes=[
             pltpu.VMEM((4, line, 2, 2, height, cut), low),
             pltpu.VMEM((tokens, width), full_type),
@@ -1299,10 +1401,11 @@
             pltpu.VMEM((tokens, width), low),
             pltpu.VMEM((tokens, width), low),
             pltpu.VMEM((tokens, width), low),
+            pltpu.VMEM((tokens, width), low),
             pltpu.VMEM((count, heads, SEQ, SEQ), full_type),
             pltpu.VMEM((tokens, width), low),
             pltpu.VMEM((3, tokens + RANK, cut), low),
-            pltpu.VMEM((2, line, 2, 2, height, CHUNK), low),
+            pltpu.VMEM((2, line, 2, 2, height, CHUNK // 2), low),
             pltpu.VMEM((2, 8, width), full_type),
             pltpu.VMEM((8, width), full_type),
             pltpu.VMEM((3 * RANK, width), low),
@@ -1311,12 +1414,15 @@
             pltpu.VMEM((lines, LANES), full_type),
             pltpu.VMEM((sides, rows, widths[-1]), low),
             pltpu.VMEM((sides, 8, 128), full_type),
+            pltpu.VMEM((2, 32, width), full_type),
+            pltpu.VMEM((2, 32, width), low),
             pltpu.SemaphoreType.DMA((9,)),
             pltpu.SemaphoreType.DMA((4 * near,)),
             pltpu.SemaphoreType.DMA((2,)),
-            pltpu.SemaphoreType.DMA((count + 3,)),
-            pltpu.SemaphoreType.DMA((count + 3,)),
-            pltpu.SemaphoreType.DMA((2,)),
+            pltpu.SemaphoreType.DMA((3 * count + 1,)),
+            pltpu.SemaphoreType.DMA((3 * count + 1,)),
+            pltpu.SemaphoreType.DMA((2 * count,)),
+            pltpu.SemaphoreType.DMA((2, 2)),
             *boxes,
             *boxes,
             pltpu.SemaphoreType.DMA((copies,)),
@@ -1358,13 +1464,13 @@
     size,
     sides,
     widths,
-    offset,
-    magnitude_ref,
+    scales_offset,
     total,
     norm_out,
     gathered,
     side_box,
     norm_box,
+    meanwhile,
     *rest,
 ):
     bits = len(widths)
@@ -1413,20 +1519,44 @@
             ].astype(jnp.float32)
     mine = pl.ds(pl.multiple_of(start, 128), width)
     side_box[0] = gathered[pl.ds(0, half), mine].astype(jnp.bfloat16)
+    split = gathered[pl.ds(half, half), mine].astype(jnp.bfloat16)
+    value = split.astype(jnp.float32)
+    group, lane = divmod(scales_offset, gathered.shape[1])
+    row = lax.broadcasted_iota(jnp.int32, value.shape, 0) - RANK * group
+    column = lax.broadcasted_iota(jnp.int32, value.shape, 1) + start - lane
+    both_hold = (row >= 0) & (row < 4) & (column >= 0) & (column < LANES)
+    norm_box[0] = jnp.full(
+        norm_box.shape[1:],
+        jnp.sum(jnp.where(both_hold, value * value / sides, value * value)),
+        jnp.float32,
+    )
+    copies = []
+    for step in range(1, sides):
+        where = {"tensor": lax.rem(side + step, sides)}
+        copies.append(remote(side_box.at[0], side_box.at[step], bits + 2 * step - 2, where))
+        copies.append(remote(norm_box.at[0], norm_box.at[step], bits + 2 * step - 1, where))
+    for copy in copies:
+        copy.start()
+    meanwhile()
+    for copy in copies:
+        copy.wait()
     shared = side_box[0].astype(jnp.float32)
+    squares = norm_box[0]
     for step in range(1, sides):
-        copy = remote(
-            side_box.at[0],
-            side_box.at[step],
-            bits + step - 1,
-            {"tensor": lax.rem(side + step, sides)},
-        )
-        copy.start()
-        copy.wait()
         shared += side_box[step].astype(jnp.float32)
-    total[pl.ds(0, half), mine] = shared.astype(jnp.bfloat16)
-    total[pl.ds(half, half), mine] = gathered[pl.ds(half, half), mine].astype(jnp.bfloat16)
-    index = bits + sides - 1
+        squares += norm_box[step]
+    shared = shared.astype(jnp.bfloat16)
+    total[pl.ds(0, half), mine] = shared
+    total[pl.ds(half, half), mine] = split
+    value = shared.astype(jnp.float32)
+    rest_of = jnp.full((1, width), jnp.sum(value * value)) + squares[0:1, 0:1]
+    pieces = []
+    for _ in range(3):
+        pieces.append(rest_of.astype(jnp.bfloat16))
+        rest_of = rest_of - pieces[-1].astype(jnp.float32)
+    pieces.append(jnp.zeros((RANK - 3, width), jnp.bfloat16))
+    total[pl.ds(2 * half, RANK), mine] = jnp.concatenate(pieces, axis=0)
+    index = bits + 2 * (sides - 1)
     for step, bit, width in reversed(marks):
         mine = pl.ds(pl.multiple_of(start, 128), width)
         copy = remote(
@@ -1436,36 +1566,9 @@
         copy.wait()
         index += 1
         start = start - bit * width
-    squares = jnp.zeros((RANK, 1), jnp.float32)
-    for row in range(0, half, RANK):
-        value = total[pl.ds(row, RANK)].astype(jnp.float32)
-        squares += jnp.sum(value * value, axis=1, keepdims=True)
-    dots_offset = offset - LANES
-    dots = take_from(total, half, dots_offset, LANES) / magnitude_ref[...]
-    dots = jnp.sum(dots * dots, axis=1, keepdims=True)
-    shared_total = jnp.sum(squares) + jnp.sum(dots[:4])
-    split_squares = jnp.zeros((RANK, 1), jnp.float32)
-    start = 0
-    while start < dots_offset:
-        count = min(dots_offset - start, gathered.shape[1])
-        value = take_from(total, half, start, count)
-        split_squares += jnp.sum(value * value, axis=1, keepdims=True)
-        start += count
-    split_total = jnp.sum(split_squares) + jnp.sum(dots[4:])
-    norm_box[0] = jnp.full(norm_box.shape[1:], split_total, jnp.float32)
-    for step in range(1, sides):
-        copy = remote(
-            norm_box.at[0],
-            norm_box.at[step],
-            index + step - 1,
-            {"tensor": lax.rem(side + step, sides)},
-        )
-        copy.start()
-        copy.wait()
-    split_sum = norm_box[0]
-    for step in range(1, sides):
-        split_sum = split_sum + norm_box[step]
-    norm_out[...] = jnp.sqrt(split_sum + shared_total)
+    pieces = total[pl.ds(2 * half, RANK)].astype(jnp.float32)
+    norm = jnp.sqrt(jnp.sum(pieces) / widths[-1])
+    norm_out[...] = jnp.full(norm_out.shape, norm, jnp.float32)
 
 
 def update_kernel(*refs):
@@ -1473,7 +1576,7 @@
     values, firsts, seconds = refs[2:11], refs[11:20], refs[20:29]
     fresh, momenta, variances = refs[29:38], refs[38:47], refs[47:56]
     factor = jnp.minimum(1.0, CLIP / (norm_ref[0:1, 0:1] + 1e-06))
-    half = total.shape[0] // 2
+    half = total.shape[0] // 2 - RANK // 2
     cut, wide = values[1].shape[2], values[2].shape[2]
 
     def update(index, rate, piece, gradient):
@@ -1513,14 +1616,14 @@
     width = total.shape[1]
     for i in range(2):
         piece = slice(i, i + 1)
-        update(8, RATE_LOUD, piece, long(2 * i, width) / values[8][piece])
+        update(8, RATE_LOUD, piece, long(2 * i, width))
     for i in range(3):
         piece = slice(i, i + 1)
-        update(6, RATE_SCALE, piece, long(4 + i, cut) / values[6][piece])
+        update(6, RATE_SCALE, piece, long(4 + i, cut))
     lines = -(-wide // LANES)
     for i in range(2):
         piece = slice(i, i + 1)
-        update(7, RATE_SCALE, piece, long(7 + lines * i, wide) / values[7][piece])
+        update(7, RATE_SCALE, piece, long(7 + lines * i, wide))
 
 
 def update_all(total, norm, params, firsts, seconds):
@@ -1663,7 +1766,7 @@
             magnitudes,
         ),
     )
-    partial, partial_other, d_residual, funneled_other, total, norm = run_tail(
+    input_gradient, block_output, _, total, norm = run_tail(
         (
             full,
             turned,
@@ -1704,13 +1807,6 @@
     results = update_all(total, norm, turned_over(params), turned_over(firsts), turned_over(seconds))
     updated, momenta, variances = (turned_over(results[i : i + 9]) for i in (0, 9, 18))
     gradient_norm = norm[0, 0]
-    block_output = low(
-        residual + (funneled.astype(jnp.float32) + funneled_other.astype(jnp.float32))
-    )
-    floats = activations.astype(jnp.float32)
-    d_normed_one = partial.astype(jnp.float32) + partial_other.astype(jnp.float32)
-    unused, first_pull = jax.vjp(lambda v: root_norm(v, norm_gains[0]), floats)
-    input_gradient = d_residual + first_pull(d_normed_one)[0]
     return (
         block_output,
         input_gradient,

time: 545 us -> 510 us (0.936)
  Pallas kernels: 520 us -> 489 us
  other arithmetic: 14.6 us -> 2.49 us
    pallas_call x1, Pallas kernels: 165 us -> 150 us  [run_tail(): pl.pallas_call(functools.partial(tail_kernel, size, sides, widths), name=...]
    pallas_call x1, Pallas kernels: 319 us -> 304 us  [run_block(): pl.pallas_call(functools.partial(block_kernel, size), name='block', out_s...]
    add x1 -> x0, other arithmetic: 5.72 us -> none  [body(): input_gradient = d_residual + first_pull(d_normed_one)[0]]
where the time goes in v6:
time: 510 us; the launch traced here: 502 us
  Pallas kernels  489 us (96%)
  local copies, waits for them, and re-layouts  9.24 us (2%)
    pallas_call x1, Pallas kernels, run_block(): pl.pallas_call(functools.partial(block_kernel, size), name='block', out_s...  304 us
    pallas_call x1, Pallas kernels, run_tail(): pl.pallas_call(functools.partial(tail_kernel, size, sides, widths), name=...  150 us
    pallas_call x1, Pallas kernels, merge(): pl.pallas_call(functools.partial(merge_kernel, size, sides), name='merge'...  29.3 us

profile of v6, /device:TPU:0, one launch (start us, length us, event | category | flops | bytes accessed | tf_op | source)
XLA Modules:
  0.0 501.7 jit_solution(13169978503518734261)
XLA Ops:
  0.7 0.7 convert_element_type.10
  1.4 1.3 constant_dynamic-slice_fusion.output_ref
  2.7 1.4 dynamic-slice_bitcast_fusion.entry_ref
  4.1 1.8 fusion
  5.9 29.3 %merge.1 = (bf16[49,128,256]{2,1,0:T(8,128)(2,1)}, f32[16,1024]{1,0:T(8,128)}, f32[16,1024]{1,0:T(8,128)}) custom-call(bf16[128,1024]{1,0:T(8,128)(2,1)} %query_ref.1, bf16[128,1024]{1,0:T(8,128)(2,1)} %key_ref.1, bf16[128,1024]{1,0:T(8,128)(2,1)} %value_ref.1, bf16[128,2816]{1,0:T(8,128)(2,1)} %gate_ref.1, bf16[128,2816]{1,0:T(8,128)(2,1)} %widen_ref.1, ...), custom_call_target="tpu_custom_call" | custom-call | tf_op jit(solution)/shard_map/merge/pallas_call | solution.py:222
  35.2 303.7 %block.1 = (bf16[49,4,2,2,128,256]{5,4,3,2,1,0:T(8,128)(2,1)}, bf16[512,2048]{1,0:T(8,128)(2,1)}, bf16[12,512,256]{2,1,0:T(8,128)(2,1)}, bf16[8,512,256]{2,1,0:T...) custom-call(bf16[49,128,256]{2,1,0:T(8,128)(2,1)} %get-tuple-element, ...), custom_call_target="tpu_custom_call" | custom-call | tf_op jit(solution)/shard_map/block/pallas_call | solution.py:902
  338.9 149.8 %tail.1 = (f32[512,2048]{1,0:T(8,128)}, bf16[512,2048]{1,0:T(8,128)(2,1)}, bf16[512,2048]{1,0:T(8,128)(2,1)}, bf16[240,2048]{1,0:T(8,128)(2,1)}, f32[8,128]{1,0:T(8,128)}) custom-call(bf16[49,4,2,2,128,256]{5,4,3,2,1,0:T(8,128)(2,1)} %get-tuple-element.81.full, bf16[12,512,256]{2,1,0:T(8,128)(2,1)} %get-tuple-element.82.turned_ref, ...), custom_call_target="tpu_custom_call" | custom-call | tf_op jit(solution)/shard_map/tail/pallas_call | solution.py:1380
  488.8 1.2 slice.3
  490.0 5.9 %update.1 = (f32[5,16,2048]{2,1,0:T(8,128)}, f32[3,16,1024]{2,1,0:T(8,128)}, f32[2,16,2816]{2,1,0:T(8,128)}, f32[16,1024]{1,0:T(8,128)}, f32[16,2816]{1,0:T(8,12...) custom-call(bf16[240,2048]{1,0:T(8,128)(2,1)} %get-tuple-element.98., ...), custom_call_target="tpu_custom_call" | custom-call | tf_op jit(solution)/shard_map/update/pallas_call | solution.py:1631
  495.9 0.0 copy-start
  495.9 3.3 copy.71
  499.2 0.0 copy-done
  499.2 2.0 copy.72
  (1 shorter events, 0.0 us)
Async XLA Ops:
  495.9 3.3 copy-start

commit v7 on v6

--- a/solution.py
+++ b/solution.py
@@ -44,6 +44,23 @@
 CHUNK = 256
 
 
+def staged(kernel, before, inside):
+    def run(*refs):
+        sources, boxes, sems = refs[before : before + inside], refs[-inside - 1 : -1], refs[-1]
+        copies = [
+            pltpu.make_async_copy(source, box, sems.at[i])
+            for i, (source, box) in enumerate(zip(sources, boxes))
+        ]
+        kernel(copies, *refs[:before], *boxes, *refs[before + inside : -inside - 1])
+
+    return run
+
+
+def stage_of(operands):
+    boxes = [pltpu.VMEM(operand.shape, operand.dtype) for operand in operands]
+    return boxes + [pltpu.SemaphoreType.DMA((len(operands),))]
+
+
 def partners_of(size):
     me = lax.axis_index("dp")
     found = []
@@ -89,6 +106,7 @@
 def merge_kernel(
     size,
     sides,
+    copies,
     query_ref,
     key_ref,
     value_ref,
@@ -117,7 +135,11 @@
     sends,
     receives,
 ):
+    for copy in copies:
+        copy.start()
     greet_sum(size, sides)
+    for copy in copies:
+        copy.wait()
     rows = query_ref.shape[0]
     wide = gate_ref.shape[1]
     me = lax.axis_index("dp")
@@ -219,15 +241,16 @@
     wide = bases[3].shape[1]
     steps = len(bin(size)) - 3 + sides - 1
     lines = 16
+    operands = (*bases, entry_rows, attend, widen, mixer_down, funnel_down, output_columns, *scales)
     return pl.pallas_call(
-        functools.partial(merge_kernel, size, sides),
+        staged(functools.partial(merge_kernel, size, sides), 0, len(operands)),
         name="merge",
         out_shape=(
             jax.ShapeDtypeStruct(((4 * cut + 3 * wide) // CHUNK, rows, CHUNK), jnp.bfloat16),
             jax.ShapeDtypeStruct((lines, LANES), jnp.float32),
             jax.ShapeDtypeStruct((lines, LANES), jnp.float32),
         ),
-        in_specs=[pl.BlockSpec(memory_space=pltpu.VMEM)] * 16,
+        in_specs=[pl.BlockSpec(memory_space=pl.ANY)] * len(operands),
         out_specs=[pl.BlockSpec(memory_space=pltpu.VMEM)] * 3,
         scratch_shapes=[
             pltpu.VMEM((lines, LANES), jnp.float32),
@@ -238,11 +261,12 @@
             pltpu.VMEM((wide, rows), jnp.float32),
             pltpu.SemaphoreType.DMA((steps,)),
             pltpu.SemaphoreType.DMA((steps,)),
+            *stage_of(operands),
         ],
         compiler_params=pltpu.CompilerParams(
             collective_id=0, has_side_effects=True, vmem_limit_bytes=VMEM
         ),
-    )(*bases, entry_rows, attend, widen, mixer_down, funnel_down, output_columns, *scales)
+    )(*operands)
 
 
 def dot_nn(left, right):
@@ -262,7 +286,7 @@
 
 BLOCKS = 3
 HEAD_CHUNKS = 5
-EXTRA_TICKS = 2
+EXTRA_TICKS = 3
 
 
 def gather_parts(size, shard, full, sems):
@@ -424,9 +448,10 @@
 
 def block_kernel(
     size,
-    shard,
+    copies,
     rows_ref,
     back_ref,
+    shard,
     cosine_ref,
     sine_ref,
     keep_ref,
@@ -444,6 +469,7 @@
     mixed_out,
     residual_out,
     d_normed_out,
+    d_normed_other,
     funneled_out,
     up_out,
     down_out,
@@ -523,8 +549,9 @@
             fast[now](chunks, 0, 1)
             fast[now](0, 1, BLOCKS)
 
+    for copy in copies:
+        copy.start()
     own = pltpu.make_async_copy(shard, full.at[:, spot, column, core], local_sems.at[0])
-    own.start()
     loads = [
         pltpu.make_async_copy(rows_ref, floats, local_sems.at[1]),
         pltpu.make_async_copy(back_ref, back, local_sems.at[2]),
@@ -532,15 +559,17 @@
     for load in loads:
         load.start()
     greet()
+    copies[0].wait()
     early_start()
     send_own((0,), chunks, 0, 1)
     send_own((0,), 0, 1, BLOCKS)
+    own.start()
     own.wait()
     early_wait(0)
     send_own((1,), chunks, 0, 1)
     send_own((1,), 0, 1, BLOCKS)
     early_wait(1)
-    for load in loads:
+    for load in loads + copies[1:]:
         load.wait()
     tile = 32
 
@@ -712,6 +741,7 @@
         lax.fori_loop(0, SEQ // tile, add_up, 0)
         if part == 0:
             tick(ready + 4)
+            tick(ready + 5)
     outs.append(pltpu.make_async_copy(residual, residual_out, out_sems.at[3]))
     outs[-1].start()
     reduced[...] = dot_nt(normed[pl.ds(tokens, 2 * RANK)], normed[pl.ds(0, tokens)]).astype(
@@ -735,10 +765,18 @@
     for load in feed_load(0, 0, core):
         load.start()
     nothing = jnp.zeros((RANK, CHUNK), jnp.bfloat16)
+    ahead_copy = pltpu.make_async_remote_copy(
+        src_ref=outbox.at[:, pl.ds(0, 512)],
+        dst_ref=d_normed_other,
+        send_sem=side_sends.at[count],
+        recv_sem=side_gets.at[count],
+        device_id=sides,
+        device_id_type=MESH,
+    )
 
     def feed(index, carry):
         now = index + HEAD_CHUNKS + lag
-        first = ready + 5
+        first = ready + 6
         for early_step in range(EXTRA_TICKS):
 
             @pl.when(index == 2 * early_step + 1)
@@ -806,18 +844,31 @@
         )
         per = 512 // (4 * feed_weight.shape[4])
         for piece in range(width // 512):
-            near = pl.ds(piece * per, per)
-            funnel_rows = feed_weight[slot, near, :, :, :, pl.ds(2 * CHUNK, CHUNK)]
-            gate_rows = feed_weight[slot, near, :, :, :, pl.ds(0, 2 * CHUNK)]
+            gate_rows = feed_weight[slot, pl.ds(piece * per, per), :, :, :, pl.ds(0, 2 * CHUNK)]
             lanes = pl.ds(piece * 512, 512)
-            funneled[:, lanes] += dot_nt(sources, funnel_rows.reshape(512, CHUNK))
             d_normed[:, lanes] += dot_nt(
                 gradients, gate_rows.reshape(512, 2 * CHUNK)
             )
+            if piece == 0:
+
+                @pl.when(index == chunks - HEAD_CHUNKS - 1)
+                def _():
+                    outbox[:, pl.ds(0, 512)] = d_normed[pl.ds(0, tokens), pl.ds(0, 512)].astype(
+                        jnp.bfloat16
+                    )
+                    ahead_copy.start()
+
+        for piece in range(width // 512):
+            funnel_rows = feed_weight[
+                slot, pl.ds(piece * per, per), :, :, :, pl.ds(2 * CHUNK, CHUNK)
+            ]
+            lanes = pl.ds(piece * 512, 512)
+            funneled[:, lanes] += dot_nt(sources, funnel_rows.reshape(512, CHUNK))
         return carry
 
     lax.fori_loop(0, chunks - HEAD_CHUNKS, feed, 0)
-    outbox[...] = d_normed[pl.ds(0, tokens)].astype(jnp.bfloat16)
+    late = pl.ds(512, width - 512)
+    outbox[:, late] = d_normed[pl.ds(0, tokens), late].astype(jnp.bfloat16)
     outs.append(pltpu.make_async_copy(outbox, d_normed_out, out_sems.at[4]))
     outs[-1].start()
     down_out[...] = ADAPTER_SCALE * (
@@ -832,6 +883,7 @@
     finish(chunks - 1, 1 + BLOCKS * (chunks - 1), BLOCKS)
     for out in outs:
         out.wait()
+    ahead_copy.wait()
 
 
 def run_block(shard, rows, back, small):
@@ -854,6 +906,7 @@
         jax.ShapeDtypeStruct((cut_blocks, tokens, CHUNK), low),
         jax.ShapeDtypeStruct((tokens, width), full),
         jax.ShapeDtypeStruct((tokens, width), low),
+        jax.ShapeDtypeStruct((tokens, 512), low),
         jax.ShapeDtypeStruct((tokens, width), low),
         jax.ShapeDtypeStruct((2, RANK, wide), full),
         jax.ShapeDtypeStruct((2 * RANK, width), full),
@@ -895,33 +948,36 @@
         pltpu.SemaphoreType.DMA((4,)),
         pltpu.SemaphoreType.DMA((4,)),
         pltpu.SemaphoreType.DMA((2, 2, BLOCKS)),
-        pltpu.SemaphoreType.DMA((tokens // SEQ,)),
-        pltpu.SemaphoreType.DMA((tokens // SEQ,)),
+        pltpu.SemaphoreType.DMA((tokens // SEQ + 1,)),
+        pltpu.SemaphoreType.DMA((tokens // SEQ + 1,)),
         pltpu.SemaphoreType.DMA((6,)),
+        *stage_of((shard, *small)),
     ]
     return pl.pallas_call(
-        functools.partial(block_kernel, size),
+        staged(functools.partial(block_kernel, size), 2, 1 + len(small)),
         name="block",
         out_shape=out_shape,
-        in_specs=[local] + [anywhere] * 2 + [local] * 10,
-        out_specs=[anywhere] * 8 + [local] * 6,
+        in_specs=[anywhere] * (3 + len(small)),
+        out_specs=[anywhere] * 9 + [local] * 6,
         scratch_shapes=scratch,
         compiler_params=pltpu.CompilerParams(
             collective_id=1, has_side_effects=True, vmem_limit_bytes=VMEM
         ),
-    )(shard, rows, back, *small)
+    )(rows, back, shard, *small)
 
 
 def tail_kernel(
     size,
     sides,
     widths,
+    copies,
     full,
     turned_ref,
     plain_ref,
     mixed_ref,
     residual_ref,
     d_normed_ref,
+    d_normed_other,
     funneled_ref,
     back_ref,
     rows_ref,
@@ -1005,6 +1061,7 @@
                 (rows_ref, floats),
                 (mixed_ref, mixed),
                 (plain_ref, plain),
+                (d_normed_other, inbox.at[:, pl.ds(0, 512)]),
             )
         )
     ]
@@ -1017,7 +1074,7 @@
         for i in range(4)
         for b in range(near)
     ]
-    for load in loads[:3]:
+    for load in loads[:3] + copies:
         load.start()
     greet_sum(size, sides)
 
@@ -1035,7 +1092,11 @@
         return pl.ds(part * SEQ, SEQ)
 
     part_copies = [
-        remote(d_normed_ref.at[rows_of(part)], inbox.at[rows_of(part)], part)
+        remote(
+            d_normed_ref.at[rows_of(part), pl.ds(512, width - 512)],
+            inbox.at[rows_of(part), pl.ds(512, width - 512)],
+            part,
+        )
         for part in range(count)
     ]
     part_copies[0].start()
@@ -1050,6 +1111,8 @@
         remote(own.at[rows_of(part)], last_inbox.at[rows_of(part)], 2 * count + 1 + part)
         for part in range(count)
     ]
+    for copy in copies:
+        copy.wait()
     norms = jnp.sqrt(squares_ref[...] + COLUMN_EPS)
     ratios = magnitudes_ref[...] / norms
     pulls = 1.0 / (norms * magnitudes_ref[...])
@@ -1378,7 +1441,7 @@
     boxes = [pltpu.VMEM((2 * rows, w), low) for w in widths]
     copies = bits + halvings + 2 * (sides - 1)
     return pl.pallas_call(
-        functools.partial(tail_kernel, size, sides, widths),
+        staged(functools.partial(tail_kernel, size, sides, widths), len(big), len(small)),
         name="tail",
         out_shape=(
             jax.ShapeDtypeStruct((tokens, width), full_type),
@@ -1387,7 +1450,7 @@
             jax.ShapeDtypeStruct((2 * rows + RANK, width), low),
             jax.ShapeDtypeStruct((8, 128), full_type),
         ),
-        in_specs=[anywhere] * 10 + [local] * 16,
+        in_specs=[anywhere] * (len(big) + len(small)),
         out_specs=[anywhere] * 3 + [local] * 2,
         scratch_shapes=[
             pltpu.VMEM((4, line, 2, 2, height, cut), low),
@@ -1416,7 +1479,7 @@
             pltpu.VMEM((sides, 8, 128), full_type),
             pltpu.VMEM((2, 32, width), full_type),
             pltpu.VMEM((2, 32, width), low),
-            pltpu.SemaphoreType.DMA((9,)),
+            pltpu.SemaphoreType.DMA((10,)),
             pltpu.SemaphoreType.DMA((4 * near,)),
             pltpu.SemaphoreType.DMA((2,)),
             pltpu.SemaphoreType.DMA((3 * count + 1,)),
@@ -1427,6 +1490,7 @@
             *boxes,
             pltpu.SemaphoreType.DMA((copies,)),
             pltpu.SemaphoreType.DMA((copies,)),
+            *stage_of(small),
         ],
         compiler_params=pltpu.CompilerParams(
             collective_id=2, has_side_effects=True, vmem_limit_bytes=VMEM
@@ -1574,7 +1638,13 @@
 def update_kernel(*refs):
     total, norm_ref = refs[:2]
     values, firsts, seconds = refs[2:11], refs[11:20], refs[20:29]
-    fresh, momenta, variances = refs[29:38], refs[38:47], refs[47:56]
+    fresh, momenta, variances = refs[31:40], refs[40:49], refs[49:58]
+    norm_out, boxes, sems = refs[60], refs[61:63], refs[63]
+    ins = [pltpu.make_async_copy(refs[29 + i], boxes[i], sems.at[i]) for i in range(2)]
+    outs = [pltpu.make_async_copy(boxes[i], refs[58 + i], sems.at[2 + i]) for i in range(2)]
+    for copy in ins:
+        copy.start()
+    norm_out[...] = norm_ref[0:1, 0:1]
     factor = jnp.minimum(1.0, CLIP / (norm_ref[0:1, 0:1] + 1e-06))
     half = total.shape[0] // 2 - RANK // 2
     cut, wide = values[1].shape[2], values[2].shape[2]
@@ -1592,6 +1662,9 @@
 
     for i in range(5):
         update(0, RATE_FACTOR, i, shared(i))
+    for i in range(2):
+        ins[i].wait()
+        outs[i].start()
     for i in range(2):
         update(5, RATE_LIFT, i, shared(5 + i))
     offset = 0
@@ -1624,18 +1697,27 @@
     for i in range(2):
         piece = slice(i, i + 1)
         update(7, RATE_SCALE, piece, long(7 + lines * i, wide))
-
-
-def update_all(total, norm, params, firsts, seconds):
+    for copy in outs:
+        copy.wait()
+
+
+def update_all(total, norm, params, firsts, seconds, large):
     shapes = tuple(jax.ShapeDtypeStruct(p.shape, p.dtype) for p in params)
+    large_shapes = tuple(jax.ShapeDtypeStruct(p.shape, p.dtype) for p in large)
+    anywhere = pl.BlockSpec(memory_space=pl.ANY)
+    local = pl.BlockSpec(memory_space=pltpu.VMEM)
     return pl.pallas_call(
         update_kernel,
         name="update",
-        out_shape=shapes * 3,
-        in_specs=[pl.BlockSpec(memory_space=pltpu.VMEM)] * 29,
-        out_specs=[pl.BlockSpec(memory_space=pltpu.VMEM)] * 27,
+        out_shape=shapes * 3 + large_shapes + (jax.ShapeDtypeStruct((1, 1), jnp.float32),),
+        in_specs=[local] * 29 + [anywhere] * 2,
+        out_specs=[local] * 27 + [anywhere] * 2 + [local],
+        scratch_shapes=[
+            *(pltpu.VMEM(p.shape, p.dtype) for p in large),
+            pltpu.SemaphoreType.DMA((4,)),
+        ],
         compiler_params=pltpu.CompilerParams(vmem_limit_bytes=VMEM),
-    )(total, norm, *params, *firsts, *seconds)
+    )(total, norm, *params, *firsts, *seconds, *large)
 
 
 def body(
@@ -1742,6 +1824,7 @@
         mixed,
         residual,
         d_normed_two,
+        d_normed_other,
         funneled,
         feed_ups,
         feed_downs,
@@ -1774,6 +1857,7 @@
             mixed,
             residual,
             d_normed_two,
+            d_normed_other,
             funneled,
             cotangent,
             activations,
@@ -1804,9 +1888,17 @@
             jnp.swapaxes(item, -1, -2) if i in (0, 3, 4) else item for i, item in enumerate(items)
         ]
 
-    results = update_all(total, norm, turned_over(params), turned_over(firsts), turned_over(seconds))
+    results = update_all(
+        total,
+        norm,
+        turned_over(params),
+        turned_over(firsts),
+        turned_over(seconds),
+        (input_gradient, block_output),
+    )
+    input_gradient, block_output, gradient_norm = results[27:]
     updated, momenta, variances = (turned_over(results[i : i + 9]) for i in (0, 9, 18))
-    gradient_norm = norm[0, 0]
+    gradient_norm = gradient_norm.reshape(())
     return (
         block_output,
         input_gradient,

time: 510 us -> 496 us (0.973)
  local copies, waits for them, and re-layouts: 9.24 us -> 2.72 us
  Pallas kernels: 489 us -> 483 us
    pallas_call x4, Pallas kernels: 489 us -> 483 us  [the longest x1 302 us: run_block(): pl.pallas_call(staged(functools.partial(block_kernel, size), 2, 1 + len(s...]
    unnamed x4 -> x0, local copies, waits for them, and re-layouts: 5.33 us -> none
where the time goes in v7:
time: 496 us; the launch traced here: 490 us
  Pallas kernels  483 us (97%)
    pallas_call x1, Pallas kernels, run_block(): pl.pallas_call(staged(functools.partial(block_kernel, size), 2, 1 + len(s...  302 us
    pallas_call x1, Pallas kernels, run_tail(): pl.pallas_call(staged(functools.partial(tail_kernel, size, sides, widths)...  141 us
    pallas_call x1, Pallas kernels, merge(): pl.pallas_call(staged(functools.partial(merge_kernel, size, sides), 0, le...  29.3 us
    pallas_call x1, Pallas kernels, update_all(): pl.pallas_call(update_kernel, name='update', out_shape=shapes * 3 + large...  10.3 us

profile of v7, /device:TPU:0, one launch (start us, length us, event | category | flops | bytes accessed | tf_op | source)
XLA Modules:
  0.0 489.6 jit_solution(3322655194376846294)
XLA Ops:
  0.7 0.7 convert_element_type.10
  1.4 1.3 constant_dynamic-slice_fusion.refs_12_
  2.7 1.4 dynamic-slice_bitcast_fusion.refs_7_
  4.1 1.8 fusion
  5.9 29.3 %merge.1 = (bf16[49,128,256]{2,1,0:T(8,128)(2,1)}, f32[16,1024]{1,0:T(8,128)}, f32[16,1024]{1,0:T(8,128)}) custom-call(bf16[128,1024]{1,0:T(8,128)(2,1)} %refs_0_.2, bf16[128,1024]{1,0:T(8,128)(2,1)} %refs_1_.2, bf16[128,1024]{1,0:T(8,128)(2,1)} %refs_2_.1, bf16[128,2816]{1,0:T(8,128)(2,1)} %refs_3_.2, bf16[128,2816]{1,0:T(8,128)(2,1)} %refs_4_.2, ...), custom_call_target="tpu_custom_call" | custom-call | tf_op jit(solution)/shard_map/merge/pallas_call | solution.py:245
  35.2 302.0 %block.1 = (bf16[49,4,2,2,128,256]{5,4,3,2,1,0:T(8,128)(2,1)}, bf16[512,2048]{1,0:T(8,128)(2,1)}, bf16[12,512,256]{2,1,0:T(8,128)(2,1)}, bf16[8,512,256]{2,1,0:T...) custom-call(bf16[512,2048]{1,0:T(8,128)(2,1)} %refs_9_.6, ...), custom_call_target="tpu_custom_call" | custom-call | tf_op jit(solution)/shard_map/block/pallas_call | solution.py:956
  337.3 141.5 %tail.1 = (f32[512,2048]{1,0:T(8,128)}, bf16[512,2048]{1,0:T(8,128)(2,1)}, bf16[512,2048]{1,0:T(8,128)(2,1)}, bf16[240,2048]{1,0:T(8,128)(2,1)}, f32[8,128]{1,0:T(8,128)}) custom-call(bf16[49,4,2,2,128,256]{5,4,3,2,1,0:T(8,128)(2,1)} %get-tuple-element.85.refs_0_, bf16[12,512,256]{2,1,0:T(8,128)(2,1)} %get-tuple-element.86.refs_1_, ...), custom_call_target="tpu_custom_call" | custom-call | tf_op jit(solution)/shard_map/tail/pallas_call | solution.py:1443
  478.7 10.3 %update.1 = (f32[5,16,2048]{2,1,0:T(8,128)}, f32[3,16,1024]{2,1,0:T(8,128)}, f32[2,16,2816]{2,1,0:T(8,128)}, f32[16,1024]{1,0:T(8,128)}, f32[16,2816]{1,0:T(8,12...) custom-call(bf16[240,2048]{1,0:T(8,128)(2,1)} %get-tuple-element.100, ...), custom_call_target="tpu_custom_call" | custom-call | tf_op jit(solution)/shard_map/update/pallas_call | solution.py:1709
  (1 shorter events, 0.0 us)

commit v8 on v7

--- a/solution.py
+++ b/solution.py
@@ -44,11 +44,11 @@
 CHUNK = 256
 
 
-def staged(kernel, before, inside):
+def staged(kernel, before, inside, view=None):
     def run(*refs):
         sources, boxes, sems = refs[before : before + inside], refs[-inside - 1 : -1], refs[-1]
         copies = [
-            pltpu.make_async_copy(source, box, sems.at[i])
+            pltpu.make_async_copy(view(i, source) if view else source, box, sems.at[i])
             for i, (source, box) in enumerate(zip(sources, boxes))
         ]
         kernel(copies, *refs[:before], *boxes, *refs[before + inside : -inside - 1])
@@ -56,8 +56,12 @@
     return run
 
 
-def stage_of(operands):
-    boxes = [pltpu.VMEM(operand.shape, operand.dtype) for operand in operands]
+def stage_of(operands, shapes=()):
+    shapes = dict(shapes)
+    boxes = [
+        pltpu.VMEM(shapes.get(i, operand.shape), operand.dtype)
+        for i, operand in enumerate(operands)
+    ]
     return boxes + [pltpu.SemaphoreType.DMA((len(operands),))]
 
 
@@ -234,16 +238,29 @@
                 shard_out[4 * near + 3 * (start // CHUNK) + 2] = part
 
 
-def merge(bases, entry_rows, attend, widen, mixer_down, funnel_down, output_columns, scales):
+def merge(bases, entry, attend, widen, mixer_down, funnel_down, output, scales):
     size = lax.axis_size("dp")
     sides = lax.axis_size("tensor")
     rows, cut = bases[0].shape
     wide = bases[3].shape[1]
     steps = len(bin(size)) - 3 + sides - 1
     lines = 16
-    operands = (*bases, entry_rows, attend, widen, mixer_down, funnel_down, output_columns, *scales)
+    shapes = {7: (*entry.shape[:2], rows), 12: (*output.shape[:2], rows)}
+    direct = rows % 128 == 0
+    if not direct:
+        place = lax.axis_index("dp") * rows
+        entry, output = (
+            lax.dynamic_slice_in_dim(item, place, rows, 2) for item in (entry, output)
+        )
+    operands = (*bases, entry, attend, widen, mixer_down, funnel_down, output, *scales)
+
+    def view(index, ref):
+        if not direct or index not in shapes:
+            return ref
+        return ref.at[:, :, pl.ds(pl.multiple_of(lax.axis_index("dp") * rows, 128), rows)]
+
     return pl.pallas_call(
-        staged(functools.partial(merge_kernel, size, sides), 0, len(operands)),
+        staged(functools.partial(merge_kernel, size, sides), 0, len(operands), view),
         name="merge",
         out_shape=(
             jax.ShapeDtypeStruct(((4 * cut + 3 * wide) // CHUNK, rows, CHUNK), jnp.bfloat16),
@@ -261,7 +278,7 @@
             pltpu.VMEM((wide, rows), jnp.float32),
             pltpu.SemaphoreType.DMA((steps,)),
             pltpu.SemaphoreType.DMA((steps,)),
-            *stage_of(operands),
+            *stage_of(operands, shapes),
         ],
         compiler_params=pltpu.CompilerParams(
             collective_id=0, has_side_effects=True, vmem_limit_bytes=VMEM
@@ -452,8 +469,8 @@
     rows_ref,
     back_ref,
     shard,
-    cosine_ref,
-    sine_ref,
+    positions_ref,
+    frequency_ref,
     keep_ref,
     gain_ref,
     entry_ref,
@@ -463,6 +480,8 @@
     squares_ref,
     magnitudes_ref,
     full,
+    cosine_out,
+    sine_out,
     normed_out,
     turned_out,
     plain_out,
@@ -499,6 +518,8 @@
     ratio_ref,
     pull_ref,
     funnel_down_ref,
+    cosine_ref,
+    sine_ref,
     right_sends,
     left_sends,
     right_gets,
@@ -581,6 +602,18 @@
         return carry
 
     def prepare():
+        first_row = lax.broadcasted_iota(jnp.int32, (RANK, tokens), 0) == 0
+        places = jnp.where(first_row, positions_ref[...].astype(jnp.float32), 0.0)
+        angles = lax.dot_general(
+            places,
+            jnp.broadcast_to(frequency_ref[...], (RANK, HEAD_DIM)),
+            (((0,), (0,)), ((), ())),
+            precision=HIGH_PRECISION,
+            preferred_element_type=jnp.float32,
+        )
+        lane = lax.broadcasted_iota(jnp.int32, angles.shape, 1)
+        cosine_ref[...] = jnp.cos(angles)
+        sine_ref[...] = jnp.where(lane < HEAD_DIM // 2, -1.0, 1.0) * jnp.sin(angles)
         lax.fori_loop(0, tokens // tile, norm_rows, 0)
         norms = jnp.sqrt(squares_ref[...] + COLUMN_EPS)
         ratios = magnitudes_ref[...] / norms
@@ -655,6 +688,8 @@
 
     lax.fori_loop(0, 3 * cut_blocks, project, 0)
     outs = [
+        pltpu.make_async_copy(cosine_ref, cosine_out, out_sems.at[6]),
+        pltpu.make_async_copy(sine_ref, sine_out, out_sems.at[7]),
         pltpu.make_async_copy(turned, turned_out, out_sems.at[0]),
         pltpu.make_async_copy(plain.at[pl.ds(0, 2 * cut_blocks)], plain_out, out_sems.at[1]),
     ]
@@ -900,6 +935,8 @@
     full = jnp.float32
     out_shape = (
         jax.ShapeDtypeStruct((blocks, line, 2, 2, height, CHUNK), low),
+        jax.ShapeDtypeStruct((tokens, HEAD_DIM), full),
+        jax.ShapeDtypeStruct((tokens, HEAD_DIM), full),
         jax.ShapeDtypeStruct((tokens, width), low),
         jax.ShapeDtypeStruct((3 * cut_blocks, tokens, CHUNK), low),
         jax.ShapeDtypeStruct((2 * cut_blocks, tokens, CHUNK), low),
@@ -938,6 +975,8 @@
         pltpu.VMEM((2, wide), full),
         pltpu.VMEM((2, wide), full),
         pltpu.VMEM((RANK, wide), low),
+        pltpu.VMEM((tokens, HEAD_DIM), full),
+        pltpu.VMEM((tokens, HEAD_DIM), full),
         pltpu.SemaphoreType.DMA((chunks + 1, 2 * (line - 1))),
         pltpu.SemaphoreType.DMA((chunks + 1, 2 * (line - 1))),
         pltpu.SemaphoreType.DMA((chunks + 1, 2 * (line - 1))),
@@ -950,7 +989,7 @@
         pltpu.SemaphoreType.DMA((2, 2, BLOCKS)),
         pltpu.SemaphoreType.DMA((tokens // SEQ + 1,)),
         pltpu.SemaphoreType.DMA((tokens // SEQ + 1,)),
-        pltpu.SemaphoreType.DMA((6,)),
+        pltpu.SemaphoreType.DMA((8,)),
         *stage_of((shard, *small)),
     ]
     return pl.pallas_call(
@@ -958,7 +997,7 @@
         name="block",
         out_shape=out_shape,
         in_specs=[anywhere] * (3 + len(small)),
-        out_specs=[anywhere] * 9 + [local] * 6,
+        out_specs=[anywhere] * 11 + [local] * 6,
         scratch_shapes=scratch,
         compiler_params=pltpu.CompilerParams(
             collective_id=1, has_side_effects=True, vmem_limit_bytes=VMEM
@@ -1104,11 +1143,12 @@
         load.start()
     dots_copy = remote(dots_box.at[0], dots_box.at[1], count)
     funneled_copies = [
-        remote(funneled_ref.at[rows_of(part)], funneled_out.at[rows_of(part)], count + 1 + part)
-        for part in range(count)
+        remote(funneled_ref.at[rows], funneled_out.at[rows], count + 1 + piece)
+        for piece in range(2 * count)
+        for rows in (pl.ds(piece * (SEQ // 2), SEQ // 2),)
     ]
     last_copies = [
-        remote(own.at[rows_of(part)], last_inbox.at[rows_of(part)], 2 * count + 1 + part)
+        remote(own.at[rows_of(part)], last_inbox.at[rows_of(part)], 3 * count + 1 + part)
         for part in range(count)
     ]
     for copy in copies:
@@ -1215,7 +1255,8 @@
     for part in range(count):
         part_copies[part].wait()
         if part == count - 1:
-            funneled_copies[0].start()
+            for copy in funneled_copies[: 2 * count - 2]:
+                copy.start()
 
         def pull_back(index, carry, part=part):
             place = pl.ds(pl.multiple_of(part * SEQ + index * small, small), small)
@@ -1267,6 +1308,8 @@
             return carry
 
         lax.fori_loop(0, near, attend_back, 0)
+        if part == count - 1:
+            funneled_copies[2 * count - 2].start()
     per = 512 // (4 * weights.shape[4])
     for i in range(3):
         dots = []
@@ -1283,21 +1326,7 @@
             )
         dots = jnp.concatenate(dots, axis=1)
         dots_out[4 + i : 5 + i] = dots
-        head_ratio = ratios[4 + i : 5 + i]
         pulled = (attend_ref[i] * (pulls[4 + i : 5 + i] * dots)).astype(jnp.bfloat16)
-        place_in(
-            gathered,
-            half_rows,
-            cut * i,
-            ADAPTER_SCALE
-            * (
-                dot_nn(reduced[RANK * i : RANK * (i + 1)], d_heads[i, :tokens]) * head_ratio
-                - head_seen[i] * (pulls[4 + i : 5 + i] * dots)
-            ),
-        )
-        low_lift = (attend_ref[i] * head_ratio).astype(jnp.bfloat16)
-        lowered = dot_nt(low_lift, d_heads[i, :tokens]).astype(jnp.bfloat16)
-        gathered[pl.ds(RANK * i, RANK)] = ADAPTER_SCALE * dot_nn(lowered, normed[...])
         d_heads[i, tokens:] = pulled
     for piece in range(width // 512):
         lanes = slice(piece * 512, (piece + 1) * 512)
@@ -1309,8 +1338,23 @@
             results[0][:tokens] + results[1][:tokens] + results[2][:tokens]
         ).astype(jnp.bfloat16)
         for i in range(3):
-            gathered[pl.ds(RANK * i, RANK), lanes] -= ADAPTER_SCALE * results[i][tokens:]
+            gathered[pl.ds(RANK * i, RANK), lanes] = -ADAPTER_SCALE * results[i][tokens:]
     last_copies[0].start()
+    for i in range(3):
+        head_ratio = ratios[4 + i : 5 + i]
+        place_in(
+            gathered,
+            half_rows,
+            cut * i,
+            ADAPTER_SCALE
+            * (
+                dot_nn(reduced[RANK * i : RANK * (i + 1)], d_heads[i, :tokens]) * head_ratio
+                - head_seen[i] * (pulls[4 + i : 5 + i] * dots_out[4 + i : 5 + i])
+            ),
+        )
+        low_lift = (attend_ref[i] * head_ratio).astype(jnp.bfloat16)
+        lowered = dot_nt(low_lift, d_heads[i, :tokens]).astype(jnp.bfloat16)
+        gathered[pl.ds(RANK * i, RANK)] += ADAPTER_SCALE * dot_nn(lowered, normed[...])
     mixer_total = jnp.sum(mixer_dots[...], axis=0, keepdims=True)
     joined = jnp.concatenate([mixed[b] for b in range(near)], axis=1)
     low_output = (output_ref[0] * output_ratio[0]).astype(jnp.bfloat16)
@@ -1347,7 +1391,7 @@
     rest_columns = half_rows // RANK * width - offset
     place_in(gathered, half_rows, offset, jnp.zeros((RANK, rest_columns), jnp.float32))
     def meanwhile():
-        for copy in last_copies[1:] + funneled_copies[1:]:
+        for copy in last_copies[1:] + funneled_copies[2 * count - 1 :]:
             copy.start()
 
     sum_up(
@@ -1387,7 +1431,8 @@
         )
         gradient_copies[-1].start()
     for part in range(count):
-        funneled_copies[part].wait()
+        funneled_copies[2 * part].wait()
+        funneled_copies[2 * part + 1].wait()
         for load in kept_loads(part, 0, 0):
             load.start()
 
@@ -1482,8 +1527,8 @@
             pltpu.SemaphoreType.DMA((10,)),
             pltpu.SemaphoreType.DMA((4 * near,)),
             pltpu.SemaphoreType.DMA((2,)),
-            pltpu.SemaphoreType.DMA((3 * count + 1,)),
-            pltpu.SemaphoreType.DMA((3 * count + 1,)),
+            pltpu.SemaphoreType.DMA((4 * count + 1,)),
+            pltpu.SemaphoreType.DMA((4 * count + 1,)),
             pltpu.SemaphoreType.DMA((2 * count,)),
             pltpu.SemaphoreType.DMA((2, 2)),
             *boxes,
@@ -1794,30 +1839,25 @@
         amplitude_second,
         loudness_second,
     )
-    rows, cut = base_query.shape
-    width = activations.shape[1]
-    place = lax.axis_index("dp") * rows
     entry_down = jnp.swapaxes(entry_value, 1, 2)
     shard, squares, magnitudes = merge(
         (base_query, base_key, base_value, base_gate, base_widen, base_mixer, base_funnel),
-        lax.dynamic_slice_in_dim(entry_down, place, rows, 2),
+        entry_down,
         attend_value,
         widen_value,
         mixer_value.T,
         funnel_value.T,
-        lax.dynamic_slice_in_dim(output_value, place, rows, 2),
+        output_value,
         (stature_value, amplitude_value, loudness_value),
     )
     count = activations.shape[0] // SEQ
-    half = HEAD_DIM // 2
-    lane = jnp.arange(HEAD_DIM)
-    frequency = ROPE_BASE ** (-2.0 * (lane % half).astype(jnp.float32) / HEAD_DIM)
-    angles = positions.astype(jnp.float32)[:, None] * frequency[None]
-    cosine = jnp.cos(angles)
-    sine = jnp.sin(angles) * jnp.where(lane < half, -1.0, 1.0)[None]
+    half = jnp.arange(HEAD_DIM) % (HEAD_DIM // 2)
+    frequency = (ROPE_BASE ** (-2.0 * half.astype(jnp.float32) / HEAD_DIM))[None]
     keep = padding_mask.reshape(count, 1, SEQ)
     (
         full,
+        cosine,
+        sine,
         normed_one,
         turned,
         plain,
@@ -1837,8 +1877,8 @@
         activations,
         cotangent,
         (
-            cosine,
-            sine,
+            positions.reshape(1, -1),
+            frequency,
             keep,
             norm_gains,
             entry_down,

time: 496 us -> 491 us (0.990)
  no operation moved by 1% of the time
where the time goes in v8:
time: 491 us; the launch traced here: 485 us
  Pallas kernels  483 us (98%)
    pallas_call x1, Pallas kernels, run_block(): pl.pallas_call(staged(functools.partial(block_kernel, size), 2, 1 + len(s...  302 us
    pallas_call x1, Pallas kernels, run_tail(): pl.pallas_call(staged(functools.partial(tail_kernel, size, sides, widths)...  142 us
    pallas_call x1, Pallas kernels, merge(): pl.pallas_call(staged(functools.partial(merge_kernel, size, sides), 0, le...  29.3 us
    pallas_call x1, Pallas kernels, update_all(): pl.pallas_call(update_kernel, name='update', out_shape=shapes * 3 + large...  10.3 us

profile of v8, /device:TPU:0, one launch (start us, length us, event | category | flops | bytes accessed | tf_op | source)
XLA Modules:
  0.0 485.0 jit_solution(1445881483075759288)
XLA Ops:
  0.7 0.5 fusion.2.refs_4_
  1.2 29.3 %merge.1 = (bf16[49,128,256]{2,1,0:T(8,128)(2,1)}, f32[16,1024]{1,0:T(8,128)}, f32[16,1024]{1,0:T(8,128)}) custom-call(bf16[128,1024]{1,0:T(8,128)(2,1)} %refs_0_.2, bf16[128,1024]{1,0:T(8,128)(2,1)} %refs_1_.2, bf16[128,1024]{1,0:T(8,128)(2,1)} %refs_2_.1, bf16[128,2816]{1,0:T(8,128)(2,1)} %refs_3_.2, bf16[128,2816]{1,0:T(8,128)(2,1)} %refs_4_.2, ...), custom_call_target="tpu_custom_call" | custom-call | tf_op jit(solution)/shard_map/merge/pallas_call | solution.py:262
  30.5 302.1 %block.1 = (bf16[49,4,2,2,128,256]{5,4,3,2,1,0:T(8,128)(2,1)}, f32[512,128]{1,0:T(8,128)}, f32[512,128]{1,0:T(8,128)}, bf16[512,2048]{1,0:T(8,128)(2,1)}, bf16[1...) custom-call(bf16[512,2048]{1,0:T(8,128)(2,1)} %refs_9_.6, ...), custom_call_target="tpu_custom_call" | custom-call | tf_op jit(solution)/shard_map/block/pallas_call | solution.py:995
  332.6 141.5 %tail.1 = (f32[512,2048]{1,0:T(8,128)}, bf16[512,2048]{1,0:T(8,128)(2,1)}, bf16[512,2048]{1,0:T(8,128)(2,1)}, bf16[240,2048]{1,0:T(8,128)(2,1)}, f32[8,128]{1,0:T(8,128)}) custom-call(bf16[49,4,2,2,128,256]{5,4,3,2,1,0:T(8,128)(2,1)} %get-tuple-element.87.refs_0_, bf16[12,512,256]{2,1,0:T(8,128)(2,1)} %get-tuple-element.88.refs_1_, ...), custom_call_target="tpu_custom_call" | custom-call | tf_op jit(solution)/shard_map/tail/pallas_call | solution.py:1488
  474.2 10.3 %update.1 = (f32[5,16,2048]{2,1,0:T(8,128)}, f32[3,16,1024]{2,1,0:T(8,128)}, f32[2,16,2816]{2,1,0:T(8,128)}, f32[16,1024]{1,0:T(8,128)}, f32[16,2816]{1,0:T(8,12...) custom-call(bf16[240,2048]{1,0:T(8,128)(2,1)} %get-tuple-element.104, ...), custom_call_target="tpu_custom_call" | custom-call | tf_op jit(solution)/shard_map/update/pallas_call | solution.py:1754
